TPU v7x, 32 devices: a whole 2x2x4 slice. The times are simulated.
32 devices in a mesh: groups: 2 (over y), gx: 4 (over z), gy: 2 (over core), gz: 2 (over x).
Axes of the slice: x: 2, y: 2, z: 4, core: 2. Of those that a mesh axis runs over, the one named last changes fastest.
Arguments:
- east_strip: bfloat16 [4, 8, 4, 64, 2048], P(('groups', 'gz'), 'gy', 'gx'), parts along dimension 0
- west_strip: bfloat16 [4, 8, 4, 64, 2048], P(('groups', 'gz'), 'gy', 'gx'), parts along dimension 0
- north_strip: bfloat16 [4, 8, 4, 64, 2048], P(('groups', 'gz'), 'gy', 'gx'), parts along dimension 0
- south_strip: bfloat16 [4, 8, 4, 64, 2048], P(('groups', 'gz'), 'gy', 'gx'), parts along dimension 0
- patch_start: int32 [16], replicated, may hold values from 0 to 1984, as said below
- segment_offset: float32 [4, 8, 4, 2], P(('groups', 'gz'), 'gy', 'gx'), parts along dimension 0, may hold values from -6 to 6
- col_stiffness: float32 [4, 8, 4], P(('groups', 'gz'), 'gy', 'gx'), parts along dimension 0, may hold values from 0.25 to 1
- row_stiffness: float32 [4, 8, 4], P(('groups', 'gz'), 'gy', 'gx'), parts along dimension 0, may hold values from 0.25 to 1
Outputs:
- patch_shift: float32 [4, 8, 4, 2, 2, 16], P(('groups', 'gz'), 'gy', 'gx'), parts along dimension 0
- placed_offset: float32 [4, 8, 4, 2], P(('groups', 'gz'), 'gy', 'gx'), parts along dimension 0
There are 2 independent parts, one for each index of `groups`. A program takes and returns all parts, laid end to end along the dimension named above; an argument that names none is the same for every part. Nothing has to cross between parts.
Inputs may be any that keep to these rules, and one draw needn't show every extreme that they name: `patch_start`: increasing; patch k starts in the k-th of 16 equal cells of the edge and ends within it; the first start is 0 and the last is 1984.
All inputs are finite; a program needn't handle non-finite values.
Results may differ from a plain program's by a relative error of at most 0.0003.
Values may be sent and summed in bfloat16 or wider, within the bound.
No kernel may reach another device: no remote copies, remote signals or barrier semaphores. Data moves between devices by JAX's collectives and lax.ppermute only.
A program may use at most 64 MiB of HBM per device.

v0:
```python
import functools
import math

import jax
import jax.numpy as jnp
import numpy as np
from jax import lax
from jax.experimental import pallas as pl
from jax.experimental.pallas import tpu as pltpu
from jax.sharding import PartitionSpec as P

ITERS = 3
EPS_VAR = 1e-05
EPS_WEIGHT = 1e-06
STEP_SIZE = 0.12
LINK_STIFF = 0.5
F32 = jnp.float32
BF16 = jnp.bfloat16
PART = ("gx", "gz", "gy")
VMEM_LIMIT = 48 * 1024 * 1024

EAST, SOUTH = 0, 32
D_SOUTH, D_EAST, POSITION, COL, ROW = 64, 66, 68, 70, 71


def waves(width):
    quarter = width // 4
    first = np.cos(2.0 * np.pi * np.arange(quarter + 1) / width)
    first[quarter] = 0.0
    cosine = np.zeros(width)
    cosine[: quarter + 1] = first
    cosine[quarter : 2 * quarter + 1] = -first[::-1]
    cosine[2 * quarter :] = -cosine[: 2 * quarter]
    return cosine, np.roll(cosine, quarter)


def basis(width):
    cosine, sine = waves(width)
    half = width // 2
    phase = np.arange(half)[:, None] * np.arange(width)[None, :] % width
    low, high = cosine[phase], sine[phase]
    high[0] = cosine[half * np.arange(width) % width]
    return np.concatenate([low, high], axis=0)


def two_terms(table):
    high = table.astype(np.float32).astype(jnp.bfloat16)
    low = (table - high.astype(np.float64)).astype(np.float32).astype(jnp.bfloat16)
    return high, low


def spread(table, width):
    half = width // 2
    wide = np.zeros((4, width, 2, 4, half))
    for patch in range(4):
        for side in range(2):
            wide[patch, :, side, patch, :] = table[:, side * half : (side + 1) * half]
    return wide.reshape(4 * width, 4 * width)


def tables(width, count):
    plain = basis(width)
    half = width // 2
    norm = np.full((width, 1), math.sqrt(2.0 / width))
    norm[0] = norm[half] = math.sqrt(1.0 / width)
    unit = plain * norm
    right_high, right_low = two_terms(spread(unit.T, width))
    right = np.concatenate([right_high, right_low], axis=0)
    left_high, left_low = two_terms(unit)
    left = np.concatenate([left_high, left_high, left_low], axis=1)
    back_high, back_low = two_terms(spread(plain.T, width).T)
    right_back = np.concatenate([back_high, back_high, back_low], axis=0)
    inv_high, inv_low = two_terms(plain.T)
    left_back = np.concatenate([inv_high, inv_high, inv_low], axis=1)
    energy = np.full(width, width / 2.0)
    energy[0] = energy[half] = width
    energy = energy / float(width) ** 4
    signed = np.where(np.arange(width) < half, np.arange(width), np.arange(width) - width)
    slot_sum = np.zeros((count // 4, 2, 4, half, 128))
    place_sum = np.zeros((count // 4, 4, width, 128))
    for quad in range(count // 4):
        for patch in range(4):
            for side in range(2):
                slot_sum[quad, side, patch, :, quad * 4 + patch] = energy[side * half : (side + 1) * half]
            place_sum[quad, patch, :, quad * 4 + patch] = signed * (width / 2.0) / float(width) ** 4
    sums = np.concatenate(
        [slot_sum.reshape(count * width, 128), place_sum.reshape(count * width, 128)], axis=1
    )
    ones = np.kron(np.eye(4), np.ones((half, half)))
    return (
        right,
        left,
        right_back,
        left_back,
        sums.astype(jnp.bfloat16),
        ones.astype(jnp.bfloat16),
    )


def dot(left, right):
    return jnp.dot(left, right, preferred_element_type=F32)


def split(value):
    high = value.astype(BF16)
    return high, (value - high.astype(F32)).astype(BF16)


def split3(value):
    high = value.astype(BF16)
    rest = value - high.astype(F32)
    middle = rest.astype(BF16)
    return high, middle, (rest - middle.astype(F32)).astype(BF16)


def exact_dot(value, table):
    rows = value.shape[0]
    high, middle, low = split3(value)
    out = dot(jnp.concatenate([high, middle, low], axis=0), table)
    return out[:rows] + out[rows : 2 * rows] + out[2 * rows :]


def cut_tile(start_ref, load, store, width, cell, count):
    lane = lax.broadcasted_iota(jnp.int32, (width, cell), 1)
    for pair in range(count // 2):
        parts = []
        for odd in range(2):
            k = 2 * pair + odd
            offset = start_ref[k] - k * cell
            turn = lax.rem(cell + odd * width - offset, cell)
            parts.append(pltpu.roll(load(k).astype(F32), turn, 1))
        store(pair // 2, pair % 2, jnp.where(lane < width, parts[0], parts[1]).astype(BF16))


def forward(d_ref, q_ref, e_ref, right_ref, left_ref, groups, width):
    span = 4 * width
    lane = lax.broadcasted_iota(jnp.int32, (8, span // 2), 1)
    row = lax.broadcasted_iota(jnp.int32, (8, span // 2), 0)
    keep = jnp.where((row == 0) & (lane % (width // 2) == 0), 0.0, 1.0)
    step = 4

    def body(i, carry):
        base = pl.multiple_of(i * step * width, step * width)
        data = d_ref[pl.ds(base, step * width), :]
        y = dot(jnp.concatenate([data, data], axis=1), right_ref[...])
        high, low = split(y)
        for j in range(step):
            rows = slice(j * width, (j + 1) * width)
            stack = jnp.concatenate([high[rows], low[rows], high[rows]], axis=0)
            q = dot(left_ref[...], stack)
            q_ref[i * step + j] = q
            head = q[0:8, : span // 2] * keep
            q_ref[i * step + j, 0:8, 0 : span // 2] = head
            squares = head * head
            for r in range(8, width, 8):
                squares = squares + q[r : r + 8, : span // 2] * q[r : r + 8, : span // 2]
            for r in range(0, width, 8):
                squares = squares + q[r : r + 8, span // 2 :] * q[r : r + 8, span // 2 :]
            e_ref[i * step + j] = squares
        return carry

    lax.fori_loop(0, groups // step, body, 0)


def products(f, g, width):
    half = width // 2
    span = 2 * width
    lane = lax.broadcasted_iota(jnp.int32, (8, span), 1)
    row = lax.broadcasted_iota(jnp.int32, (8, span), 0)
    plain_lane = lane % half != 0
    plain_row = row != 0
    out = [[], [], [], []]
    for r in range(0, half, 8):
        fcc, fcs = f[r : r + 8, :span], f[r : r + 8, span:]
        fsc, fss = f[half + r : half + r + 8, :span], f[half + r : half + r + 8, span:]
        gcc, gcs = g[r : r + 8, :span], g[r : r + 8, span:]
        gsc, gss = g[half + r : half + r + 8, :span], g[half + r : half + r + 8, span:]
        gcc_s = jnp.where(plain_lane, gcc, gcs)
        gsc_s = jnp.where(plain_lane, gsc, gss)
        gcs = jnp.where(plain_lane, gcs, 0.0)
        gss = jnp.where(plain_lane, gss, 0.0)
        hcc, hcs, hcc_s = gcc, gcs, gcc_s
        if r == 0:
            hcc = jnp.where(plain_row, gcc, gsc)
            hcs = jnp.where(plain_row, gcs, gss)
            hcc_s = jnp.where(plain_row, gcc_s, gsc_s)
            gsc = jnp.where(plain_row, gsc, 0.0)
            gss = jnp.where(plain_row, gss, 0.0)
            gsc_s = jnp.where(plain_row, gsc_s, 0.0)
        out[0].append((fcc * gcc + fcs * gcs) + (fsc * gsc + fss * gss))
        out[1].append((fcs * gcc_s - fcc * gcs) + (fss * gsc_s - fsc * gss))
        out[2].append((fsc * hcc + fss * hcs) - (fcc * gsc + fcs * gss))
        out[3].append((fss * hcc_s - fsc * hcs) - (fcs * gsc_s - fcc * gss))
    top = jnp.concatenate([jnp.concatenate(out[0], 0), jnp.concatenate(out[1], 0)], axis=1)
    low = jnp.concatenate([jnp.concatenate(out[2], 0), jnp.concatenate(out[3], 0)], axis=1)
    return jnp.concatenate([top, low], axis=0)


def backward(qf_ref, qg_ref, ef_ref, eg_ref, scale_ref, sum_ref, right_ref, left_ref, ones_ref, groups, width):
    span = 4 * width
    pixels = float(width * width)

    def factors(e_ref):
        energy = exact_dot(jnp.sum(e_ref[0:groups], axis=1), ones_ref[...])
        return lax.rsqrt(energy * (1.0 / pixels) + EPS_VAR)

    scale_ref[0:groups, 0, :] = factors(ef_ref) * factors(eg_ref)
    row = lax.broadcasted_iota(jnp.int32, (8, span), 0)
    special = jnp.where(row == 0, 2.0, 1.0)
    step = 4

    def body(i, carry):
        highs, lows = [], []
        for j in range(step):
            index = i * step + j
            scale = scale_ref[index]
            scale = jnp.concatenate([scale, scale], axis=1)
            z = products(qf_ref[index] * scale, qg_ref[index], width)
            high, low = split(z)
            highs.append(high)
            lows.append(low)
        high = jnp.concatenate(highs, axis=0)
        low = jnp.concatenate(lows, axis=0)
        v = dot(jnp.concatenate([high, low, high], axis=1), right_ref[...])
        for j in range(step):
            u = dot(left_ref[...], jnp.concatenate([highs[j], lows[j], highs[j]], axis=0))
            strength = jnp.zeros((8, span), F32)
            across = jnp.zeros((8, span), F32)
            along = jnp.zeros((8, span), F32)
            for r in range(0, width, 8):
                square = u[r : r + 8] * u[r : r + 8]
                strength = strength + square
                first = r if r < width // 2 else r - width
                across = across + square * (row + first).astype(F32)
                piece = v[j * width + r : j * width + r + 8]
                piece = piece * piece
                if r % (width // 2) == 0:
                    piece = piece * special
                along = along + piece
            lanes = slice(j * span, (j + 1) * span)
            for kind, value in enumerate((strength, across, along)):
                sum_ref[kind, pl.ds(i, 1), lanes] = jnp.sum(value, axis=0, keepdims=True)
        return carry

    lax.fori_loop(0, groups // step, body, 0)


def finish(sum_ref, sums_ref):
    both = exact_dot(jnp.concatenate([sum_ref[0], sum_ref[1]], axis=0), sums_ref[:, :128])
    strength, across = both[:8], both[8:]
    along = exact_dot(sum_ref[2], sums_ref[:, 128:])
    across = across / (strength + EPS_WEIGHT)
    along = along / (strength + EPS_WEIGHT)
    total = jnp.sum(strength, axis=1, keepdims=True) + EPS_WEIGHT
    first = jnp.sum(strength * across, axis=1, keepdims=True) / total
    second = jnp.sum(strength * along, axis=1, keepdims=True) / total
    return across, along, first, second


def at_lane(first, second, where):
    lane = lax.broadcasted_iota(jnp.int32, (8, 128), 1)
    return jnp.where(lane == where, first, 0.0) + jnp.where(lane == where + 1, second, 0.0)


def cut_kernel(sizes, start_ref, west_ref, east_ref, north_ref, west_out, east_out, north_out):
    width, cell, count, half_rows = sizes

    def one(source, tile, target, slot):
        def load(k):
            return source[0, tile, 0, :, k * cell : (k + 1) * cell]

        def store(quad, side, value):
            target[slot, quad, :, side * cell : (side + 1) * cell] = value

        cut_tile(start_ref, load, store, width, cell, count)

    one(north_ref, 0, north_out, 0)
    for slot in range(half_rows):
        one(west_ref, slot, west_out, slot)
        one(east_ref, slot, east_out, slot)


def fill(d_ref, slot, source_ref, tile, start_ref, sizes):
    width, cell, count = sizes

    def load(k):
        return source_ref[0, tile, 0, :, k * cell : (k + 1) * cell]

    def store(quad, side, value):
        base = (slot * (count // 4) + quad) * width
        d_ref[base : base + width, side * cell : (side + 1) * cell] = value

    cut_tile(start_ref, load, store, width, cell, count)


def copy_in(d_ref, slot, source_ref, tile, sizes):
    width, cell, count = sizes
    for quad in range(count // 4):
        base = (slot * (count // 4) + quad) * width
        d_ref[base : base + width, :] = source_ref[tile, quad]


def south_kernel(sizes, rows, start_ref, south_ref, north_ref, rim_ref, right_ref, left_ref, right_back_ref, left_back_ref, sums_ref, ones_ref, out_ref, d_ref, q_ref, e_ref, scale_ref, sum_ref):
    width, cell, count = sizes
    groups = rows * count // 4
    span = groups * width
    for tile in range(rows):
        fill(d_ref, tile, south_ref, tile, start_ref, sizes)
    for tile in range(rows - 1):
        fill(d_ref, rows + tile, north_ref, tile + 1, start_ref, sizes)
    copy_in(d_ref, 2 * rows - 1, rim_ref, 0, sizes)
    forward(d_ref, q_ref, e_ref, right_ref, left_ref, 2 * groups, width)
    sum_ref[...] = jnp.zeros_like(sum_ref)
    backward(q_ref.at[0:groups], q_ref.at[groups : 2 * groups], e_ref.at[0:groups], e_ref.at[groups : 2 * groups], scale_ref, sum_ref, right_back_ref, left_back_ref, ones_ref, groups, width)
    across, along, first, second = finish(sum_ref, sums_ref)
    out_ref[...] = pltpu.roll(across, SOUTH, 1) + pltpu.roll(along, SOUTH + 16, 1) + at_lane(first, second, D_SOUTH)


def east_kernel(sizes, rows, start_ref, east_ref, west_ref, from_east_ref, from_west_ref, south_ref, position_ref, col_ref, row_ref, right_ref, left_ref, right_back_ref, left_back_ref, sums_ref, ones_ref, out_ref, d_ref, q_ref, e_ref, scale_ref, sum_ref, place_ref):
    width, cell, count = sizes
    groups = rows * count // 4
    own = rows // 2
    for tile in range(own):
        fill(d_ref, tile, east_ref, tile, start_ref, sizes)
        copy_in(d_ref, rows + tile, from_east_ref, tile, sizes)
    for tile in range(own, rows):
        copy_in(d_ref, tile, from_west_ref, tile - own, sizes)
        fill(d_ref, rows + tile, west_ref, tile, start_ref, sizes)
    forward(d_ref, q_ref, e_ref, right_ref, left_ref, 2 * groups, width)
    sum_ref[...] = jnp.zeros_like(sum_ref)
    backward(q_ref.at[0:groups], q_ref.at[groups : 2 * groups], e_ref.at[0:groups], e_ref.at[groups : 2 * groups], scale_ref, sum_ref, right_back_ref, left_back_ref, ones_ref, groups, width)
    across, along, first, second = finish(sum_ref, sums_ref)
    place_ref[...] = jnp.zeros_like(place_ref)
    place_ref[0, 0:rows, 0:2] = position_ref[0, :, 0, :]
    place_ref[1, 0:rows, 0:1] = col_ref[0]
    place_ref[2, 0:rows, 0:1] = row_ref[0]
    packet = south_ref[...] + across + pltpu.roll(along, EAST + 16, 1) + at_lane(first, second, D_EAST)
    packet = packet + pltpu.roll(place_ref[0], POSITION, 1) + pltpu.roll(place_ref[1], COL, 1) + pltpu.roll(place_ref[2], ROW, 1)
    out_ref[...] = jnp.broadcast_to(packet[None], out_ref.shape)


def turned(value, by):
    count = value.shape[0]
    by = by % count
    return value if by == 0 else jnp.concatenate([value[by:], value[:by]], axis=0)


def relax_kernel(counts, rows, patches, all_ref, shift_ref, placed_ref, x_ref):
    nx, nz, ny = counts
    total = nx * nz * ny
    packet = all_ref[...]
    sub = lax.broadcasted_iota(jnp.int32, packet.shape, 1)
    device = lax.broadcasted_iota(jnp.int32, packet.shape, 0)
    gx, gz, gy = device // (nz * ny), device // ny % nz, device % ny

    def field(where):
        return pltpu.roll(packet, 128 - where, 2)

    def one(where):
        return jnp.broadcast_to(packet[:, :, where : where + 1], packet.shape)

    def east(value):
        return turned(value, nz * ny)

    def west(value):
        return turned(value, -nz * ny)

    def south(value):
        inside = pltpu.roll(value, 7, 1)
        beyond = pltpu.roll(turned(value, 1), rows - 1, 1)
        return jnp.where(sub == rows - 1, beyond, inside)

    def north(value):
        inside = pltpu.roll(value, 1, 1)
        beyond = pltpu.roll(turned(value, -1), 8 - (rows - 1), 1)
        return jnp.where(sub == 0, beyond, inside)

    x = field(POSITION)
    d_east = field(D_EAST)
    d_east = jnp.where(sub < rows // 2, d_east, east(d_east))
    d_south = field(D_SOUTH)
    ke = jnp.where(gx < nx - 1, one(COL), 0.0)
    ks = jnp.where((gy == ny - 1) & (sub == rows - 1), 0.0, one(ROW))
    kw, d_west = west(ke), west(d_east)
    kn, d_north = north(ks), north(d_south)
    has_next = jnp.where(gz < nz - 1, LINK_STIFF, 0.0)
    has_prev = jnp.where(gz > 0, LINK_STIFF, 0.0)
    for _ in range(ITERS):
        force = ke * (east(x) - x - d_east) - kw * (x - west(x) - d_west)
        force = force + ks * (south(x) - x - d_south) - kn * (x - north(x) - d_north)
        force = force + has_next * (turned(x, ny) - x) + has_prev * (turned(x, -ny) - x)
        x = x + STEP_SIZE * force
    x_ref[...] = x
    me = (lax.axis_index("gx") * nz + lax.axis_index("gz")) * ny + lax.axis_index("gy")
    next_east = lax.rem(me + nz * ny, total)
    placed_ref[0, :, 0, :] = x_ref[me, 0:rows, 0:2]
    own, other = all_ref[me], all_ref[next_east]
    row = lax.broadcasted_iota(jnp.int32, own.shape, 0)
    mixed = jnp.where(row < rows // 2, own, other)
    for kind, (source, where) in enumerate(((mixed, EAST), (own, SOUTH))):
        for part in range(2):
            value = source
            if where + part * patches:
                value = pltpu.roll(source, 128 - where - part * patches, 1)
            for tile in range(rows):
                shift_ref[0, tile, 0, kind, part : part + 1, :] = value[tile : tile + 1, :patches]


def neighbour(block, axis, distance):
    count = lax.axis_size(axis)
    route = [(i, i + distance) for i in range(count) if 0 <= i + distance < count]
    return lax.ppermute(block, axis, route)


def shards(east_strip, west_strip, north_strip, south_strip, patch_start, segment_offset, col_stiffness, row_stiffness):
    _, rows, _, width, length = east_strip.shape
    count = patch_start.shape[0]
    cell = length // count
    sizes = (width, cell, count)
    half_rows = rows // 2
    quads = count // 4
    span = 4 * width
    groups = rows * quads
    counts = tuple(lax.axis_size(axis) for axis in PART)
    total = math.prod(counts)
    constants = [jnp.asarray(table) for table in tables(width, count)]
    params = pltpu.CompilerParams(vmem_limit_bytes=VMEM_LIMIT)
    smem = pl.BlockSpec(memory_space=pltpu.SMEM)
    vmem = pl.BlockSpec(memory_space=pltpu.VMEM)

    def some_rows(number, block):
        return pl.BlockSpec((1, number, 1, width, length), lambda i: (0, block, 0, 0, 0))

    west_cut, east_cut, north_cut = pl.pallas_call(
        functools.partial(cut_kernel, (width, cell, count, half_rows)),
        grid=(1,),
        out_shape=[
            jax.ShapeDtypeStruct((half_rows, quads, width, span), BF16),
            jax.ShapeDtypeStruct((half_rows, quads, width, span), BF16),
            jax.ShapeDtypeStruct((1, quads, width, span), BF16),
        ],
        in_specs=[smem, some_rows(half_rows, 0), some_rows(half_rows, 1), some_rows(1, 0)],
        out_specs=[
            pl.BlockSpec((half_rows, quads, width, span), lambda i: (0, 0, 0, 0)),
            pl.BlockSpec((half_rows, quads, width, span), lambda i: (0, 0, 0, 0)),
            pl.BlockSpec((1, quads, width, span), lambda i: (0, 0, 0, 0)),
        ],
        compiler_params=params,
        name="cut",
    )(patch_start, west_strip, east_strip, north_strip)

    from_east = neighbour(west_cut, "gx", -1)
    from_west = neighbour(east_cut, "gx", 1)
    from_south = neighbour(north_cut, "gy", -1)

    scratch = [
        pltpu.VMEM((2 * groups * width, span), BF16),
        pltpu.VMEM((2 * groups, width, span), F32),
        pltpu.VMEM((2 * groups, 8, span // 2), F32),
        pltpu.VMEM((groups, 1, span // 2), F32),
        pltpu.VMEM((3, 8, quads * span), F32),
    ]
    cost = pl.CostEstimate(flops=6_000_000_000, bytes_accessed=4_000_000, transcendentals=0)
    south = pl.pallas_call(
        functools.partial(south_kernel, sizes, rows),
        out_shape=jax.ShapeDtypeStruct((8, 128), F32),
        in_specs=[smem] + [vmem] * 9,
        out_specs=vmem,
        scratch_shapes=scratch,
        compiler_params=params,
        cost_estimate=cost,
        name="south",
    )(patch_start, south_strip, north_strip, from_south, *constants)
    packet = pl.pallas_call(
        functools.partial(east_kernel, sizes, rows),
        out_shape=jax.ShapeDtypeStruct((total, 8, 128), F32),
        in_specs=[smem] + [vmem] * 14,
        out_specs=vmem,
        scratch_shapes=scratch + [pltpu.VMEM((3, 8, 128), F32)],
        compiler_params=params,
        cost_estimate=cost,
        name="east",
    )(patch_start, east_strip, west_strip, from_east, from_west, south, segment_offset, col_stiffness, row_stiffness, *constants)
    gathered = lax.all_to_all(packet, PART, 0, 0)
    return tuple(
        pl.pallas_call(
            functools.partial(relax_kernel, counts, rows, count),
            out_shape=[
                jax.ShapeDtypeStruct((1, rows, 1, 2, 2, count), F32),
                jax.ShapeDtypeStruct((1, rows, 1, 2), F32),
            ],
            in_specs=[vmem],
            out_specs=[vmem, vmem],
            scratch_shapes=[pltpu.VMEM((total, 8, 128), F32)],
            compiler_params=params,
            name="relax",
        )(gathered)
    )


def solution(mesh):
    placed = (
        P(("groups", "gz"), "gy", "gx", None, None),
        P(("groups", "gz"), "gy", "gx", None, None),
        P(("groups", "gz"), "gy", "gx", None, None),
        P(("groups", "gz"), "gy", "gx", None, None),
        P(),
        P(("groups", "gz"), "gy", "gx", None),
        P(("groups", "gz"), "gy", "gx"),
        P(("groups", "gz"), "gy", "gx"),
    )
    return jax.shard_map(
        shards,
        mesh=mesh,
        in_specs=placed,
        out_specs=(
            P(("groups", "gz"), "gy", "gx", None, None, None),
            P(("groups", "gz"), "gy", "gx", None),
        ),
        check_vma=False,
    )
```

profile of v0, /device:TPU:0, one launch (start us, length us, event | category | flops | bytes accessed | tf_op | source)
XLA Modules:
  0.0 45.5 jit_solution(17744938183647338166)
XLA Ops:
  0.6 0.0 copy-start
  0.6 1.2 %copy-done = bf16[1,4,1,64,2048]{4,3,2,1,0:T(8,128)(2,1)S(1)} copy-done((bf16[1,4,1,64,2048]{4,3,2,1,0:T(8,128)(2,1)S(1)}, bf16[1,4,1,64,2048]{4,3,2,1,0:T(8,128)(2,1)}, u32[]{:S(2)}) %copy-start) | copy-done | bytes 1048600
  1.9 0.0 copy-start.2
  1.9 1.2 %copy-done.2 = bf16[1,4,1,64,2048]{4,3,2,1,0:T(8,128)(2,1)S(1)} copy-done((bf16[1,4,1,64,2048]{4,3,2,1,0:T(8,128)(2,1)S(1)}, bf16[1,4,1,64,2048]{4,3,2,1,0:T(8,128)(2,1)}, u32[]{:S(2)}) %copy-start.2) | copy-done | bytes 1048600
  3.1 0.0 copy-start.4
  3.1 1.2 %copy-done.4 = bf16[1,4,1,64,2048]{4,3,2,1,0:T(8,128)(2,1)S(1)} copy-done((bf16[1,4,1,64,2048]{4,3,2,1,0:T(8,128)(2,1)S(1)}, bf16[1,4,1,64,2048]{4,3,2,1,0:T(8,128)(2,1)}, u32[]{:S(2)}) %copy-start.4) | copy-done | bytes 1048600
  4.3 0.0 copy-start.6
  4.3 0.7 %copy-done.6 = s32[16]{0:T(128)S(1)} copy-done((s32[16]{0:T(128)S(1)}, s32[16]{0:T(128)}, u32[]{:S(2)}) %copy-start.6) | copy-done | bytes 88
  5.0 0.0 copy-start.1
  5.0 0.0 copy-start.8
  5.0 0.0 copy-start.14
  5.0 0.0 copy-start.15
  5.0 0.0 copy-start.16
  5.0 1.0 %cut.1 = (bf16[2,4,64,256]{3,2,1,0:T(8,128)(2,1)S(1)}, bf16[2,4,64,256]{3,2,1,0:T(8,128)(2,1)S(1)}, bf16[1,4,64,256]{3,2,1,0:T(8,128)(2,1)S(1)}) custom-call(s32[16]{0:T(128)S(1)} %copy-done.6, bf16[1,4,1,64,2048]{4,3,2,1,0:T(8,128)(2,1)S(1)} %copy-done.4, bf16[1,4,1,64,2048]{4,3,2,1,0:T(8,128)(2,1)S(1)} %copy-done.2, bf16[1,4,1,64,2048]{4,3,2,1,0:T(8,128)(2,1)S(1)} %copy-done), custom_call_target="tpu_custom_call" | custom-call | tf_op jit(solution)/shard_map/cut/pallas_call | solution.py:434
  5.9 1.3 %collective-permute-start.2 = (bf16[1,4,64,256]{3,2,1,0:T(8,128)(2,1)S(1)}, bf16[1,4,64,256]{3,2,1,0:T(8,128)(2,1)S(1)}, u32[]{:S(2)}, u32[]{:S(2)}) collective-permute-start(bf16[1,4,64,256]{3,2,1,0:T(8,128)(2,1)S(1)} %get-tuple-element.7), channel_id=1, source_target_pairs={{2,0},{3,1},{6,4},{7,5},{10,8},{11,9},{14,12},{15,13},{18,16},{19,... | collective-permute-start | bytes 393224 | tf_op jit(solution)/shard_map/ppermute | solution.py:412
  7.2 0.0 copy-start.17
  7.3 1.3 %collective-permute-start = (bf16[2,4,64,256]{3,2,1,0:T(8,128)(2,1)S(1)}, bf16[2,4,64,256]{3,2,1,0:T(8,128)(2,1)S(1)}, u32[]{:S(2)}, u32[]{:S(2)}) collective-permute-start(bf16[2,4,64,256]{3,2,1,0:T(8,128)(2,1)S(1)} %get-tuple-element.5), channel_id=1, source_target_pairs={{4,0},{8,4},{12,8},{5,1},{9,5},{13,9},{6,2},{10,6},{14,10},{7,3},{... | collective-permute-start | bytes 786440 | tf_op jit(solution)/shard_map/ppermute | solution.py:412
  8.6 0.0 copy-start.18
  8.6 5.6 %collective-permute-start.1 = (bf16[2,4,64,256]{3,2,1,0:T(8,128)(2,1)S(1)}, bf16[2,4,64,256]{3,2,1,0:T(8,128)(2,1)S(1)}, u32[]{:S(2)}, u32[]{:S(2)}) collective-permute-start(bf16[2,4,64,256]{3,2,1,0:T(8,128)(2,1)S(1)} %get-tuple-element.6), channel_id=1, source_target_pairs={{0,4},{4,8},{8,12},{1,5},{5,9},{9,13},{2,6},{6,10},{10,14},{3,7},{... | collective-permute-start | bytes 786440 | tf_op jit(solution)/shard_map/ppermute | solution.py:412
  14.1 0.0 copy-done.17
  14.2 0.1 copy.16.position_ref
  14.3 0.0 copy-done.18
  14.3 0.0 copy-start.19
  14.3 0.1 copy.17.col_ref
  14.3 0.6 %copy-done.19 = f32[1,4,1]{1,2,0:T(1,128)S(1)} copy-done((f32[1,4,1]{1,2,0:T(1,128)S(1)}, f32[1,4,1]{1,2,0:T(1,128)}, u32[]{:S(2)}) %copy-start.19) | copy-done | bytes 40
  14.9 0.0 copy-start.7
  14.9 0.1 copy.18.row_ref
  15.0 0.0 collective-permute-done.2.rim_ref
  15.0 0.0 copy-done.1
  15.0 0.0 copy-done.8
  15.0 0.0 copy-done.14
  15.0 0.0 copy-done.15
  15.1 0.0 copy-done.16
  15.1 0.5 %copy-done.7 = s32[16]{0:T(128)S(1)} copy-done((s32[16]{0:T(128)S(1)}, s32[16]{0:T(128)}, u32[]{:S(2)}) %copy-start.7) | copy-done | bytes 88
  15.6 1.1 %copy-done.9 = bf16[1024,256]{1,0:T(8,128)(2,1)S(1)} copy-done((bf16[1024,256]{1,0:T(8,128)(2,1)S(1)}, bf16[1024,256]{1,0:T(8,128)(2,1)}, u32[]{:S(2)}) %copy-start.9) | copy-done | bytes 524312
  16.7 1.0 %copy-done.11 = bf16[768,256]{1,0:T(8,128)(2,1)S(1)} copy-done((bf16[768,256]{1,0:T(8,128)(2,1)S(1)}, bf16[768,256]{1,0:T(8,128)(2,1)}, u32[]{:S(2)}) %copy-start.11) | copy-done | bytes 393240
  17.7 0.9 %copy-done.13 = bf16[512,256]{1,0:T(8,128)(2,1)S(1)} copy-done((bf16[512,256]{1,0:T(8,128)(2,1)S(1)}, bf16[512,256]{1,0:T(8,128)(2,1)}, u32[]{:S(2)}) %copy-start.13) | copy-done | bytes 262168
  18.6 6.6 %south.1.south_ref = f32[8,128]{1,0:T(8,128)S(1)} custom-call(s32[16]{0:T(128)S(1)} %copy-done.7, bf16[1,4,1,64,2048]{4,3,2,1,0:T(8,128)(2,1)S(1)} %copy-done.8, bf16[1,4,1,64,2048]{4,3,2,1,0:T(8,128)(2,1)S(1)} %copy-done.1, bf16[1,4,64,256]{3,2,1,0:T(8,128)(2,1)S(1)} %collective-permute-done.2.rim_ref, bf16[512,256]{1,0:T(8,128)(2,1)S(1)} %copy-done.13, ...), custom_call_target="tpu_custom_call" | custom-call | flops 6000000000 | bytes 4000000 | tf_op jit(solution)/shard_map/south/pallas_call | solution.py:464
  25.2 0.0 collective-permute-done.from_east_ref
  25.2 0.0 collective-permute-done.1.from_west_ref
  25.2 0.0 copy-done.3
  25.3 0.0 copy-done.5
  25.3 0.0 copy-done.10
  25.3 0.0 copy-done.12
  25.3 6.4 %east.1 = f32[16,8,128]{2,1,0:T(8,128)S(1)} custom-call(s32[16]{0:T(128)S(1)} %copy-done.7, bf16[1,4,1,64,2048]{4,3,2,1,0:T(8,128)(2,1)S(1)} %copy-done.3, bf16[1,4,1,64,2048]{4,3,2,1,0:T(8,128)(2,1)S(1)} %copy-done.5, bf16[2,4,64,256]{3,2,1,0:T(8,128)(2,1)S(1)} %collective-permute-done.from_east_ref, ...), custom_call_target="tpu_custom_call" | custom-call | flops 6000000000 | bytes 4000000 | tf_op jit(solution)/shard_map/east/pallas_call | solution.py:474
  31.7 12.2 %all_to_all.5.all_ref = f32[16,8,128]{2,1,0:T(8,128)S(1)} all-to-all(f32[16,8,128]{2,1,0:T(8,128)S(1)} %east.1), channel_id=1, replica_groups=mesh['groups'=2,'gx'=4,'gy'=2,'gz'=2] {'gx','gz','gy'}, dimensions={0} | all-to-all | bytes 131072 | tf_op jit(solution)/shard_map/all_to_all | solution.py:484
  43.9 0.9 %relax.1 = (f32[1,4,1,2,2,16]{5,4,3,2,1,0:T(2,128)}, f32[1,4,1,2]{3,2,1,0:T(1,128)S(1)}) custom-call(f32[16,8,128]{2,1,0:T(8,128)S(1)} %all_to_all.5.all_ref), custom_call_target="tpu_custom_call" | custom-call | tf_op jit(solution)/shard_map/relax/pallas_call | solution.py:486
  44.8 0.6 %copy.19 = f32[1,4,1,2]{1,3,2,0:T(2,128)} copy(f32[1,4,1,2]{3,2,1,0:T(1,128)S(1)} %get-tuple-element.9) | data formatting | bytes 64 | tf_op jit(solution)/shard_map/relax/pallas_call | solution.py:486
  (7 shorter events, 0.0 us)
Async XLA Ops:
  0.6 1.2 %copy-start = (bf16[1,4,1,64,2048]{4,3,2,1,0:T(8,128)(2,1)S(1)}, bf16[1,4,1,64,2048]{4,3,2,1,0:T(8,128)(2,1)}, u32[]{:S(2)}) copy-start(bf16[1,4,1,64,2048]{4,3,2,1,0:T(8,128)(2,1)} %north_ref.3) | copy-start | bytes 3145732
  1.9 1.2 %copy-start.2 = (bf16[1,4,1,64,2048]{4,3,2,1,0:T(8,128)(2,1)S(1)}, bf16[1,4,1,64,2048]{4,3,2,1,0:T(8,128)(2,1)}, u32[]{:S(2)}) copy-start(bf16[1,4,1,64,2048]{4,3,2,1,0:T(8,128)(2,1)} %east_ref.3) | copy-start | bytes 3145732
  3.1 1.2 %copy-start.4 = (bf16[1,4,1,64,2048]{4,3,2,1,0:T(8,128)(2,1)S(1)}, bf16[1,4,1,64,2048]{4,3,2,1,0:T(8,128)(2,1)}, u32[]{:S(2)}) copy-start(bf16[1,4,1,64,2048]{4,3,2,1,0:T(8,128)(2,1)} %west_ref.3) | copy-start | bytes 3145732
  4.3 0.7 %copy-start.6 = (s32[16]{0:T(128)S(1)}, s32[16]{0:T(128)}, u32[]{:S(2)}) copy-start(s32[16]{0:T(128)} %start_ref.5) | copy-start | bytes 196
  5.0 10.1 %copy-start.1 = (bf16[1,4,1,64,2048]{4,3,2,1,0:T(8,128)(2,1)S(1)}, bf16[1,4,1,64,2048]{4,3,2,1,0:T(8,128)(2,1)}, u32[]{:S(2)}) copy-start(bf16[1,4,1,64,2048]{4,3,2,1,0:T(8,128)(2,1)} %north_ref.3) | copy-start | bytes 3145732
  5.0 10.1 %copy-start.8 = (bf16[1,4,1,64,2048]{4,3,2,1,0:T(8,128)(2,1)S(1)}, bf16[1,4,1,64,2048]{4,3,2,1,0:T(8,128)(2,1)}, u32[]{:S(2)}) copy-start(bf16[1,4,1,64,2048]{4,3,2,1,0:T(8,128)(2,1)} %south_ref.1) | copy-start | bytes 3145732
  5.0 10.1 %copy-start.14 = (bf16[128,128]{1,0:T(8,128)(2,1)S(1)}, bf16[128,128]{1,0:T(8,128)(2,1)}, u32[]{:S(2)}) copy-start(bf16[128,128]{1,0:T(8,128)(2,1)} %constant.17.clone.ones_ref) | copy-start | bytes 98308
  5.0 10.1 %copy-start.15 = (bf16[64,192]{1,0:T(8,128)(2,1)S(1)}, bf16[64,192]{1,0:T(8,128)(2,1)}, u32[]{:S(2)}) copy-start(bf16[64,192]{1,0:T(8,128)(2,1)} %constant.15.clone.left_back_ref) | copy-start | bytes 73732
  5.0 10.1 %copy-start.16 = (bf16[64,192]{1,0:T(8,128)(2,1)S(1)}, bf16[64,192]{1,0:T(8,128)(2,1)}, u32[]{:S(2)}) copy-start(bf16[64,192]{1,0:T(8,128)(2,1)} %constant.13.clone.left_ref) | copy-start | bytes 73732
  5.9 9.1 %collective-permute-start.2 = (bf16[1,4,64,256]{3,2,1,0:T(8,128)(2,1)S(1)}, bf16[1,4,64,256]{3,2,1,0:T(8,128)(2,1)S(1)}, u32[]{:S(2)}, u32[]{:S(2)}) collective-permute-start(bf16[1,4,64,256]{3,2,1,0:T(8,128)(2,1)S(1)} %get-tuple-element.7), channel_id=1, source_target_pairs={{2,0},{3,1},{6,4},{7,5},{10,8},{11,9},{14,12},{15,13},{18,16},{19,... | collective-permute-start | bytes 393224 | tf_op jit(solution)/shard_map/ppermute | solution.py:412
  7.2 6.9 %copy-start.17 = (f32[1,4,1,2]{1,3,2,0:T(2,128)S(1)}, f32[1,4,1,2]{1,3,2,0:T(2,128)}, u32[]{:S(2)}) copy-start(f32[1,4,1,2]{1,3,2,0:T(2,128)} %param.19) | copy-start | bytes 100
  7.3 18.0 %collective-permute-start = (bf16[2,4,64,256]{3,2,1,0:T(8,128)(2,1)S(1)}, bf16[2,4,64,256]{3,2,1,0:T(8,128)(2,1)S(1)}, u32[]{:S(2)}, u32[]{:S(2)}) collective-permute-start(bf16[2,4,64,256]{3,2,1,0:T(8,128)(2,1)S(1)} %get-tuple-element.5), channel_id=1, source_target_pairs={{4,0},{8,4},{12,8},{5,1},{9,5},{13,9},{6,2},{10,6},{14,10},{7,3},{... | collective-permute-start | bytes 786440 | tf_op jit(solution)/shard_map/ppermute | solution.py:412
  8.6 5.7 %copy-start.18 = (f32[1,4,1]{1,2,0:T(1,128)S(1)}, f32[1,4,1]{1,2,0:T(1,128)}, u32[]{:S(2)}) copy-start(f32[1,4,1]{1,2,0:T(1,128)} %param.20) | copy-start | bytes 52
  8.6 16.7 %collective-permute-start.1 = (bf16[2,4,64,256]{3,2,1,0:T(8,128)(2,1)S(1)}, bf16[2,4,64,256]{3,2,1,0:T(8,128)(2,1)S(1)}, u32[]{:S(2)}, u32[]{:S(2)}) collective-permute-start(bf16[2,4,64,256]{3,2,1,0:T(8,128)(2,1)S(1)} %get-tuple-element.6), channel_id=1, source_target_pairs={{0,4},{4,8},{8,12},{1,5},{5,9},{9,13},{2,6},{6,10},{10,14},{3,7},{... | collective-permute-start | bytes 786440 | tf_op jit(solution)/shard_map/ppermute | solution.py:412
  14.3 0.7 %copy-start.19 = (f32[1,4,1]{1,2,0:T(1,128)S(1)}, f32[1,4,1]{1,2,0:T(1,128)}, u32[]{:S(2)}) copy-start(f32[1,4,1]{1,2,0:T(1,128)} %param.21) | copy-start | bytes 52
  14.9 0.7 %copy-start.7 = (s32[16]{0:T(128)S(1)}, s32[16]{0:T(128)}, u32[]{:S(2)}) copy-start(s32[16]{0:T(128)} %start_ref.5) | copy-start | bytes 196
  15.0 10.2 %copy-start.3 = (bf16[1,4,1,64,2048]{4,3,2,1,0:T(8,128)(2,1)S(1)}, bf16[1,4,1,64,2048]{4,3,2,1,0:T(8,128)(2,1)}, u32[]{:S(2)}) copy-start(bf16[1,4,1,64,2048]{4,3,2,1,0:T(8,128)(2,1)} %east_ref.3) | copy-start | bytes 3145732
  15.0 10.2 %copy-start.5 = (bf16[1,4,1,64,2048]{4,3,2,1,0:T(8,128)(2,1)S(1)}, bf16[1,4,1,64,2048]{4,3,2,1,0:T(8,128)(2,1)}, u32[]{:S(2)}) copy-start(bf16[1,4,1,64,2048]{4,3,2,1,0:T(8,128)(2,1)} %west_ref.3) | copy-start | bytes 3145732
  15.6 1.1 %copy-start.9 = (bf16[1024,256]{1,0:T(8,128)(2,1)S(1)}, bf16[1024,256]{1,0:T(8,128)(2,1)}, u32[]{:S(2)}) copy-start(bf16[1024,256]{1,0:T(8,128)(2,1)} %constant.16.clone.sums_ref) | copy-start | bytes 1572868
  16.7 1.0 %copy-start.11 = (bf16[768,256]{1,0:T(8,128)(2,1)S(1)}, bf16[768,256]{1,0:T(8,128)(2,1)}, u32[]{:S(2)}) copy-start(bf16[768,256]{1,0:T(8,128)(2,1)} %constant.14.clone.right_back_ref) | copy-start | bytes 1179652
  17.7 0.9 %copy-start.13 = (bf16[512,256]{1,0:T(8,128)(2,1)S(1)}, bf16[512,256]{1,0:T(8,128)(2,1)}, u32[]{:S(2)}) copy-start(bf16[512,256]{1,0:T(8,128)(2,1)} %constant.12.clone.right_ref) | copy-start | bytes 786436
  18.6 6.6 %copy-start.10 = (bf16[1024,256]{1,0:T(8,128)(2,1)S(1)}, bf16[1024,256]{1,0:T(8,128)(2,1)}, u32[]{:S(2)}) copy-start(bf16[1024,256]{1,0:T(8,128)(2,1)} %constant.16.clone.sums_ref) | copy-start | bytes 1572868
  18.6 6.6 %copy-start.12 = (bf16[768,256]{1,0:T(8,128)(2,1)S(1)}, bf16[768,256]{1,0:T(8,128)(2,1)}, u32[]{:S(2)}) copy-start(bf16[768,256]{1,0:T(8,128)(2,1)} %constant.14.clone.right_back_ref) | copy-start | bytes 1179652
where the time goes:
time: 45.9 us; the launch traced here: 45.5 us
  Pallas kernels  14.8 us (32%)
  blocking collectives  12.2 us (27%)
  local copies, waits for them, and re-layouts  9.42 us (21%)
  starting transfers between devices  8.16 us (18%)
  between operations  0.81 us (2%)
    all_to_all x1, blocking collectives, shards(): gathered = lax.all_to_all(packet, PART, 0, 0)  12.2 us
    unnamed x43, local copies, waits for them, and re-layouts  8.77 us
    ppermute x3, starting transfers between devices, neighbour(): return lax.ppermute(block, axis, route)  8.16 us
    pallas_call x1, Pallas kernels, shards(): pl.pallas_call(functools.partial(south_kernel, sizes, rows), out_shape=ja...  6.57 us
    pallas_call x1, Pallas kernels, shards(): pl.pallas_call(functools.partial(east_kernel, sizes, rows), out_shape=jax...  6.44 us
    pallas_call x1, Pallas kernels, shards(): pl.pallas_call(functools.partial(cut_kernel, (width, cell, count, half_ro...  0.95 us
  transfers between devices with their start and end apart: 3, of which 0 were waited for; matrix products, arithmetic and copies ran while one was open for 1% of the time, Pallas kernels for 14%

commit v1 on v0

v1 whole, which is shorter than its diff:
```python
import functools
import math

import jax
import jax.numpy as jnp
import numpy as np
from jax import lax
from jax.experimental import pallas as pl
from jax.experimental.pallas import tpu as pltpu
from jax.sharding import PartitionSpec as P

ITERS = 3
EPS_VAR = 1e-05
EPS_WEIGHT = 1e-06
STEP_SIZE = 0.12
LINK_STIFF = 0.5
F32 = jnp.float32
BF16 = jnp.bfloat16
PART = ("gx", "gz", "gy")
MIB = 1024 * 1024
CUT_VMEM, SOUTH_VMEM, EAST_VMEM, RELAX_VMEM = 62 * MIB, 52 * MIB, 32 * MIB, 16 * MIB

EAST, SOUTH = 0, 32
D_SOUTH, D_EAST, POSITION, COL, ROW = 64, 66, 68, 70, 71


def waves(width):
    quarter = width // 4
    first = np.cos(2.0 * np.pi * np.arange(quarter + 1) / width)
    first[quarter] = 0.0
    cosine = np.zeros(width)
    cosine[: quarter + 1] = first
    cosine[quarter : 2 * quarter + 1] = -first[::-1]
    cosine[2 * quarter :] = -cosine[: 2 * quarter]
    return cosine, np.roll(cosine, quarter)


def basis(width):
    cosine, sine = waves(width)
    half = width // 2
    phase = np.arange(half)[:, None] * np.arange(width)[None, :] % width
    low, high = cosine[phase], sine[phase]
    high[0] = cosine[half * np.arange(width) % width]
    return np.concatenate([low, high], axis=0)


def two_terms(table):
    high = table.astype(np.float32).astype(jnp.bfloat16)
    low = (table - high.astype(np.float64)).astype(np.float32).astype(jnp.bfloat16)
    return high, low


def spread(table, width):
    half = width // 2
    wide = np.zeros((4, width, 2, 4, half))
    for patch in range(4):
        for side in range(2):
            wide[patch, :, side, patch, :] = table[:, side * half : (side + 1) * half]
    return wide.reshape(4 * width, 4 * width)


def tables(width):
    plain = basis(width)
    half = width // 2
    norm = np.full((width, 1), math.sqrt(2.0 / width))
    norm[0] = norm[half] = math.sqrt(1.0 / width)
    unit = plain * norm
    right = np.concatenate(two_terms(spread(unit.T, width)), axis=0)
    right_back = np.concatenate(two_terms(spread(plain.T, width).T), axis=0)
    lefts = []
    for table in (unit, plain.T):
        high, low = two_terms(table)
        lefts.append(np.concatenate([high, high, low], axis=1))
    energy = np.full(width, width / 2.0)
    energy[0] = energy[half] = width
    signed = np.where(np.arange(width) < half, np.arange(width), np.arange(width) - width) * (width / 2.0)
    slot_sum = np.zeros((2, 4, half, 128))
    place_sum = np.zeros((4, width, 128))
    for patch in range(4):
        for side in range(2):
            slot_sum[side, patch, :, patch] = energy[side * half : (side + 1) * half]
        place_sum[patch, :, patch] = signed
    sums = np.concatenate([slot_sum.reshape(4 * width, 128), place_sum.reshape(4 * width, 128)], axis=1)
    sums = sums / float(width) ** 4
    ones = np.kron(np.eye(4), np.ones((half, half)))
    return (right, right_back, np.stack(lefts), sums.astype(jnp.bfloat16), ones.astype(jnp.bfloat16))


def dot(left, right):
    return jnp.dot(left, right, preferred_element_type=F32)


def split(value):
    high = value.astype(BF16)
    return high, (value - high.astype(F32)).astype(BF16)


def split3(value):
    high = value.astype(BF16)
    rest = value - high.astype(F32)
    middle = rest.astype(BF16)
    return high, middle, (rest - middle.astype(F32)).astype(BF16)


def exact_dot(value, table):
    rows = value.shape[0]
    high, middle, low = split3(value)
    out = dot(jnp.concatenate([high, middle, low], axis=0), table)
    return out[:rows] + out[rows : 2 * rows] + out[2 * rows :]


def cut_tile(start_ref, load, store, width, cell, count):
    lane = lax.broadcasted_iota(jnp.int32, (width, cell), 1)
    for pair in range(count // 2):
        parts = []
        for odd in range(2):
            k = 2 * pair + odd
            offset = start_ref[k] - k * cell
            turn = lax.rem(cell + odd * width - offset, cell)
            parts.append(pltpu.roll(load(k).astype(F32), turn, 1))
        store(pair // 2, pair % 2, jnp.where(lane < width, parts[0], parts[1]).astype(BF16))


def forward(source, q_ref, e_ref, right_ref, left_ref, first, groups, width):
    span = 4 * width
    lane = lax.broadcasted_iota(jnp.int32, (8, span // 2), 1)
    row = lax.broadcasted_iota(jnp.int32, (8, span // 2), 0)
    keep = jnp.where((row == 0) & (lane % (width // 2) == 0), 0.0, 1.0)
    step = 4
    for i in range(0, groups, step):
        data = source(i)
        y = dot(jnp.concatenate([data, data], axis=1), right_ref[...])
        high, low = split(y)
        for j in range(step):
            rows = slice(j * width, (j + 1) * width)
            stack = jnp.concatenate([high[rows], low[rows], high[rows]], axis=0)
            q = dot(left_ref[0], stack)
            index = first + i + j
            head = q[0:8, : span // 2] * keep
            q_ref[index, 0:8, 0 : span // 2] = head
            q_ref[index, 0:8, span // 2 :] = q[0:8, span // 2 :]
            q_ref[index, 8:width, :] = q[8:width]
            squares = head * head
            for r in range(8, width, 8):
                squares = squares + q[r : r + 8, : span // 2] * q[r : r + 8, : span // 2]
            for r in range(0, width, 8):
                squares = squares + q[r : r + 8, span // 2 :] * q[r : r + 8, span // 2 :]
            e_ref[pl.ds(index, 1), :] = jnp.sum(squares, axis=0, keepdims=True)


def products(f, g, width):
    half = width // 2
    span = 2 * width
    lane = lax.broadcasted_iota(jnp.int32, (8, span), 1)
    row = lax.broadcasted_iota(jnp.int32, (8, span), 0)
    plain_lane = lane % half != 0
    plain_row = row != 0
    out = [[], [], [], []]
    for r in range(0, half, 8):
        fcc, fcs = f[r : r + 8, :span], f[r : r + 8, span:]
        fsc, fss = f[half + r : half + r + 8, :span], f[half + r : half + r + 8, span:]
        gcc, gcs = g[r : r + 8, :span], g[r : r + 8, span:]
        gsc, gss = g[half + r : half + r + 8, :span], g[half + r : half + r + 8, span:]
        gcc_s = jnp.where(plain_lane, gcc, gcs)
        gsc_s = jnp.where(plain_lane, gsc, gss)
        gcs = jnp.where(plain_lane, gcs, 0.0)
        gss = jnp.where(plain_lane, gss, 0.0)
        hcc, hcs, hcc_s = gcc, gcs, gcc_s
        if r == 0:
            hcc = jnp.where(plain_row, gcc, gsc)
            hcs = jnp.where(plain_row, gcs, gss)
            hcc_s = jnp.where(plain_row, gcc_s, gsc_s)
            gsc = jnp.where(plain_row, gsc, 0.0)
            gss = jnp.where(plain_row, gss, 0.0)
            gsc_s = jnp.where(plain_row, gsc_s, 0.0)
        out[0].append((fcc * gcc + fcs * gcs) + (fsc * gsc + fss * gss))
        out[1].append((fcs * gcc_s - fcc * gcs) + (fss * gsc_s - fsc * gss))
        out[2].append((fsc * hcc + fss * hcs) - (fcc * gsc + fcs * gss))
        out[3].append((fss * hcc_s - fsc * hcs) - (fcs * gsc_s - fcc * gss))
    top = jnp.concatenate([jnp.concatenate(out[0], 0), jnp.concatenate(out[1], 0)], axis=1)
    low = jnp.concatenate([jnp.concatenate(out[2], 0), jnp.concatenate(out[3], 0)], axis=1)
    return jnp.concatenate([top, low], axis=0)


def factors(e_ref, first, groups, ones_ref, width):
    energy = exact_dot(e_ref[first : first + groups], ones_ref[...])
    return lax.rsqrt(energy * (1.0 / (width * width)) + EPS_VAR)


def backward(load_f, load_g, scales, sum_ref, right_ref, left_ref, groups, width):
    span = 4 * width
    row = lax.broadcasted_iota(jnp.int32, (8, span), 0)
    special = jnp.where(row == 0, 2.0, 1.0)
    step = 4
    sum_ref[...] = jnp.zeros_like(sum_ref)
    table = right_ref[...]
    table = jnp.concatenate([table[:span], table[:span], table[span:]], axis=0)
    for i in range(0, groups, step):
        highs, lows = [], []
        for j in range(step):
            scale = jnp.broadcast_to(scales[i + j : i + j + 1], (width, span // 2))
            scale = jnp.concatenate([scale, scale], axis=1)
            z = products(load_f(i + j) * scale, load_g(i + j), width)
            high, low = split(z)
            highs.append(high)
            lows.append(low)
        high = jnp.concatenate(highs, axis=0)
        low = jnp.concatenate(lows, axis=0)
        v = dot(jnp.concatenate([high, low, high], axis=1), table)
        for j in range(step):
            u = dot(left_ref[1], jnp.concatenate([highs[j], lows[j], highs[j]], axis=0))
            strength = jnp.zeros((8, span), F32)
            across = jnp.zeros((8, span), F32)
            along = jnp.zeros((8, span), F32)
            for r in range(0, width, 8):
                square = u[r : r + 8] * u[r : r + 8]
                strength = strength + square
                first = r if r < width // 2 else r - width
                across = across + square * (row + first).astype(F32)
                piece = v[j * width + r : j * width + r + 8]
                piece = piece * piece
                if r % (width // 2) == 0:
                    piece = piece * special
                along = along + piece
            tile = i // step
            for kind, value in enumerate((strength, across, along)):
                sum_ref[kind, j, tile : tile + 1, :] = jnp.sum(value, axis=0, keepdims=True)


def finish(sum_ref, sums_ref):
    _, quads, rows, span = sum_ref.shape
    flat = jnp.concatenate([sum_ref[kind, quad] for kind in range(3) for quad in range(quads)], axis=0)
    done = exact_dot(flat, sums_ref[...])
    kinds = []
    for kind in range(3):
        value = jnp.zeros((rows, 128), F32)
        for quad in range(quads):
            base = (kind * quads + quad) * rows
            part = done[base : base + rows, :128] if kind < 2 else done[base : base + rows, 128:]
            value = value + (pltpu.roll(part, 4 * quad, 1) if quad else part)
        kinds.append(value)
    strength, across, along = kinds
    across = across / (strength + EPS_WEIGHT)
    along = along / (strength + EPS_WEIGHT)
    total = jnp.sum(strength, axis=1, keepdims=True) + EPS_WEIGHT
    first = jnp.sum(strength * across, axis=1, keepdims=True) / total
    second = jnp.sum(strength * along, axis=1, keepdims=True) / total
    return across, along, first, second


def at_lane(first, second, where):
    lane = lax.broadcasted_iota(jnp.int32, (8, 128), 1)
    return jnp.where(lane == where, first, 0.0) + jnp.where(lane == where + 1, second, 0.0)


class Copies:
    def __init__(self, sems):
        self.sems, self.count = sems, 0

    def start(self, source, target):
        copy = pltpu.make_async_copy(source, target, self.sems.at[self.count])
        self.count += 1
        copy.start()
        return copy

    def start_either(self, even, first, second, target):
        sem = self.sems.at[self.count]
        self.count += 1

        @pl.when(even)
        def _():
            pltpu.make_async_copy(first, target, sem).start()

        @pl.when(jnp.logical_not(even))
        def _():
            pltpu.make_async_copy(second, target, sem).start()

        return pltpu.make_async_copy(first, target, sem)


def is_even():
    return lax.rem(lax.axis_index("gy"), 2) == 0


def cut_into(target, source, start_ref, sizes):
    width, cell, count = sizes

    def load(k):
        return source[:, k * cell : (k + 1) * cell]

    def store(quad, side, value):
        target[quad, :, side * cell : (side + 1) * cell] = value

    cut_tile(start_ref, load, store, width, cell, count)


def cut_kernel(sizes, rows, start_hbm, west_ref, east_ref, north_ref, send_out, north_out, start_ref, raw_ref, cut_ref, sems):
    copies = Copies(sems)
    even = is_even()
    start = copies.start(start_hbm, start_ref)
    loads = []
    for tile in range(rows):
        loads.append(copies.start_either(even, west_ref.at[0, tile, 0], east_ref.at[0, tile, 0], raw_ref.at[tile]))
    loads.append(copies.start(north_ref.at[0, 0, 0], raw_ref.at[rows]))
    stores = []
    start.wait()
    for tile in range(rows + 1):
        loads[tile].wait()
        cut_into(cut_ref.at[tile], raw_ref.at[tile], start_ref, sizes)
        stores.append(copies.start(cut_ref.at[tile], send_out.at[tile] if tile < rows else north_out.at[0]))
    for store in stores:
        store.wait()


def south_kernel(sizes, rows, start_hbm, south_ref, north_ref, rim_ref, east_ref, west_ref, right_hbm, back_hbm, left_hbm, sums_hbm, ones_hbm, out_ref, q_out, e_out, start_ref, raw_ref, d_ref, q_ref, e_ref, sum_ref, right_ref, back_ref, left_ref, sums_ref, ones_ref, sems):
    width, cell, count = sizes
    quads = count // 4
    groups = rows * quads
    copies = Copies(sems)
    even = is_even()
    batches = [[copies.start(start_hbm, start_ref)], [], []]
    for tile in range(rows):
        batches[0].append(copies.start(south_ref.at[0, tile, 0], raw_ref.at[tile]))
    batches[0] += [copies.start(right_hbm, right_ref), copies.start(left_hbm, left_ref)]
    for tile in range(rows - 1):
        batches[1].append(copies.start(north_ref.at[0, tile + 1, 0], raw_ref.at[rows + tile]))
    for tile in range(rows):
        slot = 2 * rows + tile
        batches[2].append(copies.start_either(even, east_ref.at[0, tile, 0], west_ref.at[0, tile, 0], raw_ref.at[slot]))
    batches[2] += [copies.start(back_hbm, back_ref), copies.start(sums_hbm, sums_ref), copies.start(ones_hbm, ones_ref)]

    def arrive(batch):
        for copy in batches[batch]:
            copy.wait()

    def cut(batch):
        for slot in range(batch * rows, (batch + 1) * rows):
            if slot != 2 * rows - 1:
                cut_into(d_ref.at[slot], raw_ref.at[slot], start_ref, sizes)

    def transform(batch):
        def source(i):
            slot = batch * rows + i // quads
            value = rim_ref[0] if slot == 2 * rows - 1 else d_ref[slot]
            return value.reshape(quads * width, 4 * width)

        forward(source, q_ref, e_ref, right_ref, left_ref, batch * groups, groups, width)

    arrive(0)
    cut(0)
    arrive(1)
    transform(0)
    cut(1)
    arrive(2)
    transform(1)
    cut(2)
    transform(2)
    own = copies.start(q_ref.at[2 * groups : 3 * groups], q_out)
    e_out[...] = e_ref[2 * groups : 3 * groups]
    scales = factors(e_ref, 0, groups, ones_ref, width) * factors(e_ref, groups, groups, ones_ref, width)
    backward(lambda i: q_ref[i], lambda i: q_ref[groups + i], scales, sum_ref, back_ref, left_ref, groups, width)
    across, along, first, second = finish(sum_ref, sums_ref)
    out_ref[...] = pltpu.roll(across, SOUTH, 1) + pltpu.roll(along, SOUTH + 16, 1) + at_lane(first, second, D_SOUTH)
    own.wait()


def east_kernel(sizes, rows, received_ref, q_own, e_own, south_ref, position_ref, col_ref, row_ref, right_hbm, back_hbm, left_hbm, sums_hbm, ones_hbm, out_ref, q_ref, e_ref, sum_ref, right_ref, back_ref, left_ref, sums_ref, ones_ref, place_ref, sems):
    width, cell, count = sizes
    quads = count // 4
    groups = rows * quads
    copies = Copies(sems)
    arriving = [copies.start(right_hbm, right_ref), copies.start(left_hbm, left_ref)]
    own = [copies.start(q_own, q_ref.at[0]), copies.start(back_hbm, back_ref), copies.start(sums_hbm, sums_ref), copies.start(ones_hbm, ones_ref)]
    for copy in arriving:
        copy.wait()

    def source(i):
        return received_ref[i // quads].reshape(quads * width, 4 * width)

    forward(source, q_ref.at[1], e_ref, right_ref, left_ref, 0, groups, width)
    for copy in own:
        copy.wait()
    scales = factors(e_ref, 0, groups, ones_ref, width) * factors(e_own, 0, groups, ones_ref, width)
    odd = lax.rem(lax.axis_index("gy"), 2)
    backward(lambda i: q_ref[odd, i], lambda i: q_ref[1 - odd, i], scales, sum_ref, back_ref, left_ref, groups, width)
    across, along, first, second = finish(sum_ref, sums_ref)
    place_ref[...] = jnp.zeros_like(place_ref)
    place_ref[0:2, 0:rows] = position_ref[0, 0]
    place_ref[2:3, 0:rows] = col_ref[0]
    place_ref[3:4, 0:rows] = row_ref[0]
    lane = lax.broadcasted_iota(jnp.int32, (8, 128), 1)
    row = lax.broadcasted_iota(jnp.int32, (8, 128), 0)
    packet = south_ref[...] + across + pltpu.roll(along, EAST + 16, 1) + at_lane(first, second, D_EAST)
    for field, where in enumerate((POSITION, POSITION + 1, COL, ROW)):
        value = jnp.where(lane == row, place_ref[field : field + 1, :], 0.0)
        packet = packet + jnp.where(lane == where, jnp.sum(value, axis=1, keepdims=True), 0.0)
    out_ref[...] = jnp.broadcast_to(packet[None], out_ref.shape)


def turned(value, by):
    count = value.shape[0]
    by = by % count
    return value if by == 0 else jnp.concatenate([value[by:], value[:by]], axis=0)


def relax_kernel(counts, rows, patches, all_ref, shift_ref, placed_ref, x_ref):
    nx, nz, ny = counts
    total = nx * nz * ny
    packet = all_ref[...]
    sub = lax.broadcasted_iota(jnp.int32, packet.shape, 1)
    device = lax.broadcasted_iota(jnp.int32, packet.shape, 0)
    gx, gz, gy = device // (nz * ny), device // ny % nz, device % ny

    def field(where):
        return pltpu.roll(packet, 128 - where, 2)

    def one(where):
        return jnp.broadcast_to(packet[:, :, where : where + 1], packet.shape)

    def east(value):
        return turned(value, nz * ny)

    def west(value):
        return turned(value, -nz * ny)

    def south(value):
        inside = pltpu.roll(value, 7, 1)
        beyond = pltpu.roll(turned(value, 1), rows - 1, 1)
        return jnp.where(sub == rows - 1, beyond, inside)

    def north(value):
        inside = pltpu.roll(value, 1, 1)
        beyond = pltpu.roll(turned(value, -1), 8 - (rows - 1), 1)
        return jnp.where(sub == 0, beyond, inside)

    x = field(POSITION)
    d_east = field(D_EAST)
    d_east = jnp.where(gy % 2 == 0, d_east, east(d_east))
    d_south = field(D_SOUTH)
    ke = jnp.where(gx < nx - 1, one(COL), 0.0)
    ks = jnp.where((gy == ny - 1) & (sub == rows - 1), 0.0, one(ROW))
    kw, d_west = west(ke), west(d_east)
    kn, d_north = north(ks), north(d_south)
    has_next = jnp.where(gz < nz - 1, LINK_STIFF, 0.0)
    has_prev = jnp.where(gz > 0, LINK_STIFF, 0.0)
    for _ in range(ITERS):
        force = ke * (east(x) - x - d_east) - kw * (x - west(x) - d_west)
        force = force + ks * (south(x) - x - d_south) - kn * (x - north(x) - d_north)
        force = force + has_next * (turned(x, ny) - x) + has_prev * (turned(x, -ny) - x)
        x = x + STEP_SIZE * force
    x_ref[...] = x
    mine = lax.axis_index("gy")
    me = (lax.axis_index("gx") * nz + lax.axis_index("gz")) * ny + mine
    holder = lax.rem(me + lax.rem(mine, 2) * (nz * ny), total)
    lane = lax.broadcasted_iota(jnp.int32, (8, 128), 1)
    row = lax.broadcasted_iota(jnp.int32, (8, 128), 0)
    own = x_ref[me]
    for part in range(2):
        value = jnp.where((lane == row) & (row < rows), own[:, part : part + 1], 0.0)
        placed_ref[0, 0, part : part + 1, :] = jnp.sum(value, axis=0, keepdims=True)[:, :rows]
    for kind, (source, where) in enumerate(((all_ref[holder], EAST), (all_ref[me], SOUTH))):
        for part in range(2):
            value = source
            if where + part * patches:
                value = pltpu.roll(source, 128 - where - part * patches, 1)
            for tile in range(rows):
                shift_ref[0, tile, 0, kind, part : part + 1, :] = value[tile : tile + 1, :patches]


def to_pair_owner(block):
    nx, ny = lax.axis_size("gx"), lax.axis_size("gy")
    route = []
    for x in range(nx):
        for y in range(ny):
            target = x - 1 if y % 2 == 0 else x + 1
            if 0 <= target < nx:
                route.append((x * ny + y, target * ny + y))
    return lax.ppermute(block, ("gx", "gy"), route)


def to_north(block):
    return lax.ppermute(block, "gy", [(i, i - 1) for i in range(1, lax.axis_size("gy"))])


def shards(east_strip, west_strip, north_strip, south_strip, patch_start, segment_offset, col_stiffness, row_stiffness):
    _, rows, _, width, length = east_strip.shape
    count = patch_start.shape[0]
    sizes = (width, length // count, count)
    quads = count // 4
    span = 4 * width
    groups = rows * quads
    counts = tuple(lax.axis_size(axis) for axis in PART)
    total = math.prod(counts)
    constants = [jnp.asarray(table) for table in tables(width)]
    vmem = pl.BlockSpec(memory_space=pltpu.VMEM)
    hbm = pl.BlockSpec(memory_space=pl.ANY)

    send, north_cut = pl.pallas_call(
        functools.partial(cut_kernel, sizes, rows),
        out_shape=[
            jax.ShapeDtypeStruct((rows, quads, width, span), BF16),
            jax.ShapeDtypeStruct((1, quads, width, span), BF16),
        ],
        in_specs=[hbm, hbm, hbm, hbm],
        out_specs=[hbm, hbm],
        scratch_shapes=[
            pltpu.SMEM((count,), jnp.int32),
            pltpu.VMEM((rows + 1, width, length), BF16),
            pltpu.VMEM((rows + 1, quads, width, span), BF16),
            pltpu.SemaphoreType.DMA((2 * rows + 3,)),
        ],
        compiler_params=pltpu.CompilerParams(vmem_limit_bytes=CUT_VMEM),
        name="cut",
    )(patch_start, west_strip, east_strip, north_strip)
    received = to_pair_owner(send)
    rim = to_north(north_cut)

    tables_in_vmem = [pltpu.VMEM(table.shape, table.dtype) for table in constants]
    sums = pltpu.VMEM((3, quads, 8, span), F32)
    south, q_own, e_own = pl.pallas_call(
        functools.partial(south_kernel, sizes, rows),
        out_shape=[
            jax.ShapeDtypeStruct((8, 128), F32),
            jax.ShapeDtypeStruct((groups, width, span), F32),
            jax.ShapeDtypeStruct((groups, span // 2), F32),
        ],
        in_specs=[hbm] * 3 + [vmem] + [hbm] * 7,
        out_specs=[vmem, hbm, vmem],
        scratch_shapes=[
            pltpu.SMEM((count,), jnp.int32),
            pltpu.VMEM((3 * rows, width, length), BF16),
            pltpu.VMEM((3 * rows, quads, width, span), BF16),
            pltpu.VMEM((3 * groups, width, span), F32),
            pltpu.VMEM((3 * groups, span // 2), F32),
            sums,
            *tables_in_vmem,
            pltpu.SemaphoreType.DMA((3 * rows + len(constants) + 1,)),
        ],
        compiler_params=pltpu.CompilerParams(vmem_limit_bytes=SOUTH_VMEM),
        cost_estimate=pl.CostEstimate(flops=6_000_000_000, bytes_accessed=8_000_000, transcendentals=0),
        name="south",
    )(patch_start, south_strip, north_strip, rim, east_strip, west_strip, *constants)
    packet = pl.pallas_call(
        functools.partial(east_kernel, sizes, rows),
        out_shape=jax.ShapeDtypeStruct((total, 8, 128), F32),
        in_specs=[vmem, hbm] + [vmem] * 5 + [hbm] * 5,
        out_specs=vmem,
        scratch_shapes=[
            pltpu.VMEM((2, groups, width, span), F32),
            pltpu.VMEM((groups, span // 2), F32),
            sums,
            *tables_in_vmem,
            pltpu.VMEM((8, 128), F32),
            pltpu.SemaphoreType.DMA((1 + len(constants),)),
        ],
        compiler_params=pltpu.CompilerParams(vmem_limit_bytes=EAST_VMEM),
        cost_estimate=pl.CostEstimate(flops=3_000_000_000, bytes_accessed=2_000_000, transcendentals=0),
        name="east",
    )(
        received,
        q_own,
        e_own,
        south,
        jnp.transpose(segment_offset, (0, 2, 3, 1)),
        jnp.transpose(col_stiffness, (0, 2, 1)),
        jnp.transpose(row_stiffness, (0, 2, 1)),
        *constants,
    )
    gathered = lax.all_to_all(packet, PART, 0, 0)
    patch_shift, placed = pl.pallas_call(
        functools.partial(relax_kernel, counts, rows, count),
        out_shape=[
            jax.ShapeDtypeStruct((1, rows, 1, 2, 2, count), F32),
            jax.ShapeDtypeStruct((1, 1, 2, rows), F32),
        ],
        in_specs=[vmem],
        out_specs=[vmem, vmem],
        scratch_shapes=[pltpu.VMEM((total, 8, 128), F32)],
        compiler_params=pltpu.CompilerParams(vmem_limit_bytes=RELAX_VMEM),
        name="relax",
    )(gathered)
    return patch_shift, jnp.transpose(placed, (0, 3, 1, 2))


def solution(mesh):
    placed = (
        P(("groups", "gz"), "gy", "gx", None, None),
        P(("groups", "gz"), "gy", "gx", None, None),
        P(("groups", "gz"), "gy", "gx", None, None),
        P(("groups", "gz"), "gy", "gx", None, None),
        P(),
        P(("groups", "gz"), "gy", "gx", None),
        P(("groups", "gz"), "gy", "gx"),
        P(("groups", "gz"), "gy", "gx"),
    )
    return jax.shard_map(
        shards,
        mesh=mesh,
        in_specs=placed,
        out_specs=(
            P(("groups", "gz"), "gy", "gx", None, None, None),
            P(("groups", "gz"), "gy", "gx", None),
        ),
        check_vma=False,
    )
```

time: 45.9 us -> 34.5 us (0.75)
  local copies, waits for them, and re-layouts: 9.42 us -> 0.72 us
  starting transfers between devices: 8.16 us -> 2.58 us
  waiting for transfers between devices: 0.03 us -> 4.22 us
  Pallas kernels: 14.8 us -> 13.3 us
    unnamed x43 -> x18, local copies, waits for them, and re-layouts: 8.77 us -> 0.72 us
    ppermute x3 -> x2, starting transfers between devices: 8.16 us -> 2.58 us  [the longest x1 1.29 us: to_north(): lax.ppermute(block, 'gy', [(i, i - 1) for i in range(1, lax.axis_size('gy...]
    ppermute x3 -> x2, waiting for transfers between devices: 0.03 us -> 4.22 us  [the longest x1 3.36 us: to_pair_owner(): return lax.ppermute(block, ('gx', 'gy'), route)]
    pallas_call x1, Pallas kernels: 6.44 us -> 3.16 us  [shards(): pl.pallas_call(functools.partial(east_kernel, sizes, rows), out_shape=jax...]
    pallas_call x2, Pallas kernels: 7.53 us -> 9.2 us  [the longest x1 6.72 us: shards(): pl.pallas_call(functools.partial(south_kernel, sizes, rows), out_shape=[j...]
    pallas_call x1 -> x0, local copies, waits for them, and re-layouts: 0.65 us -> none  [shards(): pl.pallas_call(functools.partial(relax_kernel, counts, rows, count), out_...]
  transfers between devices with their start and end apart: 3 -> 2, of which waited for: 0 -> 2; matrix products, arithmetic and copies ran while one was open for 1% -> 0% of each run, Pallas kernels for 14% -> 20%
where the time goes in v1:
time: 34.5 us; the launch traced here: 34.2 us
  Pallas kernels  13.3 us (39%)
  blocking collectives  12.6 us (37%)
  waiting for transfers between devices  4.22 us (12%)
  starting transfers between devices  2.58 us (7%)
  between operations  0.76 us (2%)
  local copies, waits for them, and re-layouts  0.72 us (2%)
    all_to_all x1, blocking collectives, shards(): gathered = lax.all_to_all(packet, PART, 0, 0)  12.6 us
    pallas_call x1, Pallas kernels, shards(): pl.pallas_call(functools.partial(south_kernel, sizes, rows), out_shape=[j...  6.72 us
    ppermute x1, waiting for transfers between devices, to_pair_owner(): return lax.ppermute(block, ('gx', 'gy'), route)  3.36 us
    pallas_call x1, Pallas kernels, shards(): pl.pallas_call(functools.partial(east_kernel, sizes, rows), out_shape=jax...  3.16 us
    pallas_call x1, Pallas kernels, shards(): pl.pallas_call(functools.partial(cut_kernel, sizes, rows), out_shape=[jax...  2.48 us
    ppermute x1, starting transfers between devices, to_north(): lax.ppermute(block, 'gy', [(i, i - 1) for i in range(1, lax.axis_size('gy...  1.29 us
    ppermute x1, starting transfers between devices, to_pair_owner(): return lax.ppermute(block, ('gx', 'gy'), route)  1.29 us
    pallas_call x1, Pallas kernels, shards(): pl.pallas_call(functools.partial(relax_kernel, counts, rows, count), out_...  0.95 us
  transfers between devices with their start and end apart: 2, of which 2 were waited for; matrix products, arithmetic and copies ran while one was open for 0% of the time, Pallas kernels for 20%

profile of v1, /device:TPU:0, one launch (start us, length us, event | category | flops | bytes accessed | tf_op | source)
XLA Modules:
  0.0 34.2 jit_solution(6917560043180748430)
XLA Ops:
  0.6 0.0 copy-start.4
  0.6 0.0 copy-start.5
  0.7 0.0 copy-start.6
  0.7 0.0 copy-start.7
  0.7 0.0 copy-start.8
  0.7 2.5 %cut.1 = (bf16[4,4,64,256]{3,2,1,0:T(8,128)(2,1)}, bf16[1,4,64,256]{3,2,1,0:T(8,128)(2,1)}) custom-call(s32[16]{0:T(128)} %start_hbm.3, bf16[1,4,1,64,2048]{4,3,2,1,0:T(8,128)(2,1)} %west_ref.3, bf16[1,4,1,64,2048]{4,3,2,1,0:T(8,128)(2,1)} %east_ref.3, bf16[1,4,1,64,2048]{4,3,2,1,0:T(8,128)(2,1)} %north_ref.3), custom_call_target="tpu_custom_call" | custom-call | tf_op jit(solution)/shard_map/cut/pallas_call | solution.py:498
  3.2 0.0 copy-start
  3.2 1.3 %collective-permute-start.1 = (bf16[1,4,64,256]{3,2,1,0:T(8,128)(2,1)}, bf16[1,4,64,256]{3,2,1,0:T(8,128)(2,1)S(1)}, u32[]{:S(2)}, u32[]{:S(2)}) collective-permute-start(bf16[1,4,64,256]{3,2,1,0:T(8,128)(2,1)} %get-tuple-element.10), channel_id=1, source_target_pairs={{2,0},{3,1},{6,4},{7,5},{10,8},{11,9},{14,12},{15,13},{18,16},{19,... | collective-permute-start | bytes 393224 | tf_op jit(solution)/shard_map/ppermute | solution.py:482
  4.5 1.3 %collective-permute-start = (bf16[4,4,64,256]{3,2,1,0:T(8,128)(2,1)}, bf16[4,4,64,256]{3,2,1,0:T(8,128)(2,1)S(1)}, u32[]{:S(2)}, u32[]{:S(2)}) collective-permute-start(bf16[4,4,64,256]{3,2,1,0:T(8,128)(2,1)} %get-tuple-element.9), channel_id=1, source_target_pairs={{2,6},{4,0},{6,10},{8,4},{10,14},{12,8},{3,7},{5,1},{7,11},{9,5},{... | collective-permute-start | bytes 1572872 | tf_op jit(solution)/shard_map/ppermute | solution.py:478
  5.8 0.9 %collective-permute-done.1.rim_ref = bf16[1,4,64,256]{3,2,1,0:T(8,128)(2,1)S(1)} collective-permute-done((bf16[1,4,64,256]{3,2,1,0:T(8,128)(2,1)}, bf16[1,4,64,256]{3,2,1,0:T(8,128)(2,1)S(1)}, u32[]{:S(2)}, u32[]{:S(2)}) %collective-permute-start.1) | collective-permute-done | bytes 131104 | tf_op jit(solution)/shard_map/ppermute | solution.py:482
  6.6 0.0 copy-done.4
  6.7 0.0 copy-done.5
  6.7 0.0 copy-done.6
  6.7 0.0 copy-done.7
  6.7 0.0 copy-done.8
  6.7 0.0 copy-done
  6.7 0.0 copy-start.3
  6.7 6.7 %south.1 = (f32[8,128]{1,0:T(8,128)S(1)}, f32[16,64,256]{2,1,0:T(8,128)S(1)}, f32[16,128]{1,0:T(8,128)S(1)}) custom-call(s32[16]{0:T(128)S(1)} %copy-done, bf16[1,4,1,64,2048]{4,3,2,1,0:T(8,128)(2,1)} %south_ref.1, bf16[1,4,1,64,2048]{4,3,2,1,0:T(8,128)(2,1)} %north_ref.3, bf16[1,4,64,256]{3,2,1,0:T(8,128)(2,1)S(1)} %collective-permute-done.1.rim_ref, ...), custom_call_target="tpu_custom_call" | custom-call | flops 6000000000 | bytes 8000000 | tf_op jit(solution)/shard_map/south/pallas_call | solution.py:520
  13.4 3.4 %collective-permute-done.received_ref = bf16[4,4,64,256]{3,2,1,0:T(8,128)(2,1)S(1)} collective-permute-done((bf16[4,4,64,256]{3,2,1,0:T(8,128)(2,1)}, bf16[4,4,64,256]{3,2,1,0:T(8,128)(2,1)S(1)}, u32[]{:S(2)}, u32[]{:S(2)}) %collective-permute-start) | collective-permute-done | bytes 524320 | tf_op jit(solution)/shard_map/ppermute | solution.py:478
  16.8 0.0 copy-start.1
  16.8 0.0 copy-start.2
  16.8 0.0 copy-done.3
  16.8 0.7 %copy-done.1 = f32[1,4,1,2]{1,3,2,0:T(2,128)S(1)} copy-done((f32[1,4,1,2]{1,3,2,0:T(2,128)S(1)}, f32[1,4,1,2]{1,3,2,0:T(2,128)}, u32[]{:S(2)}) %copy-start.1) | copy-done | bytes 56
  17.5 0.0 copy-done.2
  17.5 3.2 %east.1 = f32[16,8,128]{2,1,0:T(8,128)S(1)} custom-call(bf16[4,4,64,256]{3,2,1,0:T(8,128)(2,1)S(1)} %collective-permute-done.received_ref, f32[16,64,256]{2,1,0:T(8,128)S(1)} %get-tuple-element.11.q_own, f32[16,128]{1,0:T(8,128)S(1)} %get-tuple-element.12.e_own, f32[8,128]{1,0:T(8,128)S(1)} %get-tuple-element.13.south_ref, f32[1,1,2,4]{3,2,1,0:T(2,128)S(1)} %bitcast.4, ...), custom_call_target="tpu_custom_call" | custom-call | flops 3000000000 | bytes 2000000 | tf_op jit(solution)/shard_map/east/pallas_call | solution.py:543
  20.6 12.6 %all_to_all.5.all_ref = f32[16,8,128]{2,1,0:T(8,128)S(1)} all-to-all(f32[16,8,128]{2,1,0:T(8,128)S(1)} %east.1), channel_id=1, replica_groups=mesh['groups'=2,'gx'=4,'gy'=2,'gz'=2] {'gx','gz','gy'}, dimensions={0} | all-to-all | bytes 131072 | tf_op jit(solution)/shard_map/all_to_all | solution.py:569
  33.3 1.0 %relax.1 = (f32[1,4,1,2,2,16]{5,4,3,2,1,0:T(2,128)}, f32[1,1,2,4]{3,2,1,0:T(2,128)}) custom-call(f32[16,8,128]{2,1,0:T(8,128)S(1)} %all_to_all.5.all_ref), custom_call_target="tpu_custom_call" | custom-call | tf_op jit(solution)/shard_map/relax/pallas_call | solution.py:570
Async XLA Ops:
  0.6 6.0 %copy-start.4 = (bf16[512,256]{1,0:T(8,128)(2,1)S(1)}, bf16[512,256]{1,0:T(8,128)(2,1)}, u32[]{:S(2)}) copy-start(bf16[512,256]{1,0:T(8,128)(2,1)} %constant.11.clone.back_hbm) | copy-start | bytes 786436
  0.6 6.0 %copy-start.5 = (bf16[512,256]{1,0:T(8,128)(2,1)S(1)}, bf16[512,256]{1,0:T(8,128)(2,1)}, u32[]{:S(2)}) copy-start(bf16[512,256]{1,0:T(8,128)(2,1)} %constant.10.clone.right_hbm) | copy-start | bytes 786436
  0.7 6.0 %copy-start.6 = (bf16[256,256]{1,0:T(8,128)(2,1)S(1)}, bf16[256,256]{1,0:T(8,128)(2,1)}, u32[]{:S(2)}) copy-start(bf16[256,256]{1,0:T(8,128)(2,1)} %constant.13.clone.sums_hbm) | copy-start | bytes 393220
  0.7 6.0 %copy-start.7 = (bf16[2,64,192]{2,1,0:T(8,128)(2,1)S(1)}, bf16[2,64,192]{2,1,0:T(8,128)(2,1)}, u32[]{:S(2)}) copy-start(bf16[2,64,192]{2,1,0:T(8,128)(2,1)} %constant.12.clone.left_hbm) | copy-start | bytes 147460
  0.7 6.0 %copy-start.8 = (bf16[128,128]{1,0:T(8,128)(2,1)S(1)}, bf16[128,128]{1,0:T(8,128)(2,1)}, u32[]{:S(2)}) copy-start(bf16[128,128]{1,0:T(8,128)(2,1)} %constant.14.clone.ones_hbm) | copy-start | bytes 98308
  3.2 3.5 %copy-start = (s32[16]{0:T(128)S(1)}, s32[16]{0:T(128)}, u32[]{:S(2)}) copy-start(s32[16]{0:T(128)} %start_hbm.3) | copy-start | bytes 196
  3.2 3.5 %collective-permute-start.1 = (bf16[1,4,64,256]{3,2,1,0:T(8,128)(2,1)}, bf16[1,4,64,256]{3,2,1,0:T(8,128)(2,1)S(1)}, u32[]{:S(2)}, u32[]{:S(2)}) collective-permute-start(bf16[1,4,64,256]{3,2,1,0:T(8,128)(2,1)} %get-tuple-element.10), channel_id=1, source_target_pairs={{2,0},{3,1},{6,4},{7,5},{10,8},{11,9},{14,12},{15,13},{18,16},{19,... | collective-permute-start | bytes 393224 | tf_op jit(solution)/shard_map/ppermute | solution.py:482
  4.5 12.3 %collective-permute-start = (bf16[4,4,64,256]{3,2,1,0:T(8,128)(2,1)}, bf16[4,4,64,256]{3,2,1,0:T(8,128)(2,1)S(1)}, u32[]{:S(2)}, u32[]{:S(2)}) collective-permute-start(bf16[4,4,64,256]{3,2,1,0:T(8,128)(2,1)} %get-tuple-element.9), channel_id=1, source_target_pairs={{2,6},{4,0},{6,10},{8,4},{10,14},{12,8},{3,7},{5,1},{7,11},{9,5},{... | collective-permute-start | bytes 1572872 | tf_op jit(solution)/shard_map/ppermute | solution.py:478
  6.7 10.1 %copy-start.3 = (f32[1,4,1]{1,2,0:T(1,128)S(1)}, f32[1,4,1]{1,2,0:T(1,128)}, u32[]{:S(2)}) copy-start(f32[1,4,1]{1,2,0:T(1,128)} %param.20) | copy-start | bytes 52
  16.8 0.7 %copy-start.1 = (f32[1,4,1,2]{1,3,2,0:T(2,128)S(1)}, f32[1,4,1,2]{1,3,2,0:T(2,128)}, u32[]{:S(2)}) copy-start(f32[1,4,1,2]{1,3,2,0:T(2,128)} %param.18) | copy-start | bytes 100
  16.8 0.7 %copy-start.2 = (f32[1,4,1]{1,2,0:T(1,128)S(1)}, f32[1,4,1]{1,2,0:T(1,128)}, u32[]{:S(2)}) copy-start(f32[1,4,1]{1,2,0:T(1,128)} %param.19) | copy-start | bytes 52

commit v2 on v1

--- a/solution.py
+++ b/solution.py
@@ -18,7 +18,7 @@
 BF16 = jnp.bfloat16
 PART = ("gx", "gz", "gy")
 MIB = 1024 * 1024
-CUT_VMEM, SOUTH_VMEM, EAST_VMEM, RELAX_VMEM = 62 * MIB, 52 * MIB, 32 * MIB, 16 * MIB
+CUT_VMEM, SOUTH_VMEM, EAST_VMEM, RELAX_VMEM = 62 * MIB, 52 * MIB, 52 * MIB, 16 * MIB
 
 EAST, SOUTH = 0, 32
 D_SOUTH, D_EAST, POSITION, COL, ROW = 64, 66, 68, 70, 71
@@ -192,7 +192,6 @@
     row = lax.broadcasted_iota(jnp.int32, (8, span), 0)
     special = jnp.where(row == 0, 2.0, 1.0)
     step = 4
-    sum_ref[...] = jnp.zeros_like(sum_ref)
     table = right_ref[...]
     table = jnp.concatenate([table[:span], table[:span], table[span:]], axis=0)
     for i in range(0, groups, step):
@@ -242,15 +241,16 @@
     strength, across, along = kinds
     across = across / (strength + EPS_WEIGHT)
     along = along / (strength + EPS_WEIGHT)
+    return strength, across, along
+
+
+def pack(strength, across, along, where, offset):
+    lane = lax.broadcasted_iota(jnp.int32, (8, 128), 1)
     total = jnp.sum(strength, axis=1, keepdims=True) + EPS_WEIGHT
     first = jnp.sum(strength * across, axis=1, keepdims=True) / total
     second = jnp.sum(strength * along, axis=1, keepdims=True) / total
-    return across, along, first, second
-
-
-def at_lane(first, second, where):
-    lane = lax.broadcasted_iota(jnp.int32, (8, 128), 1)
-    return jnp.where(lane == where, first, 0.0) + jnp.where(lane == where + 1, second, 0.0)
+    shifts = (pltpu.roll(across, where, 1) if where else across) + pltpu.roll(along, where + 16, 1)
+    return shifts + jnp.where(lane == offset, first, 0.0) + jnp.where(lane == offset + 1, second, 0.0)
 
 
 class Copies:
@@ -294,7 +294,7 @@
     cut_tile(start_ref, load, store, width, cell, count)
 
 
-def cut_kernel(sizes, rows, start_hbm, west_ref, east_ref, north_ref, send_out, north_out, start_ref, raw_ref, cut_ref, sems):
+def cut_kernel(sizes, rows, start_hbm, west_ref, east_ref, north_ref, send_ref, rim_ref, start_ref, raw_ref, sems):
     copies = Copies(sems)
     even = is_even()
     start = copies.start(start_hbm, start_ref)
@@ -302,49 +302,46 @@
     for tile in range(rows):
         loads.append(copies.start_either(even, west_ref.at[0, tile, 0], east_ref.at[0, tile, 0], raw_ref.at[tile]))
     loads.append(copies.start(north_ref.at[0, 0, 0], raw_ref.at[rows]))
-    stores = []
     start.wait()
     for tile in range(rows + 1):
         loads[tile].wait()
-        cut_into(cut_ref.at[tile], raw_ref.at[tile], start_ref, sizes)
-        stores.append(copies.start(cut_ref.at[tile], send_out.at[tile] if tile < rows else north_out.at[0]))
-    for store in stores:
-        store.wait()
-
-
-def south_kernel(sizes, rows, start_hbm, south_ref, north_ref, rim_ref, east_ref, west_ref, right_hbm, back_hbm, left_hbm, sums_hbm, ones_hbm, out_ref, q_out, e_out, start_ref, raw_ref, d_ref, q_ref, e_ref, sum_ref, right_ref, back_ref, left_ref, sums_ref, ones_ref, sems):
+        target = send_ref.at[tile] if tile < rows else rim_ref.at[0]
+        cut_into(target, raw_ref.at[tile], start_ref, sizes)
+
+
+def south_kernel(sizes, rows, start_hbm, south_ref, north_ref, east_ref, west_ref, position_ref, col_ref, row_ref, right_ref, back_ref, left_ref, sums_ref, ones_ref, out_ref, q_out, e_out, start_ref, raw_ref, d_ref, q_ref, e_ref, sum_ref, place_ref, sems):
     width, cell, count = sizes
     quads = count // 4
     groups = rows * quads
+    inner = groups - quads
     copies = Copies(sems)
     even = is_even()
     batches = [[copies.start(start_hbm, start_ref)], [], []]
+    for tile in range(rows - 1):
+        batches[0].append(copies.start(south_ref.at[0, tile, 0], raw_ref.at[tile]))
+    for tile in range(rows - 1):
+        batches[1].append(copies.start(north_ref.at[0, tile + 1, 0], raw_ref.at[rows - 1 + tile]))
+    batches[2].append(copies.start(south_ref.at[0, rows - 1, 0], raw_ref.at[2 * rows - 2]))
     for tile in range(rows):
-        batches[0].append(copies.start(south_ref.at[0, tile, 0], raw_ref.at[tile]))
-    batches[0] += [copies.start(right_hbm, right_ref), copies.start(left_hbm, left_ref)]
-    for tile in range(rows - 1):
-        batches[1].append(copies.start(north_ref.at[0, tile + 1, 0], raw_ref.at[rows + tile]))
-    for tile in range(rows):
-        slot = 2 * rows + tile
+        slot = 2 * rows - 1 + tile
         batches[2].append(copies.start_either(even, east_ref.at[0, tile, 0], west_ref.at[0, tile, 0], raw_ref.at[slot]))
-    batches[2] += [copies.start(back_hbm, back_ref), copies.start(sums_hbm, sums_ref), copies.start(ones_hbm, ones_ref)]
+    slots = [range(0, rows - 1), range(rows - 1, 2 * rows - 2), range(2 * rows - 2, 3 * rows - 1)]
 
     def arrive(batch):
         for copy in batches[batch]:
             copy.wait()
 
     def cut(batch):
-        for slot in range(batch * rows, (batch + 1) * rows):
-            if slot != 2 * rows - 1:
-                cut_into(d_ref.at[slot], raw_ref.at[slot], start_ref, sizes)
+        for slot in slots[batch]:
+            cut_into(d_ref.at[slot], raw_ref.at[slot], start_ref, sizes)
 
     def transform(batch):
+        first = slots[batch][0]
+
         def source(i):
-            slot = batch * rows + i // quads
-            value = rim_ref[0] if slot == 2 * rows - 1 else d_ref[slot]
-            return value.reshape(quads * width, 4 * width)
-
-        forward(source, q_ref, e_ref, right_ref, left_ref, batch * groups, groups, width)
+            return d_ref[first + i // quads].reshape(quads * width, 4 * width)
+
+        forward(source, q_ref, e_ref, right_ref, left_ref, first * quads, len(slots[batch]) * quads, width)
 
     arrive(0)
     cut(0)
@@ -355,45 +352,61 @@
     transform(1)
     cut(2)
     transform(2)
-    own = copies.start(q_ref.at[2 * groups : 3 * groups], q_out)
-    e_out[...] = e_ref[2 * groups : 3 * groups]
-    scales = factors(e_ref, 0, groups, ones_ref, width) * factors(e_ref, groups, groups, ones_ref, width)
-    backward(lambda i: q_ref[i], lambda i: q_ref[groups + i], scales, sum_ref, back_ref, left_ref, groups, width)
-    across, along, first, second = finish(sum_ref, sums_ref)
-    out_ref[...] = pltpu.roll(across, SOUTH, 1) + pltpu.roll(along, SOUTH + 16, 1) + at_lane(first, second, D_SOUTH)
-    own.wait()
-
-
-def east_kernel(sizes, rows, received_ref, q_own, e_own, south_ref, position_ref, col_ref, row_ref, right_hbm, back_hbm, left_hbm, sums_hbm, ones_hbm, out_ref, q_ref, e_ref, sum_ref, right_ref, back_ref, left_ref, sums_ref, ones_ref, place_ref, sems):
-    width, cell, count = sizes
-    quads = count // 4
-    groups = rows * quads
-    copies = Copies(sems)
-    arriving = [copies.start(right_hbm, right_ref), copies.start(left_hbm, left_ref)]
-    own = [copies.start(q_own, q_ref.at[0]), copies.start(back_hbm, back_ref), copies.start(sums_hbm, sums_ref), copies.start(ones_hbm, ones_ref)]
-    for copy in arriving:
-        copy.wait()
-
-    def source(i):
-        return received_ref[i // quads].reshape(quads * width, 4 * width)
-
-    forward(source, q_ref.at[1], e_ref, right_ref, left_ref, 0, groups, width)
-    for copy in own:
-        copy.wait()
-    scales = factors(e_ref, 0, groups, ones_ref, width) * factors(e_own, 0, groups, ones_ref, width)
-    odd = lax.rem(lax.axis_index("gy"), 2)
-    backward(lambda i: q_ref[odd, i], lambda i: q_ref[1 - odd, i], scales, sum_ref, back_ref, left_ref, groups, width)
-    across, along, first, second = finish(sum_ref, sums_ref)
+    kept = slots[2][0] * quads
+    own = copies.start(q_ref.at[kept : kept + groups + quads], q_out)
+    e_out[...] = e_ref[kept : kept + groups + quads]
+    scales = factors(e_ref, 0, inner, ones_ref, width) * factors(e_ref, inner, inner, ones_ref, width)
+    sum_ref[...] = jnp.zeros_like(sum_ref)
+    backward(lambda i: q_ref[i], lambda i: q_ref[inner + i], scales, sum_ref, back_ref, left_ref, inner, width)
+    strength, across, along = finish(sum_ref, sums_ref)
     place_ref[...] = jnp.zeros_like(place_ref)
     place_ref[0:2, 0:rows] = position_ref[0, 0]
     place_ref[2:3, 0:rows] = col_ref[0]
     place_ref[3:4, 0:rows] = row_ref[0]
     lane = lax.broadcasted_iota(jnp.int32, (8, 128), 1)
     row = lax.broadcasted_iota(jnp.int32, (8, 128), 0)
-    packet = south_ref[...] + across + pltpu.roll(along, EAST + 16, 1) + at_lane(first, second, D_EAST)
+    packet = pack(strength, across, along, SOUTH, D_SOUTH)
     for field, where in enumerate((POSITION, POSITION + 1, COL, ROW)):
         value = jnp.where(lane == row, place_ref[field : field + 1, :], 0.0)
         packet = packet + jnp.where(lane == where, jnp.sum(value, axis=1, keepdims=True), 0.0)
+    out_ref[...] = packet
+    own.wait()
+
+
+def east_kernel(sizes, rows, received_ref, rim_ref, q_own, e_own, south_ref, right_ref, back_ref, left_ref, sums_ref, ones_ref, out_ref, q_ref, e_ref, sum_ref, sems):
+    width, cell, count = sizes
+    quads = count // 4
+    groups = rows * quads
+    own = Copies(sems).start(q_own, q_ref.at[0])
+
+    def source(i):
+        value = rim_ref[0] if i < quads else received_ref[i // quads - 1]
+        return value.reshape(quads * width, 4 * width)
+
+    forward(source, q_ref.at[1], e_ref, right_ref, left_ref, 0, quads + groups, width)
+    scales = factors(e_ref, 0, quads + groups, ones_ref, width) * factors(e_own, 0, quads + groups, ones_ref, width)
+    own.wait()
+    odd = lax.rem(lax.axis_index("gy"), 2)
+    sum_ref[...] = jnp.zeros_like(sum_ref)
+    backward(
+        lambda i: q_ref[0 if i < quads else odd, i],
+        lambda i: q_ref[1 if i < quads else 1 - odd, i],
+        scales,
+        sum_ref,
+        back_ref,
+        left_ref,
+        quads + groups,
+        width,
+    )
+    strength, across, along = finish(sum_ref, sums_ref)
+    row = lax.broadcasted_iota(jnp.int32, (8, 128), 0)
+
+    def only(value, keep):
+        return jnp.where(keep, value, 0.0)
+
+    rim = [only(pltpu.roll(value, rows - 1, 0), row == rows - 1) for value in (strength, across, along)]
+    east = [only(pltpu.roll(value, 7, 0), row < rows) for value in (strength, across, along)]
+    packet = south_ref[...] + pack(*rim, SOUTH, D_SOUTH) + pack(*east, EAST, D_EAST)
     out_ref[...] = jnp.broadcast_to(packet[None], out_ref.shape)
 
 
@@ -495,77 +508,75 @@
     vmem = pl.BlockSpec(memory_space=pltpu.VMEM)
     hbm = pl.BlockSpec(memory_space=pl.ANY)
 
-    send, north_cut = pl.pallas_call(
+    send, rim_cut = pl.pallas_call(
         functools.partial(cut_kernel, sizes, rows),
         out_shape=[
             jax.ShapeDtypeStruct((rows, quads, width, span), BF16),
             jax.ShapeDtypeStruct((1, quads, width, span), BF16),
         ],
-        in_specs=[hbm, hbm, hbm, hbm],
-        out_specs=[hbm, hbm],
+        in_specs=[hbm] * 4,
+        out_specs=[vmem, vmem],
         scratch_shapes=[
             pltpu.SMEM((count,), jnp.int32),
             pltpu.VMEM((rows + 1, width, length), BF16),
-            pltpu.VMEM((rows + 1, quads, width, span), BF16),
-            pltpu.SemaphoreType.DMA((2 * rows + 3,)),
+            pltpu.SemaphoreType.DMA((rows + 2,)),
         ],
         compiler_params=pltpu.CompilerParams(vmem_limit_bytes=CUT_VMEM),
         name="cut",
     )(patch_start, west_strip, east_strip, north_strip)
     received = to_pair_owner(send)
-    rim = to_north(north_cut)
-
-    tables_in_vmem = [pltpu.VMEM(table.shape, table.dtype) for table in constants]
+    rim = to_north(rim_cut)
+
     sums = pltpu.VMEM((3, quads, 8, span), F32)
+    kept = groups + quads
     south, q_own, e_own = pl.pallas_call(
         functools.partial(south_kernel, sizes, rows),
         out_shape=[
             jax.ShapeDtypeStruct((8, 128), F32),
-            jax.ShapeDtypeStruct((groups, width, span), F32),
-            jax.ShapeDtypeStruct((groups, span // 2), F32),
+            jax.ShapeDtypeStruct((kept, width, span), F32),
+            jax.ShapeDtypeStruct((kept, span // 2), F32),
         ],
-        in_specs=[hbm] * 3 + [vmem] + [hbm] * 7,
+        in_specs=[hbm] * 5 + [vmem] * 8,
         out_specs=[vmem, hbm, vmem],
         scratch_shapes=[
             pltpu.SMEM((count,), jnp.int32),
-            pltpu.VMEM((3 * rows, width, length), BF16),
-            pltpu.VMEM((3 * rows, quads, width, span), BF16),
-            pltpu.VMEM((3 * groups, width, span), F32),
-            pltpu.VMEM((3 * groups, span // 2), F32),
+            pltpu.VMEM((3 * rows - 1, width, length), BF16),
+            pltpu.VMEM((3 * rows - 1, quads, width, span), BF16),
+            pltpu.VMEM((3 * groups - quads, width, span), F32),
+            pltpu.VMEM((3 * groups - quads, span // 2), F32),
             sums,
-            *tables_in_vmem,
-            pltpu.SemaphoreType.DMA((3 * rows + len(constants) + 1,)),
+            pltpu.VMEM((8, 128), F32),
+            pltpu.SemaphoreType.DMA((3 * rows + 1,)),
         ],
         compiler_params=pltpu.CompilerParams(vmem_limit_bytes=SOUTH_VMEM),
-        cost_estimate=pl.CostEstimate(flops=6_000_000_000, bytes_accessed=8_000_000, transcendentals=0),
+        cost_estimate=pl.CostEstimate(flops=1_000, bytes_accessed=1_000, transcendentals=0),
         name="south",
-    )(patch_start, south_strip, north_strip, rim, east_strip, west_strip, *constants)
-    packet = pl.pallas_call(
-        functools.partial(east_kernel, sizes, rows),
-        out_shape=jax.ShapeDtypeStruct((total, 8, 128), F32),
-        in_specs=[vmem, hbm] + [vmem] * 5 + [hbm] * 5,
-        out_specs=vmem,
-        scratch_shapes=[
-            pltpu.VMEM((2, groups, width, span), F32),
-            pltpu.VMEM((groups, span // 2), F32),
-            sums,
-            *tables_in_vmem,
-            pltpu.VMEM((8, 128), F32),
-            pltpu.SemaphoreType.DMA((1 + len(constants),)),
-        ],
-        compiler_params=pltpu.CompilerParams(vmem_limit_bytes=EAST_VMEM),
-        cost_estimate=pl.CostEstimate(flops=3_000_000_000, bytes_accessed=2_000_000, transcendentals=0),
-        name="east",
     )(
-        received,
-        q_own,
-        e_own,
-        south,
+        patch_start,
+        south_strip,
+        north_strip,
+        east_strip,
+        west_strip,
         jnp.transpose(segment_offset, (0, 2, 3, 1)),
         jnp.transpose(col_stiffness, (0, 2, 1)),
         jnp.transpose(row_stiffness, (0, 2, 1)),
         *constants,
     )
+    packet = pl.pallas_call(
+        functools.partial(east_kernel, sizes, rows),
+        out_shape=jax.ShapeDtypeStruct((total, 8, 128), F32),
+        in_specs=[vmem, vmem, hbm] + [vmem] * 7,
+        out_specs=vmem,
+        scratch_shapes=[
+            pltpu.VMEM((2, kept, width, span), F32),
+            pltpu.VMEM((kept, span // 2), F32),
+            sums,
+            pltpu.SemaphoreType.DMA((1,)),
+        ],
+        compiler_params=pltpu.CompilerParams(vmem_limit_bytes=EAST_VMEM),
+        cost_estimate=pl.CostEstimate(flops=3_000_000_000, bytes_accessed=2_000_000, transcendentals=0),
+        name="east",
+    )(received, rim, q_own, e_own, south, *constants)
     gathered = lax.all_to_all(packet, PART, 0, 0)
     patch_shift, placed = pl.pallas_call(
         functools.partial(relax_kernel, counts, rows, count),

time: 34.5 us -> 32.2 us (0.933)
  Pallas kernels: 13.3 us -> 12.6 us
  local copies, waits for them, and re-layouts: 0.72 us -> 0.06 us
  waiting for transfers between devices: 4.22 us -> 3.69 us
  blocking collectives: 12.6 us -> 12.2 us
    ppermute x1, waiting for transfers between devices: 0.85 us -> 0.01 us  [to_north(): lax.ppermute(block, 'gy', [(i, i - 1) for i in range(1, lax.axis_size('gy...]
    pallas_call x1, Pallas kernels: 6.72 us -> 5.89 us  [shards(): pl.pallas_call(functools.partial(south_kernel, sizes, rows), out_shape=[j...]
    unnamed x18 -> x20, local copies, waits for them, and re-layouts: 0.72 us -> 0.06 us
    all_to_all x1, blocking collectives: 12.6 us -> 12.2 us  [shards(): gathered = lax.all_to_all(packet, PART, 0, 0)]
  transfers between devices with their start and end apart: 2 -> 2, of which waited for: 2 -> 1; matrix products, arithmetic and copies ran while one was open for 0% -> 0% of each run, Pallas kernels for 20% -> 18%
where the time goes in v2:
time: 32.2 us; the launch traced here: 32 us
  Pallas kernels  12.6 us (39%)
  blocking collectives  12.2 us (38%)
  waiting for transfers between devices  3.69 us (11%)
  starting transfers between devices  2.58 us (8%)
  between operations  0.84 us (3%)
    all_to_all x1, blocking collectives, shards(): gathered = lax.all_to_all(packet, PART, 0, 0)  12.2 us
    pallas_call x1, Pallas kernels, shards(): pl.pallas_call(functools.partial(south_kernel, sizes, rows), out_shape=[j...  5.89 us
    ppermute x1, waiting for transfers between devices, to_pair_owner(): return lax.ppermute(block, ('gx', 'gy'), route)  3.68 us
    pallas_call x1, Pallas kernels, shards(): pl.pallas_call(functools.partial(east_kernel, sizes, rows), out_shape=jax...  3.17 us
    pallas_call x1, Pallas kernels, shards(): pl.pallas_call(functools.partial(cut_kernel, sizes, rows), out_shape=[jax...  2.61 us
    ppermute x1, starting transfers between devices, to_pair_owner(): return lax.ppermute(block, ('gx', 'gy'), route)  1.29 us
    ppermute x1, starting transfers between devices, to_north(): lax.ppermute(block, 'gy', [(i, i - 1) for i in range(1, lax.axis_size('gy...  1.29 us
    pallas_call x1, Pallas kernels, shards(): pl.pallas_call(functools.partial(relax_kernel, counts, rows, count), out_...  0.95 us
  transfers between devices with their start and end apart: 2, of which 1 were waited for; matrix products, arithmetic and copies ran while one was open for 0% of the time, Pallas kernels for 18%

profile of v2, /device:TPU:0, one launch (start us, length us, event | category | flops | bytes accessed | tf_op | source)
XLA Modules:
  0.0 32.0 jit_solution(6938699120654178013)
XLA Ops:
  0.6 0.0 copy-start.1
  0.6 0.0 copy-start.2
  0.7 0.0 copy-start.3
  0.7 0.0 copy-start.4
  0.7 0.0 copy-start.5
  0.7 0.0 copy-start.6
  0.7 0.0 copy-start.9
  0.7 0.0 copy-start.8
  0.7 0.0 copy-start.7
  0.7 0.0 copy-start
  0.7 2.6 %cut.1 = (bf16[4,4,64,256]{3,2,1,0:T(8,128)(2,1)}, bf16[1,4,64,256]{3,2,1,0:T(8,128)(2,1)}) custom-call(s32[16]{0:T(128)} %start_hbm.3, bf16[1,4,1,64,2048]{4,3,2,1,0:T(8,128)(2,1)} %west_ref.3, bf16[1,4,1,64,2048]{4,3,2,1,0:T(8,128)(2,1)} %east_ref.3, bf16[1,4,1,64,2048]{4,3,2,1,0:T(8,128)(2,1)} %north_ref.3), custom_call_target="tpu_custom_call" | custom-call | tf_op jit(solution)/shard_map/cut/pallas_call | solution.py:511
  3.4 1.3 %collective-permute-start = (bf16[4,4,64,256]{3,2,1,0:T(8,128)(2,1)}, bf16[4,4,64,256]{3,2,1,0:T(8,128)(2,1)S(1)}, u32[]{:S(2)}, u32[]{:S(2)}) collective-permute-start(bf16[4,4,64,256]{3,2,1,0:T(8,128)(2,1)} %get-tuple-element.9), channel_id=1, source_target_pairs={{2,6},{4,0},{6,10},{8,4},{10,14},{12,8},{3,7},{5,1},{7,11},{9,5},{... | collective-permute-start | bytes 1572872 | tf_op jit(solution)/shard_map/ppermute | solution.py:491
  4.7 1.3 %collective-permute-start.1 = (bf16[1,4,64,256]{3,2,1,0:T(8,128)(2,1)}, bf16[1,4,64,256]{3,2,1,0:T(8,128)(2,1)S(1)}, u32[]{:S(2)}, u32[]{:S(2)}) collective-permute-start(bf16[1,4,64,256]{3,2,1,0:T(8,128)(2,1)} %get-tuple-element.10), channel_id=1, source_target_pairs={{2,0},{3,1},{6,4},{7,5},{10,8},{11,9},{14,12},{15,13},{18,16},{19,... | collective-permute-start | bytes 393224 | tf_op jit(solution)/shard_map/ppermute | solution.py:495
  6.0 0.0 copy-done.1
  6.0 0.0 copy-done.2
  6.0 0.0 copy-done.3
  6.0 0.0 copy-done.4
  6.0 0.0 copy-done.5
  6.0 0.0 copy-done.6
  6.0 0.0 copy-done.9
  6.0 0.0 copy-done.8
  6.0 0.0 copy-done.7
  6.1 0.0 copy-done
  6.1 5.9 %south.1 = (f32[8,128]{1,0:T(8,128)S(1)}, f32[20,64,256]{2,1,0:T(8,128)}, f32[20,128]{1,0:T(8,128)S(1)}) custom-call(s32[16]{0:T(128)S(1)} %copy-done.6, bf16[1,4,1,64,2048]{4,3,2,1,0:T(8,128)(2,1)S(1)} %copy-done, bf16[1,4,1,64,2048]{4,3,2,1,0:T(8,128)(2,1)} %north_ref.3, bf16[1,4,1,64,2048]{4,3,2,1,0:T(8,128)(2,1)} %east_ref.3, ...), custom_call_target="tpu_custom_call" | custom-call | flops 1000 | bytes 1000 | tf_op jit(solution)/shard_map/south/pallas_call | solution.py:532
  12.0 0.0 collective-permute-done.1.rim_ref
  12.0 3.7 %collective-permute-done.received_ref = bf16[4,4,64,256]{3,2,1,0:T(8,128)(2,1)S(1)} collective-permute-done((bf16[4,4,64,256]{3,2,1,0:T(8,128)(2,1)}, bf16[4,4,64,256]{3,2,1,0:T(8,128)(2,1)S(1)}, u32[]{:S(2)}, u32[]{:S(2)}) %collective-permute-start) | collective-permute-done | bytes 524320 | tf_op jit(solution)/shard_map/ppermute | solution.py:491
  15.7 3.2 %east.1 = f32[16,8,128]{2,1,0:T(8,128)S(1)} custom-call(bf16[4,4,64,256]{3,2,1,0:T(8,128)(2,1)S(1)} %collective-permute-done.received_ref, bf16[1,4,64,256]{3,2,1,0:T(8,128)(2,1)S(1)} %collective-permute-done.1.rim_ref, f32[20,64,256]{2,1,0:T(8,128)} %get-tuple-element.11.q_own, f32[20,128]{1,0:T(8,128)S(1)} %get-tuple-element.12.e_own, ...), custom_call_target="tpu_custom_call" | custom-call | flops 3000000000 | bytes 2000000 | tf_op jit(solution)/shard_map/east/pallas_call | solution.py:565
  18.8 12.2 %all_to_all.5.all_ref = f32[16,8,128]{2,1,0:T(8,128)S(1)} all-to-all(f32[16,8,128]{2,1,0:T(8,128)S(1)} %east.1), channel_id=1, replica_groups=mesh['groups'=2,'gx'=4,'gy'=2,'gz'=2] {'gx','gz','gy'}, dimensions={0} | all-to-all | bytes 131072 | tf_op jit(solution)/shard_map/all_to_all | solution.py:580
  31.0 1.0 %relax.1 = (f32[1,4,1,2,2,16]{5,4,3,2,1,0:T(2,128)}, f32[1,1,2,4]{3,2,1,0:T(2,128)}) custom-call(f32[16,8,128]{2,1,0:T(8,128)S(1)} %all_to_all.5.all_ref), custom_call_target="tpu_custom_call" | custom-call | tf_op jit(solution)/shard_map/relax/pallas_call | solution.py:581
Async XLA Ops:
  0.6 5.3 %copy-start.1 = (bf16[512,256]{1,0:T(8,128)(2,1)S(1)}, bf16[512,256]{1,0:T(8,128)(2,1)}, u32[]{:S(2)}) copy-start(bf16[512,256]{1,0:T(8,128)(2,1)} %constant.11.clone.back_ref) | copy-start | bytes 786436
  0.6 5.3 %copy-start.2 = (bf16[512,256]{1,0:T(8,128)(2,1)S(1)}, bf16[512,256]{1,0:T(8,128)(2,1)}, u32[]{:S(2)}) copy-start(bf16[512,256]{1,0:T(8,128)(2,1)} %constant.10.clone.right_ref) | copy-start | bytes 786436
  0.7 5.3 %copy-start.3 = (bf16[256,256]{1,0:T(8,128)(2,1)S(1)}, bf16[256,256]{1,0:T(8,128)(2,1)}, u32[]{:S(2)}) copy-start(bf16[256,256]{1,0:T(8,128)(2,1)} %constant.13.clone.sums_ref) | copy-start | bytes 393220
  0.7 5.3 %copy-start.4 = (bf16[2,64,192]{2,1,0:T(8,128)(2,1)S(1)}, bf16[2,64,192]{2,1,0:T(8,128)(2,1)}, u32[]{:S(2)}) copy-start(bf16[2,64,192]{2,1,0:T(8,128)(2,1)} %constant.12.clone.left_ref) | copy-start | bytes 147460
  0.7 5.3 %copy-start.5 = (bf16[128,128]{1,0:T(8,128)(2,1)S(1)}, bf16[128,128]{1,0:T(8,128)(2,1)}, u32[]{:S(2)}) copy-start(bf16[128,128]{1,0:T(8,128)(2,1)} %constant.14.clone.ones_ref) | copy-start | bytes 98308
  0.7 5.3 %copy-start.6 = (s32[16]{0:T(128)S(1)}, s32[16]{0:T(128)}, u32[]{:S(2)}) copy-start(s32[16]{0:T(128)} %start_hbm.3) | copy-start | bytes 196
  0.7 5.3 %copy-start.9 = (f32[1,4,1]{1,2,0:T(1,128)S(1)}, f32[1,4,1]{1,2,0:T(1,128)}, u32[]{:S(2)}) copy-start(f32[1,4,1]{1,2,0:T(1,128)} %param.20) | copy-start | bytes 52
  0.7 5.3 %copy-start.8 = (f32[1,4,1]{1,2,0:T(1,128)S(1)}, f32[1,4,1]{1,2,0:T(1,128)}, u32[]{:S(2)}) copy-start(f32[1,4,1]{1,2,0:T(1,128)} %param.19) | copy-start | bytes 52
  0.7 5.3 %copy-start.7 = (f32[1,4,1,2]{1,3,2,0:T(2,128)S(1)}, f32[1,4,1,2]{1,3,2,0:T(2,128)}, u32[]{:S(2)}) copy-start(f32[1,4,1,2]{1,3,2,0:T(2,128)} %param.18) | copy-start | bytes 100
  0.7 5.3 %copy-start = (bf16[1,4,1,64,2048]{4,3,2,1,0:T(8,128)(2,1)S(1)}, bf16[1,4,1,64,2048]{4,3,2,1,0:T(8,128)(2,1)}, u32[]{:S(2)}) copy-start(bf16[1,4,1,64,2048]{4,3,2,1,0:T(8,128)(2,1)} %south_ref.1) | copy-start | bytes 3145732
  3.4 12.3 %collective-permute-start = (bf16[4,4,64,256]{3,2,1,0:T(8,128)(2,1)}, bf16[4,4,64,256]{3,2,1,0:T(8,128)(2,1)S(1)}, u32[]{:S(2)}, u32[]{:S(2)}) collective-permute-start(bf16[4,4,64,256]{3,2,1,0:T(8,128)(2,1)} %get-tuple-element.9), channel_id=1, source_target_pairs={{2,6},{4,0},{6,10},{8,4},{10,14},{12,8},{3,7},{5,1},{7,11},{9,5},{... | collective-permute-start | bytes 1572872 | tf_op jit(solution)/shard_map/ppermute | solution.py:491
  4.7 7.3 %collective-permute-start.1 = (bf16[1,4,64,256]{3,2,1,0:T(8,128)(2,1)}, bf16[1,4,64,256]{3,2,1,0:T(8,128)(2,1)S(1)}, u32[]{:S(2)}, u32[]{:S(2)}) collective-permute-start(bf16[1,4,64,256]{3,2,1,0:T(8,128)(2,1)} %get-tuple-element.10), channel_id=1, source_target_pairs={{2,0},{3,1},{6,4},{7,5},{10,8},{11,9},{14,12},{15,13},{18,16},{19,... | collective-permute-start | bytes 393224 | tf_op jit(solution)/shard_map/ppermute | solution.py:495

commit v3 on v2

--- a/solution.py
+++ b/solution.py
@@ -182,8 +182,8 @@
     return jnp.concatenate([top, low], axis=0)
 
 
-def factors(e_ref, first, groups, ones_ref, width):
-    energy = exact_dot(e_ref[first : first + groups], ones_ref[...])
+def factors(energies, ones_ref, width):
+    energy = exact_dot(energies, ones_ref[...])
     return lax.rsqrt(energy * (1.0 / (width * width)) + EPS_VAR)
 
 
@@ -278,8 +278,8 @@
         return pltpu.make_async_copy(first, target, sem)
 
 
-def is_even():
-    return lax.rem(lax.axis_index("gy"), 2) == 0
+def gx_is_odd():
+    return lax.rem(lax.axis_index("gx"), 2)
 
 
 def cut_into(target, source, start_ref, sizes):
@@ -294,18 +294,26 @@
     cut_tile(start_ref, load, store, width, cell, count)
 
 
-def cut_kernel(sizes, rows, start_hbm, west_ref, east_ref, north_ref, send_ref, rim_ref, start_ref, raw_ref, sems):
+def cut_kernel(sizes, rows, start_hbm, west_ref, east_ref, north_ref, first_ref, second_ref, rim_ref, start_ref, raw_ref, sems):
+    half = rows // 2
     copies = Copies(sems)
-    even = is_even()
+    even = gx_is_odd() == 1
     start = copies.start(start_hbm, start_ref)
     loads = []
     for tile in range(rows):
-        loads.append(copies.start_either(even, west_ref.at[0, tile, 0], east_ref.at[0, tile, 0], raw_ref.at[tile]))
+        up, down = west_ref.at[0, tile % half, 0], east_ref.at[0, half + tile % half, 0]
+        if tile < half:
+            loads.append(copies.start_either(even, down, up, raw_ref.at[tile]))
+        else:
+            loads.append(copies.start_either(even, up, down, raw_ref.at[tile]))
     loads.append(copies.start(north_ref.at[0, 0, 0], raw_ref.at[rows]))
     start.wait()
     for tile in range(rows + 1):
         loads[tile].wait()
-        target = send_ref.at[tile] if tile < rows else rim_ref.at[0]
+        if tile < half:
+            target = first_ref.at[tile]
+        else:
+            target = second_ref.at[tile - half] if tile < rows else rim_ref.at[0]
         cut_into(target, raw_ref.at[tile], start_ref, sizes)
 
 
@@ -315,7 +323,6 @@
     groups = rows * quads
     inner = groups - quads
     copies = Copies(sems)
-    even = is_even()
     batches = [[copies.start(start_hbm, start_ref)], [], []]
     for tile in range(rows - 1):
         batches[0].append(copies.start(south_ref.at[0, tile, 0], raw_ref.at[tile]))
@@ -324,7 +331,8 @@
     batches[2].append(copies.start(south_ref.at[0, rows - 1, 0], raw_ref.at[2 * rows - 2]))
     for tile in range(rows):
         slot = 2 * rows - 1 + tile
-        batches[2].append(copies.start_either(even, east_ref.at[0, tile, 0], west_ref.at[0, tile, 0], raw_ref.at[slot]))
+        source = east_ref if tile < rows // 2 else west_ref
+        batches[2].append(copies.start(source.at[0, tile, 0], raw_ref.at[slot]))
     slots = [range(0, rows - 1), range(rows - 1, 2 * rows - 2), range(2 * rows - 2, 3 * rows - 1)]
 
     def arrive(batch):
@@ -355,7 +363,7 @@
     kept = slots[2][0] * quads
     own = copies.start(q_ref.at[kept : kept + groups + quads], q_out)
     e_out[...] = e_ref[kept : kept + groups + quads]
-    scales = factors(e_ref, 0, inner, ones_ref, width) * factors(e_ref, inner, inner, ones_ref, width)
+    scales = factors(e_ref[:inner], ones_ref, width) * factors(e_ref[inner : 2 * inner], ones_ref, width)
     sum_ref[...] = jnp.zeros_like(sum_ref)
     backward(lambda i: q_ref[i], lambda i: q_ref[inner + i], scales, sum_ref, back_ref, left_ref, inner, width)
     strength, across, along = finish(sum_ref, sums_ref)
@@ -373,31 +381,48 @@
     own.wait()
 
 
-def east_kernel(sizes, rows, received_ref, rim_ref, q_own, e_own, south_ref, right_ref, back_ref, left_ref, sums_ref, ones_ref, out_ref, q_ref, e_ref, sum_ref, sems):
+def east_kernel(sizes, rows, first_ref, second_ref, rim_ref, q_own, e_own, south_ref, right_ref, back_ref, left_ref, sums_ref, ones_ref, out_ref, q_ref, e_ref, sum_ref, sems):
     width, cell, count = sizes
     quads = count // 4
     groups = rows * quads
+    half = groups // 2
     own = Copies(sems).start(q_own, q_ref.at[0])
 
     def source(i):
-        value = rim_ref[0] if i < quads else received_ref[i // quads - 1]
+        tile = i // quads - 1
+        if tile < 0:
+            value = rim_ref[0]
+        else:
+            value = first_ref[tile] if tile < rows // 2 else second_ref[tile - rows // 2]
         return value.reshape(quads * width, 4 * width)
 
     forward(source, q_ref.at[1], e_ref, right_ref, left_ref, 0, quads + groups, width)
-    scales = factors(e_ref, 0, quads + groups, ones_ref, width) * factors(e_own, 0, quads + groups, ones_ref, width)
+    odd = gx_is_odd()
+    from_east, from_west = quads + (1 - odd) * half, quads + odd * half
+    has_rim = jnp.where(lax.axis_index("gy") < lax.axis_size("gy") - 1, 1.0, 0.0)
+    received = factors(e_ref[...], ones_ref, width)
+    e_ref[...] = received
+    mine = factors(e_own[...], ones_ref, width)
+    scales = jnp.concatenate(
+        [
+            has_rim * received[:quads] * mine[:quads],
+            e_ref[pl.ds(from_east, half), :] * mine[quads : quads + half],
+            e_ref[pl.ds(from_west, half), :] * mine[quads + half :],
+        ],
+        axis=0,
+    )
     own.wait()
-    odd = lax.rem(lax.axis_index("gy"), 2)
     sum_ref[...] = jnp.zeros_like(sum_ref)
-    backward(
-        lambda i: q_ref[0 if i < quads else odd, i],
-        lambda i: q_ref[1 if i < quads else 1 - odd, i],
-        scales,
-        sum_ref,
-        back_ref,
-        left_ref,
-        quads + groups,
-        width,
-    )
+
+    def load_first(i):
+        return q_ref[0, i] if i < quads + half else q_ref[1, from_west + (i - quads - half)]
+
+    def load_second(i):
+        if i < quads:
+            return q_ref[1, i]
+        return q_ref[1, from_east + (i - quads)] if i < quads + half else q_ref[0, i]
+
+    backward(load_first, load_second, scales, sum_ref, back_ref, left_ref, quads + groups, width)
     strength, across, along = finish(sum_ref, sums_ref)
     row = lax.broadcasted_iota(jnp.int32, (8, 128), 0)
 
@@ -407,7 +432,7 @@
     rim = [only(pltpu.roll(value, rows - 1, 0), row == rows - 1) for value in (strength, across, along)]
     east = [only(pltpu.roll(value, 7, 0), row < rows) for value in (strength, across, along)]
     packet = south_ref[...] + pack(*rim, SOUTH, D_SOUTH) + pack(*east, EAST, D_EAST)
-    out_ref[...] = jnp.broadcast_to(packet[None], out_ref.shape)
+    out_ref[...] = jnp.broadcast_to(packet[None, 0 : out_ref.shape[1]], out_ref.shape)
 
 
 def turned(value, by):
@@ -419,7 +444,9 @@
 def relax_kernel(counts, rows, patches, all_ref, shift_ref, placed_ref, x_ref):
     nx, nz, ny = counts
     total = nx * nz * ny
-    packet = all_ref[...]
+    x_ref[...] = jnp.zeros_like(x_ref)
+    x_ref[:, 0:rows, :] = all_ref[...]
+    packet = x_ref[...]
     sub = lax.broadcasted_iota(jnp.int32, packet.shape, 1)
     device = lax.broadcasted_iota(jnp.int32, packet.shape, 0)
     gx, gz, gy = device // (nz * ny), device // ny % nz, device % ny
@@ -448,7 +475,7 @@
 
     x = field(POSITION)
     d_east = field(D_EAST)
-    d_east = jnp.where(gy % 2 == 0, d_east, east(d_east))
+    d_east = jnp.where(sub < rows // 2, d_east, east(d_east))
     d_south = field(D_SOUTH)
     ke = jnp.where(gx < nx - 1, one(COL), 0.0)
     ks = jnp.where((gy == ny - 1) & (sub == rows - 1), 0.0, one(ROW))
@@ -462,16 +489,16 @@
         force = force + has_next * (turned(x, ny) - x) + has_prev * (turned(x, -ny) - x)
         x = x + STEP_SIZE * force
     x_ref[...] = x
-    mine = lax.axis_index("gy")
-    me = (lax.axis_index("gx") * nz + lax.axis_index("gz")) * ny + mine
-    holder = lax.rem(me + lax.rem(mine, 2) * (nz * ny), total)
+    me = (lax.axis_index("gx") * nz + lax.axis_index("gz")) * ny + lax.axis_index("gy")
+    holder = lax.rem(me + nz * ny, total)
     lane = lax.broadcasted_iota(jnp.int32, (8, 128), 1)
     row = lax.broadcasted_iota(jnp.int32, (8, 128), 0)
     own = x_ref[me]
     for part in range(2):
         value = jnp.where((lane == row) & (row < rows), own[:, part : part + 1], 0.0)
         placed_ref[0, 0, part : part + 1, :] = jnp.sum(value, axis=0, keepdims=True)[:, :rows]
-    for kind, (source, where) in enumerate(((all_ref[holder], EAST), (all_ref[me], SOUTH))):
+    mixed = jnp.where(row[:rows] < rows // 2, all_ref[me], all_ref[holder])
+    for kind, (source, where) in enumerate(((mixed, EAST), (all_ref[me], SOUTH))):
         for part in range(2):
             value = source
             if where + part * patches:
@@ -480,19 +507,17 @@
                 shift_ref[0, tile, 0, kind, part : part + 1, :] = value[tile : tile + 1, :patches]
 
 
-def to_pair_owner(block):
-    nx, ny = lax.axis_size("gx"), lax.axis_size("gy")
+def exchange(block, first):
     route = []
-    for x in range(nx):
-        for y in range(ny):
-            target = x - 1 if y % 2 == 0 else x + 1
-            if 0 <= target < nx:
-                route.append((x * ny + y, target * ny + y))
-    return lax.ppermute(block, ("gx", "gy"), route)
+    for low in range(first, lax.axis_size("gx") - 1, 2):
+        route += [(low, low + 1), (low + 1, low)]
+    return lax.ppermute(block, "gx", route)
 
 
 def to_north(block):
-    return lax.ppermute(block, "gy", [(i, i - 1) for i in range(1, lax.axis_size("gy"))])
+    count = lax.axis_size("gy")
+    route = [(1, 0), (0, 1)] if count == 2 else [(i, i - 1) for i in range(1, count)]
+    return lax.ppermute(block, "gy", route)
 
 
 def shards(east_strip, west_strip, north_strip, south_strip, patch_start, segment_offset, col_stiffness, row_stiffness):
@@ -508,14 +533,15 @@
     vmem = pl.BlockSpec(memory_space=pltpu.VMEM)
     hbm = pl.BlockSpec(memory_space=pl.ANY)
 
-    send, rim_cut = pl.pallas_call(
+    first_cut, second_cut, rim_cut = pl.pallas_call(
         functools.partial(cut_kernel, sizes, rows),
         out_shape=[
-            jax.ShapeDtypeStruct((rows, quads, width, span), BF16),
+            jax.ShapeDtypeStruct((rows // 2, quads, width, span), BF16),
+            jax.ShapeDtypeStruct((rows // 2, quads, width, span), BF16),
             jax.ShapeDtypeStruct((1, quads, width, span), BF16),
         ],
         in_specs=[hbm] * 4,
-        out_specs=[vmem, vmem],
+        out_specs=[vmem, vmem, vmem],
         scratch_shapes=[
             pltpu.SMEM((count,), jnp.int32),
             pltpu.VMEM((rows + 1, width, length), BF16),
@@ -524,7 +550,8 @@
         compiler_params=pltpu.CompilerParams(vmem_limit_bytes=CUT_VMEM),
         name="cut",
     )(patch_start, west_strip, east_strip, north_strip)
-    received = to_pair_owner(send)
+    first = exchange(first_cut, 1)
+    second = exchange(second_cut, 0)
     rim = to_north(rim_cut)
 
     sums = pltpu.VMEM((3, quads, 8, span), F32)
@@ -564,8 +591,8 @@
     )
     packet = pl.pallas_call(
         functools.partial(east_kernel, sizes, rows),
-        out_shape=jax.ShapeDtypeStruct((total, 8, 128), F32),
-        in_specs=[vmem, vmem, hbm] + [vmem] * 7,
+        out_shape=jax.ShapeDtypeStruct((total, rows, 128), F32),
+        in_specs=[vmem, vmem, vmem, hbm] + [vmem] * 7,
         out_specs=vmem,
         scratch_shapes=[
             pltpu.VMEM((2, kept, width, span), F32),
@@ -574,9 +601,9 @@
             pltpu.SemaphoreType.DMA((1,)),
         ],
         compiler_params=pltpu.CompilerParams(vmem_limit_bytes=EAST_VMEM),
-        cost_estimate=pl.CostEstimate(flops=3_000_000_000, bytes_accessed=2_000_000, transcendentals=0),
+        cost_estimate=pl.CostEstimate(flops=1_000, bytes_accessed=1_000, transcendentals=0),
         name="east",
-    )(received, rim, q_own, e_own, south, *constants)
+    )(first, second, rim, q_own, e_own, south, *constants)
     gathered = lax.all_to_all(packet, PART, 0, 0)
     patch_shift, placed = pl.pallas_call(
         functools.partial(relax_kernel, counts, rows, count),

time: 32.2 us -> 30.9 us (0.960)
  starting transfers between devices: 2.58 us -> 6.58 us
  waiting for transfers between devices: 3.69 us -> 0.66 us
  blocking collectives: 12.2 us -> 10.5 us
  Pallas kernels: 12.6 us -> 12.1 us
    ppermute x2 -> x3, starting transfers between devices: 2.58 us -> 6.58 us  [the longest x2 6.57 us: exchange(): return lax.ppermute(block, 'gx', route)]
    ppermute x2 -> x3, waiting for transfers between devices: 3.69 us -> 0.66 us  [the longest x2 0.65 us: exchange(): return lax.ppermute(block, 'gx', route)]
    all_to_all x1, blocking collectives: 12.2 us -> 10.5 us  [shards(): gathered = lax.all_to_all(packet, PART, 0, 0)]
    pallas_call x1, Pallas kernels: 5.89 us -> 5.46 us  [shards(): pl.pallas_call(functools.partial(south_kernel, sizes, rows), out_shape=[j...]
  transfers between devices with their start and end apart: 2 -> 3, of which waited for: 1 -> 1; matrix products, arithmetic and copies ran while one was open for 0% -> 0% of each run, Pallas kernels for 18% -> 18%
where the time goes in v3:
time: 30.9 us; the launch traced here: 30.7 us
  Pallas kernels  12.1 us (39%)
  blocking collectives  10.5 us (34%)
  starting transfers between devices  6.58 us (21%)
  between operations  0.83 us (3%)
  waiting for transfers between devices  0.66 us (2%)
    all_to_all x1, blocking collectives, shards(): gathered = lax.all_to_all(packet, PART, 0, 0)  10.5 us
    ppermute x2, starting transfers between devices, exchange(): return lax.ppermute(block, 'gx', route)  6.57 us
    pallas_call x1, Pallas kernels, shards(): pl.pallas_call(functools.partial(south_kernel, sizes, rows), out_shape=[j...  5.46 us
    pallas_call x1, Pallas kernels, shards(): pl.pallas_call(functools.partial(east_kernel, sizes, rows), out_shape=jax...  3.08 us
    pallas_call x1, Pallas kernels, shards(): pl.pallas_call(functools.partial(cut_kernel, sizes, rows), out_shape=[jax...  2.59 us
    pallas_call x1, Pallas kernels, shards(): pl.pallas_call(functools.partial(relax_kernel, counts, rows, count), out_...  0.97 us
    ppermute x2, waiting for transfers between devices, exchange(): return lax.ppermute(block, 'gx', route)  0.65 us
  transfers between devices with their start and end apart: 3, of which 1 were waited for; matrix products, arithmetic and copies ran while one was open for 0% of the time, Pallas kernels for 18%

profile of v3, /device:TPU:0, one launch (start us, length us, event | category | flops | bytes accessed | tf_op | source)
XLA Modules:
  0.0 30.7 jit_solution(727821466130669981)
XLA Ops:
  0.6 0.0 copy-start.1
  0.6 0.0 copy-start.2
  0.7 0.0 copy-start.3
  0.7 0.0 copy-start.4
  0.7 0.0 copy-start.5
  0.7 0.0 copy-start.6
  0.7 0.0 copy-start.9
  0.7 0.0 copy-start.8
  0.7 0.0 copy-start.7
  0.7 0.0 copy-start
  0.7 2.6 %cut.1 = (bf16[2,4,64,256]{3,2,1,0:T(8,128)(2,1)}, bf16[2,4,64,256]{3,2,1,0:T(8,128)(2,1)}, bf16[1,4,64,256]{3,2,1,0:T(8,128)(2,1)}) custom-call(s32[16]{0:T(128)} %start_hbm.3, bf16[1,4,1,64,2048]{4,3,2,1,0:T(8,128)(2,1)} %west_ref.3, bf16[1,4,1,64,2048]{4,3,2,1,0:T(8,128)(2,1)} %east_ref.3, bf16[1,4,1,64,2048]{4,3,2,1,0:T(8,128)(2,1)} %north_ref.3), custom_call_target="tpu_custom_call" | custom-call | tf_op jit(solution)/shard_map/cut/pallas_call | solution.py:536
  3.3 0.7 %collective-permute-start = (bf16[2,4,64,256]{3,2,1,0:T(8,128)(2,1)}, bf16[2,4,64,256]{3,2,1,0:T(8,128)(2,1)S(1)}, u32[]{:S(2)}, u32[]{:S(2)}) collective-permute-start(bf16[2,4,64,256]{3,2,1,0:T(8,128)(2,1)} %get-tuple-element.10), channel_id=1, source_target_pairs={{4,8},{8,4},{5,9},{9,5},{6,10},{10,6},{7,11},{11,7},{20,24},{24,20... | collective-permute-start | bytes 786440 | tf_op jit(solution)/shard_map/ppermute | solution.py:514
  4.0 5.9 %collective-permute-start.1 = (bf16[2,4,64,256]{3,2,1,0:T(8,128)(2,1)}, bf16[2,4,64,256]{3,2,1,0:T(8,128)(2,1)S(1)}, u32[]{:S(2)}, u32[]{:S(2)}) collective-permute-start(bf16[2,4,64,256]{3,2,1,0:T(8,128)(2,1)} %get-tuple-element.11), channel_id=1, source_target_pairs={{0,4},{4,0},{8,12},{12,8},{1,5},{5,1},{9,13},{13,9},{2,6},{6,2},{1... | collective-permute-start | bytes 786440 | tf_op jit(solution)/shard_map/ppermute | solution.py:514
  9.9 0.0 collective-permute-start.2
  9.9 0.0 copy-done.1
  9.9 0.0 copy-done.2
  9.9 0.0 copy-done.3
  9.9 0.0 copy-done.4
  10.0 0.0 copy-done.5
  10.0 0.0 copy-done.6
  10.0 0.0 copy-done.9
  10.0 0.0 copy-done.8
  10.0 0.0 copy-done.7
  10.0 0.0 copy-done
  10.0 5.5 %south.1 = (f32[8,128]{1,0:T(8,128)S(1)}, f32[20,64,256]{2,1,0:T(8,128)}, f32[20,128]{1,0:T(8,128)S(1)}) custom-call(s32[16]{0:T(128)S(1)} %copy-done.6, bf16[1,4,1,64,2048]{4,3,2,1,0:T(8,128)(2,1)S(1)} %copy-done, bf16[1,4,1,64,2048]{4,3,2,1,0:T(8,128)(2,1)} %north_ref.3, bf16[1,4,1,64,2048]{4,3,2,1,0:T(8,128)(2,1)} %east_ref.3, ...), custom_call_target="tpu_custom_call" | custom-call | flops 1000 | bytes 1000 | tf_op jit(solution)/shard_map/south/pallas_call | solution.py:559
  15.5 0.0 collective-permute-done.2.rim_ref
  15.5 0.0 collective-permute-done.first_ref
  15.5 0.7 %collective-permute-done.1.second_ref = bf16[2,4,64,256]{3,2,1,0:T(8,128)(2,1)S(1)} collective-permute-done((bf16[2,4,64,256]{3,2,1,0:T(8,128)(2,1)}, bf16[2,4,64,256]{3,2,1,0:T(8,128)(2,1)S(1)}, u32[]{:S(2)}, u32[]{:S(2)}) %collective-permute-start.1) | collective-permute-done | bytes 262176 | tf_op jit(solution)/shard_map/ppermute | solution.py:514
  16.2 3.1 %east.1 = f32[16,4,128]{2,1,0:T(4,128)S(1)} custom-call(bf16[2,4,64,256]{3,2,1,0:T(8,128)(2,1)S(1)} %collective-permute-done.first_ref, bf16[2,4,64,256]{3,2,1,0:T(8,128)(2,1)S(1)} %collective-permute-done.1.second_ref, bf16[1,4,64,256]{3,2,1,0:T(8,128)(2,1)S(1)} %collective-permute-done.2.rim_ref, f32[20,64,256]{2,1,0:T(8,128)} %get-tuple-element.13.q_own, ...), custom_call_target="tpu_custom_call" | custom-call | flops 1000 | bytes 1000 | tf_op jit(solution)/shard_map/east/pallas_call | solution.py:592
  19.3 10.5 %all_to_all.5.all_ref = f32[16,4,128]{2,1,0:T(4,128)S(1)} all-to-all(f32[16,4,128]{2,1,0:T(4,128)S(1)} %east.1), channel_id=1, replica_groups=mesh['groups'=2,'gx'=4,'gy'=2,'gz'=2] {'gx','gz','gy'}, dimensions={0} | all-to-all | bytes 65536 | tf_op jit(solution)/shard_map/all_to_all | solution.py:607
  29.7 1.0 %relax.1 = (f32[1,4,1,2,2,16]{5,4,3,2,1,0:T(2,128)}, f32[1,1,2,4]{3,2,1,0:T(2,128)}) custom-call(f32[16,4,128]{2,1,0:T(4,128)S(1)} %all_to_all.5.all_ref), custom_call_target="tpu_custom_call" | custom-call | tf_op jit(solution)/shard_map/relax/pallas_call | solution.py:608
Async XLA Ops:
  0.6 9.3 %copy-start.1 = (bf16[512,256]{1,0:T(8,128)(2,1)S(1)}, bf16[512,256]{1,0:T(8,128)(2,1)}, u32[]{:S(2)}) copy-start(bf16[512,256]{1,0:T(8,128)(2,1)} %constant.11.clone.back_ref) | copy-start | bytes 786436
  0.6 9.3 %copy-start.2 = (bf16[512,256]{1,0:T(8,128)(2,1)S(1)}, bf16[512,256]{1,0:T(8,128)(2,1)}, u32[]{:S(2)}) copy-start(bf16[512,256]{1,0:T(8,128)(2,1)} %constant.10.clone.right_ref) | copy-start | bytes 786436
  0.7 9.3 %copy-start.3 = (bf16[256,256]{1,0:T(8,128)(2,1)S(1)}, bf16[256,256]{1,0:T(8,128)(2,1)}, u32[]{:S(2)}) copy-start(bf16[256,256]{1,0:T(8,128)(2,1)} %constant.13.clone.sums_ref) | copy-start | bytes 393220
  0.7 9.3 %copy-start.4 = (bf16[2,64,192]{2,1,0:T(8,128)(2,1)S(1)}, bf16[2,64,192]{2,1,0:T(8,128)(2,1)}, u32[]{:S(2)}) copy-start(bf16[2,64,192]{2,1,0:T(8,128)(2,1)} %constant.12.clone.left_ref) | copy-start | bytes 147460
  0.7 9.3 %copy-start.5 = (bf16[128,128]{1,0:T(8,128)(2,1)S(1)}, bf16[128,128]{1,0:T(8,128)(2,1)}, u32[]{:S(2)}) copy-start(bf16[128,128]{1,0:T(8,128)(2,1)} %constant.14.clone.ones_ref) | copy-start | bytes 98308
  0.7 9.3 %copy-start.6 = (s32[16]{0:T(128)S(1)}, s32[16]{0:T(128)}, u32[]{:S(2)}) copy-start(s32[16]{0:T(128)} %start_hbm.3) | copy-start | bytes 196
  0.7 9.3 %copy-start.9 = (f32[1,4,1]{1,2,0:T(1,128)S(1)}, f32[1,4,1]{1,2,0:T(1,128)}, u32[]{:S(2)}) copy-start(f32[1,4,1]{1,2,0:T(1,128)} %param.20) | copy-start | bytes 52
  0.7 9.3 %copy-start.8 = (f32[1,4,1]{1,2,0:T(1,128)S(1)}, f32[1,4,1]{1,2,0:T(1,128)}, u32[]{:S(2)}) copy-start(f32[1,4,1]{1,2,0:T(1,128)} %param.19) | copy-start | bytes 52
  0.7 9.3 %copy-start.7 = (f32[1,4,1,2]{1,3,2,0:T(2,128)S(1)}, f32[1,4,1,2]{1,3,2,0:T(2,128)}, u32[]{:S(2)}) copy-start(f32[1,4,1,2]{1,3,2,0:T(2,128)} %param.18) | copy-start | bytes 100
  0.7 9.3 %copy-start = (bf16[1,4,1,64,2048]{4,3,2,1,0:T(8,128)(2,1)S(1)}, bf16[1,4,1,64,2048]{4,3,2,1,0:T(8,128)(2,1)}, u32[]{:S(2)}) copy-start(bf16[1,4,1,64,2048]{4,3,2,1,0:T(8,128)(2,1)} %south_ref.1) | copy-start | bytes 3145732
  3.3 12.2 %collective-permute-start = (bf16[2,4,64,256]{3,2,1,0:T(8,128)(2,1)}, bf16[2,4,64,256]{3,2,1,0:T(8,128)(2,1)S(1)}, u32[]{:S(2)}, u32[]{:S(2)}) collective-permute-start(bf16[2,4,64,256]{3,2,1,0:T(8,128)(2,1)} %get-tuple-element.10), channel_id=1, source_target_pairs={{4,8},{8,4},{5,9},{9,5},{6,10},{10,6},{7,11},{11,7},{20,24},{24,20... | collective-permute-start | bytes 786440 | tf_op jit(solution)/shard_map/ppermute | solution.py:514
  4.0 12.1 %collective-permute-start.1 = (bf16[2,4,64,256]{3,2,1,0:T(8,128)(2,1)}, bf16[2,4,64,256]{3,2,1,0:T(8,128)(2,1)S(1)}, u32[]{:S(2)}, u32[]{:S(2)}) collective-permute-start(bf16[2,4,64,256]{3,2,1,0:T(8,128)(2,1)} %get-tuple-element.11), channel_id=1, source_target_pairs={{0,4},{4,0},{8,12},{12,8},{1,5},{5,1},{9,13},{13,9},{2,6},{6,2},{1... | collective-permute-start | bytes 786440 | tf_op jit(solution)/shard_map/ppermute | solution.py:514
  9.9 5.6 %collective-permute-start.2 = (bf16[1,4,64,256]{3,2,1,0:T(8,128)(2,1)}, bf16[1,4,64,256]{3,2,1,0:T(8,128)(2,1)S(1)}, u32[]{:S(2)}, u32[]{:S(2)}) collective-permute-start(bf16[1,4,64,256]{3,2,1,0:T(8,128)(2,1)} %get-tuple-element.12), channel_id=1, source_target_pairs={{2,0},{0,2},{3,1},{1,3},{6,4},{4,6},{7,5},{5,7},{10,8},{8,10},{11,... | collective-permute-start | bytes 393224 | tf_op jit(solution)/shard_map/ppermute | solution.py:520

commit v4 on v3

--- a/solution.py
+++ b/solution.py
@@ -187,7 +187,7 @@
     return lax.rsqrt(energy * (1.0 / (width * width)) + EPS_VAR)
 
 
-def backward(load_f, load_g, scales, sum_ref, right_ref, left_ref, groups, width):
+def backward(load_f, load_g, scales, sum_ref, right_ref, left_ref, groups, width, place=None):
     span = 4 * width
     row = lax.broadcasted_iota(jnp.int32, (8, span), 0)
     special = jnp.where(row == 0, 2.0, 1.0)
@@ -221,9 +221,9 @@
                 if r % (width // 2) == 0:
                     piece = piece * special
                 along = along + piece
-            tile = i // step
+            tile = i // step if place is None else place[i // step]
             for kind, value in enumerate((strength, across, along)):
-                sum_ref[kind, j, tile : tile + 1, :] = jnp.sum(value, axis=0, keepdims=True)
+                sum_ref[kind, j, pl.ds(tile, 1), :] = jnp.sum(value, axis=0, keepdims=True)
 
 
 def finish(sum_ref, sums_ref):
@@ -294,7 +294,7 @@
     cut_tile(start_ref, load, store, width, cell, count)
 
 
-def cut_kernel(sizes, rows, start_hbm, west_ref, east_ref, north_ref, first_ref, second_ref, rim_ref, start_ref, raw_ref, sems):
+def cut_kernel(sizes, rows, start_hbm, west_ref, east_ref, south_ref, first_out, second_out, rim_out, start_ref, raw_ref, cut_ref, sems):
     half = rows // 2
     copies = Copies(sems)
     even = gx_is_odd() == 1
@@ -306,15 +306,19 @@
             loads.append(copies.start_either(even, down, up, raw_ref.at[tile]))
         else:
             loads.append(copies.start_either(even, up, down, raw_ref.at[tile]))
-    loads.append(copies.start(north_ref.at[0, 0, 0], raw_ref.at[rows]))
+    loads.append(copies.start(south_ref.at[0, rows - 1, 0], raw_ref.at[rows]))
+    stores = []
     start.wait()
     for tile in range(rows + 1):
         loads[tile].wait()
+        cut_into(cut_ref.at[tile], raw_ref.at[tile], start_ref, sizes)
         if tile < half:
-            target = first_ref.at[tile]
+            target = first_out.at[tile]
         else:
-            target = second_ref.at[tile - half] if tile < rows else rim_ref.at[0]
-        cut_into(target, raw_ref.at[tile], start_ref, sizes)
+            target = second_out.at[tile - half] if tile < rows else rim_out.at[0]
+        stores.append(copies.start(cut_ref.at[tile], target))
+    for store in stores:
+        store.wait()
 
 
 def south_kernel(sizes, rows, start_hbm, south_ref, north_ref, east_ref, west_ref, position_ref, col_ref, row_ref, right_ref, back_ref, left_ref, sums_ref, ones_ref, out_ref, q_out, e_out, start_ref, raw_ref, d_ref, q_ref, e_ref, sum_ref, place_ref, sems):
@@ -328,11 +332,11 @@
         batches[0].append(copies.start(south_ref.at[0, tile, 0], raw_ref.at[tile]))
     for tile in range(rows - 1):
         batches[1].append(copies.start(north_ref.at[0, tile + 1, 0], raw_ref.at[rows - 1 + tile]))
-    batches[2].append(copies.start(south_ref.at[0, rows - 1, 0], raw_ref.at[2 * rows - 2]))
     for tile in range(rows):
-        slot = 2 * rows - 1 + tile
+        slot = 2 * rows - 2 + tile
         source = east_ref if tile < rows // 2 else west_ref
         batches[2].append(copies.start(source.at[0, tile, 0], raw_ref.at[slot]))
+    batches[2].append(copies.start(north_ref.at[0, 0, 0], raw_ref.at[3 * rows - 2]))
     slots = [range(0, rows - 1), range(rows - 1, 2 * rows - 2), range(2 * rows - 2, 3 * rows - 1)]
 
     def arrive(batch):
@@ -381,56 +385,68 @@
     own.wait()
 
 
-def east_kernel(sizes, rows, first_ref, second_ref, rim_ref, q_own, e_own, south_ref, right_ref, back_ref, left_ref, sums_ref, ones_ref, out_ref, q_ref, e_ref, sum_ref, sems):
+def east_kernel(sizes, rows, first_ref, second_ref, rim_ref, q_own, e_own, south_ref, right_ref, back_ref, left_ref, sums_ref, ones_ref, out_ref, q_first, q_second, q_rim, e_first, e_second, e_rim, sum_ref, sems):
     width, cell, count = sizes
     quads = count // 4
-    groups = rows * quads
-    half = groups // 2
-    own = Copies(sems).start(q_own, q_ref.at[0])
-
-    def source(i):
-        tile = i // quads - 1
-        if tile < 0:
-            value = rim_ref[0]
-        else:
-            value = first_ref[tile] if tile < rows // 2 else second_ref[tile - rows // 2]
-        return value.reshape(quads * width, 4 * width)
-
-    forward(source, q_ref.at[1], e_ref, right_ref, left_ref, 0, quads + groups, width)
+    half = rows // 2 * quads
+    copies = Copies(sems)
     odd = gx_is_odd()
-    from_east, from_west = quads + (1 - odd) * half, quads + odd * half
-    has_rim = jnp.where(lax.axis_index("gy") < lax.axis_size("gy") - 1, 1.0, 0.0)
-    received = factors(e_ref[...], ones_ref, width)
-    e_ref[...] = received
-    mine = factors(e_own[...], ones_ref, width)
-    scales = jnp.concatenate(
-        [
-            has_rim * received[:quads] * mine[:quads],
-            e_ref[pl.ds(from_east, half), :] * mine[quads : quads + half],
-            e_ref[pl.ds(from_west, half), :] * mine[quads + half :],
-        ],
-        axis=0,
-    )
-    own.wait()
+    first, second = pl.multiple_of((1 - odd) * half, half), pl.multiple_of(odd * half, half)
+    own = [
+        copies.start(q_own.at[pl.ds(first, half)], q_first.at[0]),
+        copies.start(q_own.at[pl.ds(second, half)], q_second.at[0]),
+        copies.start(q_own.at[2 * half : 2 * half + quads], q_rim.at[0]),
+    ]
     sum_ref[...] = jnp.zeros_like(sum_ref)
 
-    def load_first(i):
-        return q_ref[0, i] if i < quads + half else q_ref[1, from_west + (i - quads - half)]
-
-    def load_second(i):
-        if i < quads:
-            return q_ref[1, i]
-        return q_ref[1, from_east + (i - quads)] if i < quads + half else q_ref[0, i]
-
-    backward(load_first, load_second, scales, sum_ref, back_ref, left_ref, quads + groups, width)
-    strength, across, along = finish(sum_ref, sums_ref)
+    def transform(source, q_ref, e_ref, number):
+        def data(i):
+            return source[i // quads].reshape(quads * width, 4 * width)
+
+        forward(data, q_ref.at[1], e_ref, right_ref, left_ref, 0, number, width)
+
+    def scales(energies, base):
+        number = energies.shape[0]
+        found = factors(jnp.concatenate([energies, e_own[pl.ds(base, number), :]], axis=0), ones_ref, width)
+        return found[:number] * found[number:]
+
+    def correlate(q_ref, mine, factor, place):
+        def load_first(i):
+            return q_ref[1 - mine, i]
+
+        def load_second(i):
+            return q_ref[mine, i]
+
+        backward(load_first, load_second, factor, sum_ref, back_ref, left_ref, factor.shape[0], width, place)
+
+    def work(with_rim):
+        transform(first_ref, q_first, e_first, half)
+        transform(second_ref, q_second, e_second, half)
+        if with_rim:
+            transform(rim_ref, q_rim, e_rim, quads)
+        first_scales = scales(e_first[...], first)
+        second_scales = scales(e_second[...], second)
+        for copy in own:
+            copy.wait()
+        correlate(q_first, odd, first_scales, [(1 - odd) * (rows // 2) + tile for tile in range(rows // 2)])
+        correlate(q_second, 1 - odd, second_scales, [odd * (rows // 2) + tile for tile in range(rows // 2)])
+        if with_rim:
+            correlate(q_rim, 0, scales(e_rim[...], 2 * half), [rows])
+
+    has_rim = lax.axis_index("gy") > 0
+
+    @pl.when(has_rim)
+    def _():
+        work(True)
+
+    @pl.when(jnp.logical_not(has_rim))
+    def _():
+        work(False)
+
+    found = finish(sum_ref, sums_ref)
     row = lax.broadcasted_iota(jnp.int32, (8, 128), 0)
-
-    def only(value, keep):
-        return jnp.where(keep, value, 0.0)
-
-    rim = [only(pltpu.roll(value, rows - 1, 0), row == rows - 1) for value in (strength, across, along)]
-    east = [only(pltpu.roll(value, 7, 0), row < rows) for value in (strength, across, along)]
+    east = [jnp.where(row < rows, value, 0.0) for value in found]
+    rim = [jnp.where(row == rows - 1, pltpu.roll(value, 7, 0), 0.0) for value in found]
     packet = south_ref[...] + pack(*rim, SOUTH, D_SOUTH) + pack(*east, EAST, D_EAST)
     out_ref[...] = jnp.broadcast_to(packet[None, 0 : out_ref.shape[1]], out_ref.shape)
 
@@ -477,6 +493,7 @@
     d_east = field(D_EAST)
     d_east = jnp.where(sub < rows // 2, d_east, east(d_east))
     d_south = field(D_SOUTH)
+    d_south = jnp.where(sub < rows - 1, d_south, turned(d_south, 1))
     ke = jnp.where(gx < nx - 1, one(COL), 0.0)
     ks = jnp.where((gy == ny - 1) & (sub == rows - 1), 0.0, one(ROW))
     kw, d_west = west(ke), west(d_east)
@@ -490,15 +507,17 @@
         x = x + STEP_SIZE * force
     x_ref[...] = x
     me = (lax.axis_index("gx") * nz + lax.axis_index("gz")) * ny + lax.axis_index("gy")
-    holder = lax.rem(me + nz * ny, total)
+    holder, below = lax.rem(me + nz * ny, total), lax.rem(me + 1, total)
     lane = lax.broadcasted_iota(jnp.int32, (8, 128), 1)
     row = lax.broadcasted_iota(jnp.int32, (8, 128), 0)
     own = x_ref[me]
     for part in range(2):
         value = jnp.where((lane == row) & (row < rows), own[:, part : part + 1], 0.0)
         placed_ref[0, 0, part : part + 1, :] = jnp.sum(value, axis=0, keepdims=True)[:, :rows]
-    mixed = jnp.where(row[:rows] < rows // 2, all_ref[me], all_ref[holder])
-    for kind, (source, where) in enumerate(((mixed, EAST), (all_ref[me], SOUTH))):
+    row, own = row[:rows], all_ref[me]
+    easts = jnp.where(row < rows // 2, own, all_ref[holder])
+    souths = jnp.where(row < rows - 1, own, all_ref[below])
+    for kind, (source, where) in enumerate(((easts, EAST), (souths, SOUTH))):
         for part in range(2):
             value = source
             if where + part * patches:
@@ -514,9 +533,9 @@
     return lax.ppermute(block, "gx", route)
 
 
-def to_north(block):
+def to_south(block):
     count = lax.axis_size("gy")
-    route = [(1, 0), (0, 1)] if count == 2 else [(i, i - 1) for i in range(1, count)]
+    route = [(0, 1), (1, 0)] if count == 2 else [(i - 1, i) for i in range(1, count)]
     return lax.ppermute(block, "gy", route)
 
 
@@ -541,18 +560,19 @@
             jax.ShapeDtypeStruct((1, quads, width, span), BF16),
         ],
         in_specs=[hbm] * 4,
-        out_specs=[vmem, vmem, vmem],
+        out_specs=[hbm, hbm, hbm],
         scratch_shapes=[
             pltpu.SMEM((count,), jnp.int32),
             pltpu.VMEM((rows + 1, width, length), BF16),
-            pltpu.SemaphoreType.DMA((rows + 2,)),
+            pltpu.VMEM((rows + 1, quads, width, span), BF16),
+            pltpu.SemaphoreType.DMA((2 * rows + 3,)),
         ],
         compiler_params=pltpu.CompilerParams(vmem_limit_bytes=CUT_VMEM),
         name="cut",
-    )(patch_start, west_strip, east_strip, north_strip)
+    )(patch_start, west_strip, east_strip, south_strip)
     first = exchange(first_cut, 1)
     second = exchange(second_cut, 0)
-    rim = to_north(rim_cut)
+    rim = to_south(rim_cut)
 
     sums = pltpu.VMEM((3, quads, 8, span), F32)
     kept = groups + quads
@@ -595,10 +615,14 @@
         in_specs=[vmem, vmem, vmem, hbm] + [vmem] * 7,
         out_specs=vmem,
         scratch_shapes=[
-            pltpu.VMEM((2, kept, width, span), F32),
-            pltpu.VMEM((kept, span // 2), F32),
+            pltpu.VMEM((2, groups // 2, width, span), F32),
+            pltpu.VMEM((2, groups // 2, width, span), F32),
+            pltpu.VMEM((2, quads, width, span), F32),
+            pltpu.VMEM((groups // 2, span // 2), F32),
+            pltpu.VMEM((groups // 2, span // 2), F32),
+            pltpu.VMEM((quads, span // 2), F32),
             sums,
-            pltpu.SemaphoreType.DMA((1,)),
+            pltpu.SemaphoreType.DMA((3,)),
         ],
         compiler_params=pltpu.CompilerParams(vmem_limit_bytes=EAST_VMEM),
         cost_estimate=pl.CostEstimate(flops=1_000, bytes_accessed=1_000, transcendentals=0),

time: 30.9 us -> 30.6 us (level)
  Pallas kernels: 12.1 us -> 11.7 us
    pallas_call x1, Pallas kernels: 3.08 us -> 2.77 us  [shards(): pl.pallas_call(functools.partial(east_kernel, sizes, rows), out_shape=jax...]
where the time goes in v4:
time: 30.6 us; the launch traced here: 30.3 us
  Pallas kernels  11.7 us (38%)
  blocking collectives  10.5 us (34%)
  starting transfers between devices  6.58 us (22%)
  between operations  0.83 us (3%)
  waiting for transfers between devices  0.66 us (2%)
    all_to_all x1, blocking collectives, shards(): gathered = lax.all_to_all(packet, PART, 0, 0)  10.5 us
    ppermute x2, starting transfers between devices, exchange(): return lax.ppermute(block, 'gx', route)  6.57 us
    pallas_call x1, Pallas kernels, shards(): pl.pallas_call(functools.partial(south_kernel, sizes, rows), out_shape=[j...  5.46 us
    pallas_call x1, Pallas kernels, shards(): pl.pallas_call(functools.partial(east_kernel, sizes, rows), out_shape=jax...  2.77 us
    pallas_call x1, Pallas kernels, shards(): pl.pallas_call(functools.partial(cut_kernel, sizes, rows), out_shape=[jax...  2.54 us
    pallas_call x1, Pallas kernels, shards(): pl.pallas_call(functools.partial(relax_kernel, counts, rows, count), out_...  0.97 us
    ppermute x2, waiting for transfers between devices, exchange(): return lax.ppermute(block, 'gx', route)  0.66 us
  transfers between devices with their start and end apart: 3, of which 1 were waited for; matrix products, arithmetic and copies ran while one was open for 0% of the time, Pallas kernels for 18%

profile of v4, /device:TPU:0, one launch (start us, length us, event | category | flops | bytes accessed | tf_op | source)
XLA Modules:
  0.0 30.3 jit_solution(1438941077591826640)
XLA Ops:
  0.6 0.0 copy-start.1
  0.6 0.0 copy-start.2
  0.7 0.0 copy-start.3
  0.7 0.0 copy-start.4
  0.7 0.0 copy-start.5
  0.7 0.0 copy-start.6
  0.7 0.0 copy-start
  0.7 0.0 copy-start.9
  0.7 0.0 copy-start.8
  0.7 0.0 copy-start.7
  0.7 2.5 %cut.1 = (bf16[2,4,64,256]{3,2,1,0:T(8,128)(2,1)}, bf16[2,4,64,256]{3,2,1,0:T(8,128)(2,1)}, bf16[1,4,64,256]{3,2,1,0:T(8,128)(2,1)}) custom-call(s32[16]{0:T(128)} %start_hbm.3, bf16[1,4,1,64,2048]{4,3,2,1,0:T(8,128)(2,1)} %west_ref.3, bf16[1,4,1,64,2048]{4,3,2,1,0:T(8,128)(2,1)} %east_ref.3, bf16[1,4,1,64,2048]{4,3,2,1,0:T(8,128)(2,1)} %south_ref.3), custom_call_target="tpu_custom_call" | custom-call | tf_op jit(solution)/shard_map/cut/pallas_call | solution.py:555
  3.3 0.7 %collective-permute-start = (bf16[2,4,64,256]{3,2,1,0:T(8,128)(2,1)}, bf16[2,4,64,256]{3,2,1,0:T(8,128)(2,1)S(1)}, u32[]{:S(2)}, u32[]{:S(2)}) collective-permute-start(bf16[2,4,64,256]{3,2,1,0:T(8,128)(2,1)} %get-tuple-element.10), channel_id=1, source_target_pairs={{4,8},{8,4},{5,9},{9,5},{6,10},{10,6},{7,11},{11,7},{20,24},{24,20... | collective-permute-start | bytes 786440 | tf_op jit(solution)/shard_map/ppermute | solution.py:533
  4.0 5.9 %collective-permute-start.1 = (bf16[2,4,64,256]{3,2,1,0:T(8,128)(2,1)}, bf16[2,4,64,256]{3,2,1,0:T(8,128)(2,1)S(1)}, u32[]{:S(2)}, u32[]{:S(2)}) collective-permute-start(bf16[2,4,64,256]{3,2,1,0:T(8,128)(2,1)} %get-tuple-element.11), channel_id=1, source_target_pairs={{0,4},{4,0},{8,12},{12,8},{1,5},{5,1},{9,13},{13,9},{2,6},{6,2},{1... | collective-permute-start | bytes 786440 | tf_op jit(solution)/shard_map/ppermute | solution.py:533
  9.9 0.0 collective-permute-start.2
  9.9 0.0 copy-done.1
  9.9 0.0 copy-done.2
  9.9 0.0 copy-done.3
  9.9 0.0 copy-done.4
  9.9 0.0 copy-done.5
  9.9 0.0 copy-done.6
  9.9 0.0 copy-done
  9.9 0.0 copy-done.9
  9.9 0.0 copy-done.8
  10.0 0.0 copy-done.7
  10.0 5.5 %south.1 = (f32[8,128]{1,0:T(8,128)S(1)}, f32[20,64,256]{2,1,0:T(8,128)}, f32[20,128]{1,0:T(8,128)S(1)}) custom-call(s32[16]{0:T(128)S(1)} %copy-done.6, bf16[1,4,1,64,2048]{4,3,2,1,0:T(8,128)(2,1)S(1)} %copy-done, bf16[1,4,1,64,2048]{4,3,2,1,0:T(8,128)(2,1)} %north_ref.1, bf16[1,4,1,64,2048]{4,3,2,1,0:T(8,128)(2,1)} %east_ref.3, ...), custom_call_target="tpu_custom_call" | custom-call | flops 1000 | bytes 1000 | tf_op jit(solution)/shard_map/south/pallas_call | solution.py:579
  15.4 0.0 collective-permute-done.2.rim_ref
  15.4 0.0 collective-permute-done.first_ref
  15.5 0.7 %collective-permute-done.1.second_ref = bf16[2,4,64,256]{3,2,1,0:T(8,128)(2,1)S(1)} collective-permute-done((bf16[2,4,64,256]{3,2,1,0:T(8,128)(2,1)}, bf16[2,4,64,256]{3,2,1,0:T(8,128)(2,1)S(1)}, u32[]{:S(2)}, u32[]{:S(2)}) %collective-permute-start.1) | collective-permute-done | bytes 262176 | tf_op jit(solution)/shard_map/ppermute | solution.py:533
  16.1 2.8 %east.1 = f32[16,4,128]{2,1,0:T(4,128)S(1)} custom-call(bf16[2,4,64,256]{3,2,1,0:T(8,128)(2,1)S(1)} %collective-permute-done.first_ref, bf16[2,4,64,256]{3,2,1,0:T(8,128)(2,1)S(1)} %collective-permute-done.1.second_ref, bf16[1,4,64,256]{3,2,1,0:T(8,128)(2,1)S(1)} %collective-permute-done.2.rim_ref, f32[20,64,256]{2,1,0:T(8,128)} %get-tuple-element.13.q_own, ...), custom_call_target="tpu_custom_call" | custom-call | flops 1000 | bytes 1000 | tf_op jit(solution)/shard_map/east/pallas_call | solution.py:612
  18.9 10.5 %all_to_all.5.all_ref = f32[16,4,128]{2,1,0:T(4,128)S(1)} all-to-all(f32[16,4,128]{2,1,0:T(4,128)S(1)} %east.1), channel_id=1, replica_groups=mesh['groups'=2,'gx'=4,'gy'=2,'gz'=2] {'gx','gz','gy'}, dimensions={0} | all-to-all | bytes 65536 | tf_op jit(solution)/shard_map/all_to_all | solution.py:631
  29.4 1.0 %relax.1 = (f32[1,4,1,2,2,16]{5,4,3,2,1,0:T(2,128)}, f32[1,1,2,4]{3,2,1,0:T(2,128)}) custom-call(f32[16,4,128]{2,1,0:T(4,128)S(1)} %all_to_all.5.all_ref), custom_call_target="tpu_custom_call" | custom-call | tf_op jit(solution)/shard_map/relax/pallas_call | solution.py:632
Async XLA Ops:
  0.6 9.3 %copy-start.1 = (bf16[512,256]{1,0:T(8,128)(2,1)S(1)}, bf16[512,256]{1,0:T(8,128)(2,1)}, u32[]{:S(2)}) copy-start(bf16[512,256]{1,0:T(8,128)(2,1)} %constant.11.clone.back_ref) | copy-start | bytes 786436
  0.6 9.2 %copy-start.2 = (bf16[512,256]{1,0:T(8,128)(2,1)S(1)}, bf16[512,256]{1,0:T(8,128)(2,1)}, u32[]{:S(2)}) copy-start(bf16[512,256]{1,0:T(8,128)(2,1)} %constant.10.clone.right_ref) | copy-start | bytes 786436
  0.7 9.2 %copy-start.3 = (bf16[256,256]{1,0:T(8,128)(2,1)S(1)}, bf16[256,256]{1,0:T(8,128)(2,1)}, u32[]{:S(2)}) copy-start(bf16[256,256]{1,0:T(8,128)(2,1)} %constant.13.clone.sums_ref) | copy-start | bytes 393220
  0.7 9.2 %copy-start.4 = (bf16[2,64,192]{2,1,0:T(8,128)(2,1)S(1)}, bf16[2,64,192]{2,1,0:T(8,128)(2,1)}, u32[]{:S(2)}) copy-start(bf16[2,64,192]{2,1,0:T(8,128)(2,1)} %constant.12.clone.left_ref) | copy-start | bytes 147460
  0.7 9.2 %copy-start.5 = (bf16[128,128]{1,0:T(8,128)(2,1)S(1)}, bf16[128,128]{1,0:T(8,128)(2,1)}, u32[]{:S(2)}) copy-start(bf16[128,128]{1,0:T(8,128)(2,1)} %constant.14.clone.ones_ref) | copy-start | bytes 98308
  0.7 9.2 %copy-start.6 = (s32[16]{0:T(128)S(1)}, s32[16]{0:T(128)}, u32[]{:S(2)}) copy-start(s32[16]{0:T(128)} %start_hbm.3) | copy-start | bytes 196
  0.7 9.2 %copy-start = (bf16[1,4,1,64,2048]{4,3,2,1,0:T(8,128)(2,1)S(1)}, bf16[1,4,1,64,2048]{4,3,2,1,0:T(8,128)(2,1)}, u32[]{:S(2)}) copy-start(bf16[1,4,1,64,2048]{4,3,2,1,0:T(8,128)(2,1)} %south_ref.3) | copy-start | bytes 3145732
  0.7 9.2 %copy-start.9 = (f32[1,4,1]{1,2,0:T(1,128)S(1)}, f32[1,4,1]{1,2,0:T(1,128)}, u32[]{:S(2)}) copy-start(f32[1,4,1]{1,2,0:T(1,128)} %param.20) | copy-start | bytes 52
  0.7 9.2 %copy-start.8 = (f32[1,4,1]{1,2,0:T(1,128)S(1)}, f32[1,4,1]{1,2,0:T(1,128)}, u32[]{:S(2)}) copy-start(f32[1,4,1]{1,2,0:T(1,128)} %param.19) | copy-start | bytes 52
  0.7 9.2 %copy-start.7 = (f32[1,4,1,2]{1,3,2,0:T(2,128)S(1)}, f32[1,4,1,2]{1,3,2,0:T(2,128)}, u32[]{:S(2)}) copy-start(f32[1,4,1,2]{1,3,2,0:T(2,128)} %param.18) | copy-start | bytes 100
  3.3 12.2 %collective-permute-start = (bf16[2,4,64,256]{3,2,1,0:T(8,128)(2,1)}, bf16[2,4,64,256]{3,2,1,0:T(8,128)(2,1)S(1)}, u32[]{:S(2)}, u32[]{:S(2)}) collective-permute-start(bf16[2,4,64,256]{3,2,1,0:T(8,128)(2,1)} %get-tuple-element.10), channel_id=1, source_target_pairs={{4,8},{8,4},{5,9},{9,5},{6,10},{10,6},{7,11},{11,7},{20,24},{24,20... | collective-permute-start | bytes 786440 | tf_op jit(solution)/shard_map/ppermute | solution.py:533
  4.0 12.1 %collective-permute-start.1 = (bf16[2,4,64,256]{3,2,1,0:T(8,128)(2,1)}, bf16[2,4,64,256]{3,2,1,0:T(8,128)(2,1)S(1)}, u32[]{:S(2)}, u32[]{:S(2)}) collective-permute-start(bf16[2,4,64,256]{3,2,1,0:T(8,128)(2,1)} %get-tuple-element.11), channel_id=1, source_target_pairs={{0,4},{4,0},{8,12},{12,8},{1,5},{5,1},{9,13},{13,9},{2,6},{6,2},{1... | collective-permute-start | bytes 786440 | tf_op jit(solution)/shard_map/ppermute | solution.py:533
  9.9 5.6 %collective-permute-start.2 = (bf16[1,4,64,256]{3,2,1,0:T(8,128)(2,1)}, bf16[1,4,64,256]{3,2,1,0:T(8,128)(2,1)S(1)}, u32[]{:S(2)}, u32[]{:S(2)}) collective-permute-start(bf16[1,4,64,256]{3,2,1,0:T(8,128)(2,1)} %get-tuple-element.12), channel_id=1, source_target_pairs={{0,2},{2,0},{1,3},{3,1},{4,6},{6,4},{5,7},{7,5},{8,10},{10,8},{9,1... | collective-permute-start | bytes 393224 | tf_op jit(solution)/shard_map/ppermute | solution.py:539

commit v5 on v4

--- a/solution.py
+++ b/solution.py
@@ -109,16 +109,21 @@
     return out[:rows] + out[rows : 2 * rows] + out[2 * rows :]
 
 
-def cut_tile(start_ref, load, store, width, cell, count):
+def turns_of(start_ref, sizes):
+    width, cell, count = sizes
+    offsets = [start_ref[k] - k * cell for k in range(count)]
+    return [width - offset if k % 2 else (cell - offset) & (cell - 1) for k, offset in enumerate(offsets)]
+
+
+def cut_into(target, source, turns, sizes):
+    width, cell, count = sizes
     lane = lax.broadcasted_iota(jnp.int32, (width, cell), 1)
     for pair in range(count // 2):
-        parts = []
-        for odd in range(2):
-            k = 2 * pair + odd
-            offset = start_ref[k] - k * cell
-            turn = lax.rem(cell + odd * width - offset, cell)
-            parts.append(pltpu.roll(load(k).astype(F32), turn, 1))
-        store(pair // 2, pair % 2, jnp.where(lane < width, parts[0], parts[1]).astype(BF16))
+        even, odd = (
+            pltpu.roll(source[:, k * cell : (k + 1) * cell], turns[k], 1) for k in (2 * pair, 2 * pair + 1)
+        )
+        side = slice(pair % 2 * cell, (pair % 2 + 1) * cell)
+        target[pair // 2, :, side] = jnp.where(lane < width, even, odd)
 
 
 def forward(source, q_ref, e_ref, right_ref, left_ref, first, groups, width):
@@ -282,18 +287,6 @@
     return lax.rem(lax.axis_index("gx"), 2)
 
 
-def cut_into(target, source, start_ref, sizes):
-    width, cell, count = sizes
-
-    def load(k):
-        return source[:, k * cell : (k + 1) * cell]
-
-    def store(quad, side, value):
-        target[quad, :, side * cell : (side + 1) * cell] = value
-
-    cut_tile(start_ref, load, store, width, cell, count)
-
-
 def cut_kernel(sizes, rows, start_hbm, west_ref, east_ref, south_ref, first_out, second_out, rim_out, start_ref, raw_ref, cut_ref, sems):
     half = rows // 2
     copies = Copies(sems)
@@ -309,9 +302,10 @@
     loads.append(copies.start(south_ref.at[0, rows - 1, 0], raw_ref.at[rows]))
     stores = []
     start.wait()
+    turns = turns_of(start_ref, sizes)
     for tile in range(rows + 1):
         loads[tile].wait()
-        cut_into(cut_ref.at[tile], raw_ref.at[tile], start_ref, sizes)
+        cut_into(cut_ref.at[tile], raw_ref.at[tile], turns, sizes)
         if tile < half:
             target = first_out.at[tile]
         else:
@@ -345,7 +339,7 @@
 
     def cut(batch):
         for slot in slots[batch]:
-            cut_into(d_ref.at[slot], raw_ref.at[slot], start_ref, sizes)
+            cut_into(d_ref.at[slot], raw_ref.at[slot], turns, sizes)
 
     def transform(batch):
         first = slots[batch][0]
@@ -356,6 +350,7 @@
         forward(source, q_ref, e_ref, right_ref, left_ref, first * quads, len(slots[batch]) * quads, width)
 
     arrive(0)
+    turns = turns_of(start_ref, sizes)
     cut(0)
     arrive(1)
     transform(0)
@@ -366,7 +361,7 @@
     transform(2)
     kept = slots[2][0] * quads
     own = copies.start(q_ref.at[kept : kept + groups + quads], q_out)
-    e_out[...] = e_ref[kept : kept + groups + quads]
+    e_out[...] = factors(e_ref[kept : kept + groups + quads], ones_ref, width)
     scales = factors(e_ref[:inner], ones_ref, width) * factors(e_ref[inner : 2 * inner], ones_ref, width)
     sum_ref[...] = jnp.zeros_like(sum_ref)
     backward(lambda i: q_ref[i], lambda i: q_ref[inner + i], scales, sum_ref, back_ref, left_ref, inner, width)
@@ -385,7 +380,7 @@
     own.wait()
 
 
-def east_kernel(sizes, rows, first_ref, second_ref, rim_ref, q_own, e_own, south_ref, right_ref, back_ref, left_ref, sums_ref, ones_ref, out_ref, q_first, q_second, q_rim, e_first, e_second, e_rim, sum_ref, sems):
+def east_kernel(sizes, rows, first_ref, second_ref, rim_ref, q_own, own_factors, south_ref, right_ref, back_ref, left_ref, sums_ref, ones_ref, out_ref, q_first, q_second, q_rim, e_first, e_second, e_rim, sum_ref, sems):
     width, cell, count = sizes
     quads = count // 4
     half = rows // 2 * quads
@@ -406,9 +401,7 @@
         forward(data, q_ref.at[1], e_ref, right_ref, left_ref, 0, number, width)
 
     def scales(energies, base):
-        number = energies.shape[0]
-        found = factors(jnp.concatenate([energies, e_own[pl.ds(base, number), :]], axis=0), ones_ref, width)
-        return found[:number] * found[number:]
+        return factors(energies, ones_ref, width) * own_factors[pl.ds(base, energies.shape[0]), :]
 
     def correlate(q_ref, mine, factor, place):
         def load_first(i):
@@ -459,13 +452,14 @@
 
 def relax_kernel(counts, rows, patches, all_ref, shift_ref, placed_ref, x_ref):
     nx, nz, ny = counts
-    total = nx * nz * ny
-    x_ref[...] = jnp.zeros_like(x_ref)
-    x_ref[:, 0:rows, :] = all_ref[...]
+    column = ny * rows
+    every = all_ref[...].reshape(nx * nz, ny, rows, 128)
+    for gy in range(ny):
+        x_ref[:, gy * rows : (gy + 1) * rows, :] = every[:, gy]
     packet = x_ref[...]
     sub = lax.broadcasted_iota(jnp.int32, packet.shape, 1)
-    device = lax.broadcasted_iota(jnp.int32, packet.shape, 0)
-    gx, gz, gy = device // (nz * ny), device // ny % nz, device % ny
+    stack = lax.broadcasted_iota(jnp.int32, packet.shape, 0)
+    gx, gz = stack // nz, stack % nz
 
     def field(where):
         return pltpu.roll(packet, 128 - where, 2)
@@ -474,28 +468,24 @@
         return jnp.broadcast_to(packet[:, :, where : where + 1], packet.shape)
 
     def east(value):
-        return turned(value, nz * ny)
+        return turned(value, nz)
 
     def west(value):
-        return turned(value, -nz * ny)
+        return turned(value, -nz)
 
     def south(value):
-        inside = pltpu.roll(value, 7, 1)
-        beyond = pltpu.roll(turned(value, 1), rows - 1, 1)
-        return jnp.where(sub == rows - 1, beyond, inside)
+        return pltpu.roll(value, column - 1, 1)
 
     def north(value):
-        inside = pltpu.roll(value, 1, 1)
-        beyond = pltpu.roll(turned(value, -1), 8 - (rows - 1), 1)
-        return jnp.where(sub == 0, beyond, inside)
+        return pltpu.roll(value, 1, 1)
 
     x = field(POSITION)
     d_east = field(D_EAST)
-    d_east = jnp.where(sub < rows // 2, d_east, east(d_east))
+    d_east = jnp.where(sub % rows < rows // 2, d_east, east(d_east))
     d_south = field(D_SOUTH)
-    d_south = jnp.where(sub < rows - 1, d_south, turned(d_south, 1))
+    d_south = jnp.where(sub % rows < rows - 1, d_south, pltpu.roll(d_south, column - rows, 1))
     ke = jnp.where(gx < nx - 1, one(COL), 0.0)
-    ks = jnp.where((gy == ny - 1) & (sub == rows - 1), 0.0, one(ROW))
+    ks = jnp.where(sub < column - 1, one(ROW), 0.0)
     kw, d_west = west(ke), west(d_east)
     kn, d_north = north(ks), north(d_south)
     has_next = jnp.where(gz < nz - 1, LINK_STIFF, 0.0)
@@ -503,16 +493,18 @@
     for _ in range(ITERS):
         force = ke * (east(x) - x - d_east) - kw * (x - west(x) - d_west)
         force = force + ks * (south(x) - x - d_south) - kn * (x - north(x) - d_north)
-        force = force + has_next * (turned(x, ny) - x) + has_prev * (turned(x, -ny) - x)
+        force = force + has_next * (turned(x, 1) - x) + has_prev * (turned(x, -1) - x)
         x = x + STEP_SIZE * force
     x_ref[...] = x
-    me = (lax.axis_index("gx") * nz + lax.axis_index("gz")) * ny + lax.axis_index("gy")
+    mine = lax.axis_index("gy")
+    place = lax.axis_index("gx") * nz + lax.axis_index("gz")
+    me, total = place * ny + mine, nx * nz * ny
     holder, below = lax.rem(me + nz * ny, total), lax.rem(me + 1, total)
-    lane = lax.broadcasted_iota(jnp.int32, (8, 128), 1)
-    row = lax.broadcasted_iota(jnp.int32, (8, 128), 0)
-    own = x_ref[me]
+    lane = lax.broadcasted_iota(jnp.int32, (column, 128), 1)
+    row = lax.broadcasted_iota(jnp.int32, (column, 128), 0)
+    own = x_ref[place]
     for part in range(2):
-        value = jnp.where((lane == row) & (row < rows), own[:, part : part + 1], 0.0)
+        value = jnp.where((lane < rows) & (lane + mine * rows == row), own[:, part : part + 1], 0.0)
         placed_ref[0, 0, part : part + 1, :] = jnp.sum(value, axis=0, keepdims=True)[:, :rows]
     row, own = row[:rows], all_ref[me]
     easts = jnp.where(row < rows // 2, own, all_ref[holder])
@@ -637,7 +629,7 @@
         ],
         in_specs=[vmem],
         out_specs=[vmem, vmem],
-        scratch_shapes=[pltpu.VMEM((total, 8, 128), F32)],
+        scratch_shapes=[pltpu.VMEM((total // counts[2], counts[2] * rows, 128), F32)],
         compiler_params=pltpu.CompilerParams(vmem_limit_bytes=RELAX_VMEM),
         name="relax",
     )(gathered)

time: 30.6 us -> 30.4 us (level)
  no operation moved by 1% of the time
where the time goes in v5:
time: 30.4 us; the launch traced here: 30.2 us
  Pallas kernels  11.7 us (38%)
  blocking collectives  10.5 us (35%)
  starting transfers between devices  6.58 us (22%)
  between operations  0.83 us (3%)
  waiting for transfers between devices  0.55 us (2%)
    all_to_all x1, blocking collectives, shards(): gathered = lax.all_to_all(packet, PART, 0, 0)  10.5 us
    ppermute x2, starting transfers between devices, exchange(): return lax.ppermute(block, 'gx', route)  6.57 us
    pallas_call x1, Pallas kernels, shards(): pl.pallas_call(functools.partial(south_kernel, sizes, rows), out_shape=[j...  5.57 us
    pallas_call x1, Pallas kernels, shards(): pl.pallas_call(functools.partial(east_kernel, sizes, rows), out_shape=jax...  2.77 us
    pallas_call x1, Pallas kernels, shards(): pl.pallas_call(functools.partial(cut_kernel, sizes, rows), out_shape=[jax...  2.52 us
    pallas_call x1, Pallas kernels, shards(): pl.pallas_call(functools.partial(relax_kernel, counts, rows, count), out_...  0.85 us
  transfers between devices with their start and end apart: 3, of which 1 were waited for; matrix products, arithmetic and copies ran while one was open for 0% of the time, Pallas kernels for 18%

profile of v5, /device:TPU:0, one launch (start us, length us, event | category | flops | bytes accessed | tf_op | source)
XLA Modules:
  0.0 30.2 jit_solution(6773138790841487963)
XLA Ops:
  0.6 0.0 copy-start.1
  0.6 0.0 copy-start.2
  0.7 0.0 copy-start.3
  0.7 0.0 copy-start.4
  0.7 0.0 copy-start.5
  0.7 0.0 copy-start.6
  0.7 0.0 copy-start
  0.7 0.0 copy-start.9
  0.7 0.0 copy-start.8
  0.7 0.0 copy-start.7
  0.7 2.5 %cut.1 = (bf16[2,4,64,256]{3,2,1,0:T(8,128)(2,1)}, bf16[2,4,64,256]{3,2,1,0:T(8,128)(2,1)}, bf16[1,4,64,256]{3,2,1,0:T(8,128)(2,1)}) custom-call(s32[16]{0:T(128)} %start_hbm.3, bf16[1,4,1,64,2048]{4,3,2,1,0:T(8,128)(2,1)} %west_ref.3, bf16[1,4,1,64,2048]{4,3,2,1,0:T(8,128)(2,1)} %east_ref.3, bf16[1,4,1,64,2048]{4,3,2,1,0:T(8,128)(2,1)} %south_ref.3), custom_call_target="tpu_custom_call" | custom-call | tf_op jit(solution)/shard_map/cut/pallas_call | solution.py:547
  3.3 0.7 %collective-permute-start = (bf16[2,4,64,256]{3,2,1,0:T(8,128)(2,1)}, bf16[2,4,64,256]{3,2,1,0:T(8,128)(2,1)S(1)}, u32[]{:S(2)}, u32[]{:S(2)}) collective-permute-start(bf16[2,4,64,256]{3,2,1,0:T(8,128)(2,1)} %get-tuple-element.10), channel_id=1, source_target_pairs={{4,8},{8,4},{5,9},{9,5},{6,10},{10,6},{7,11},{11,7},{20,24},{24,20... | collective-permute-start | bytes 786440 | tf_op jit(solution)/shard_map/ppermute | solution.py:525
  4.0 5.9 %collective-permute-start.1 = (bf16[2,4,64,256]{3,2,1,0:T(8,128)(2,1)}, bf16[2,4,64,256]{3,2,1,0:T(8,128)(2,1)S(1)}, u32[]{:S(2)}, u32[]{:S(2)}) collective-permute-start(bf16[2,4,64,256]{3,2,1,0:T(8,128)(2,1)} %get-tuple-element.11), channel_id=1, source_target_pairs={{0,4},{4,0},{8,12},{12,8},{1,5},{5,1},{9,13},{13,9},{2,6},{6,2},{1... | collective-permute-start | bytes 786440 | tf_op jit(solution)/shard_map/ppermute | solution.py:525
  9.9 0.0 collective-permute-start.2
  9.9 0.0 copy-done.1
  9.9 0.0 copy-done.2
  9.9 0.0 copy-done.3
  9.9 0.0 copy-done.4
  9.9 0.0 copy-done.5
  9.9 0.0 copy-done.6
  9.9 0.0 copy-done
  9.9 0.0 copy-done.9
  9.9 0.0 copy-done.8
  9.9 0.0 copy-done.7
  9.9 5.6 %south.1 = (f32[8,128]{1,0:T(8,128)S(1)}, f32[20,64,256]{2,1,0:T(8,128)}, f32[20,128]{1,0:T(8,128)S(1)}) custom-call(s32[16]{0:T(128)S(1)} %copy-done.6, bf16[1,4,1,64,2048]{4,3,2,1,0:T(8,128)(2,1)S(1)} %copy-done, bf16[1,4,1,64,2048]{4,3,2,1,0:T(8,128)(2,1)} %north_ref.1, bf16[1,4,1,64,2048]{4,3,2,1,0:T(8,128)(2,1)} %east_ref.3, ...), custom_call_target="tpu_custom_call" | custom-call | flops 1000 | bytes 1000 | tf_op jit(solution)/shard_map/south/pallas_call | solution.py:571
  15.5 0.0 collective-permute-done.2.rim_ref
  15.5 0.0 collective-permute-done.first_ref
  15.5 0.5 %collective-permute-done.1.second_ref = bf16[2,4,64,256]{3,2,1,0:T(8,128)(2,1)S(1)} collective-permute-done((bf16[2,4,64,256]{3,2,1,0:T(8,128)(2,1)}, bf16[2,4,64,256]{3,2,1,0:T(8,128)(2,1)S(1)}, u32[]{:S(2)}, u32[]{:S(2)}) %collective-permute-start.1) | collective-permute-done | bytes 262176 | tf_op jit(solution)/shard_map/ppermute | solution.py:525
  16.1 2.8 %east.1 = f32[16,4,128]{2,1,0:T(4,128)S(1)} custom-call(bf16[2,4,64,256]{3,2,1,0:T(8,128)(2,1)S(1)} %collective-permute-done.first_ref, bf16[2,4,64,256]{3,2,1,0:T(8,128)(2,1)S(1)} %collective-permute-done.1.second_ref, bf16[1,4,64,256]{3,2,1,0:T(8,128)(2,1)S(1)} %collective-permute-done.2.rim_ref, f32[20,64,256]{2,1,0:T(8,128)} %get-tuple-element.13.q_own, ...), custom_call_target="tpu_custom_call" | custom-call | flops 1000 | bytes 1000 | tf_op jit(solution)/shard_map/east/pallas_call | solution.py:604
  18.9 10.5 %all_to_all.5.all_ref = f32[16,4,128]{2,1,0:T(4,128)S(1)} all-to-all(f32[16,4,128]{2,1,0:T(4,128)S(1)} %east.1), channel_id=1, replica_groups=mesh['groups'=2,'gx'=4,'gy'=2,'gz'=2] {'gx','gz','gy'}, dimensions={0} | all-to-all | bytes 65536 | tf_op jit(solution)/shard_map/all_to_all | solution.py:623
  29.3 0.8 %relax.1 = (f32[1,4,1,2,2,16]{5,4,3,2,1,0:T(2,128)}, f32[1,1,2,4]{3,2,1,0:T(2,128)}) custom-call(f32[16,4,128]{2,1,0:T(4,128)S(1)} %all_to_all.5.all_ref), custom_call_target="tpu_custom_call" | custom-call | tf_op jit(solution)/shard_map/relax/pallas_call | solution.py:624
Async XLA Ops:
  0.6 9.2 %copy-start.1 = (bf16[512,256]{1,0:T(8,128)(2,1)S(1)}, bf16[512,256]{1,0:T(8,128)(2,1)}, u32[]{:S(2)}) copy-start(bf16[512,256]{1,0:T(8,128)(2,1)} %constant.11.clone.back_ref) | copy-start | bytes 786436
  0.6 9.2 %copy-start.2 = (bf16[512,256]{1,0:T(8,128)(2,1)S(1)}, bf16[512,256]{1,0:T(8,128)(2,1)}, u32[]{:S(2)}) copy-start(bf16[512,256]{1,0:T(8,128)(2,1)} %constant.10.clone.right_ref) | copy-start | bytes 786436
  0.7 9.2 %copy-start.3 = (bf16[256,256]{1,0:T(8,128)(2,1)S(1)}, bf16[256,256]{1,0:T(8,128)(2,1)}, u32[]{:S(2)}) copy-start(bf16[256,256]{1,0:T(8,128)(2,1)} %constant.13.clone.sums_ref) | copy-start | bytes 393220
  0.7 9.2 %copy-start.4 = (bf16[2,64,192]{2,1,0:T(8,128)(2,1)S(1)}, bf16[2,64,192]{2,1,0:T(8,128)(2,1)}, u32[]{:S(2)}) copy-start(bf16[2,64,192]{2,1,0:T(8,128)(2,1)} %constant.12.clone.left_ref) | copy-start | bytes 147460
  0.7 9.2 %copy-start.5 = (bf16[128,128]{1,0:T(8,128)(2,1)S(1)}, bf16[128,128]{1,0:T(8,128)(2,1)}, u32[]{:S(2)}) copy-start(bf16[128,128]{1,0:T(8,128)(2,1)} %constant.14.clone.ones_ref) | copy-start | bytes 98308
  0.7 9.2 %copy-start.6 = (s32[16]{0:T(128)S(1)}, s32[16]{0:T(128)}, u32[]{:S(2)}) copy-start(s32[16]{0:T(128)} %start_hbm.3) | copy-start | bytes 196
  0.7 9.2 %copy-start = (bf16[1,4,1,64,2048]{4,3,2,1,0:T(8,128)(2,1)S(1)}, bf16[1,4,1,64,2048]{4,3,2,1,0:T(8,128)(2,1)}, u32[]{:S(2)}) copy-start(bf16[1,4,1,64,2048]{4,3,2,1,0:T(8,128)(2,1)} %south_ref.3) | copy-start | bytes 3145732
  0.7 9.2 %copy-start.9 = (f32[1,4,1]{1,2,0:T(1,128)S(1)}, f32[1,4,1]{1,2,0:T(1,128)}, u32[]{:S(2)}) copy-start(f32[1,4,1]{1,2,0:T(1,128)} %param.20) | copy-start | bytes 52
  0.7 9.2 %copy-start.8 = (f32[1,4,1]{1,2,0:T(1,128)S(1)}, f32[1,4,1]{1,2,0:T(1,128)}, u32[]{:S(2)}) copy-start(f32[1,4,1]{1,2,0:T(1,128)} %param.19) | copy-start | bytes 52
  0.7 9.2 %copy-start.7 = (f32[1,4,1,2]{1,3,2,0:T(2,128)S(1)}, f32[1,4,1,2]{1,3,2,0:T(2,128)}, u32[]{:S(2)}) copy-start(f32[1,4,1,2]{1,3,2,0:T(2,128)} %param.18) | copy-start | bytes 100
  3.3 12.3 %collective-permute-start = (bf16[2,4,64,256]{3,2,1,0:T(8,128)(2,1)}, bf16[2,4,64,256]{3,2,1,0:T(8,128)(2,1)S(1)}, u32[]{:S(2)}, u32[]{:S(2)}) collective-permute-start(bf16[2,4,64,256]{3,2,1,0:T(8,128)(2,1)} %get-tuple-element.10), channel_id=1, source_target_pairs={{4,8},{8,4},{5,9},{9,5},{6,10},{10,6},{7,11},{11,7},{20,24},{24,20... | collective-permute-start | bytes 786440 | tf_op jit(solution)/shard_map/ppermute | solution.py:525
  4.0 12.1 %collective-permute-start.1 = (bf16[2,4,64,256]{3,2,1,0:T(8,128)(2,1)}, bf16[2,4,64,256]{3,2,1,0:T(8,128)(2,1)S(1)}, u32[]{:S(2)}, u32[]{:S(2)}) collective-permute-start(bf16[2,4,64,256]{3,2,1,0:T(8,128)(2,1)} %get-tuple-element.11), channel_id=1, source_target_pairs={{0,4},{4,0},{8,12},{12,8},{1,5},{5,1},{9,13},{13,9},{2,6},{6,2},{1... | collective-permute-start | bytes 786440 | tf_op jit(solution)/shard_map/ppermute | solution.py:525
  9.9 5.7 %collective-permute-start.2 = (bf16[1,4,64,256]{3,2,1,0:T(8,128)(2,1)}, bf16[1,4,64,256]{3,2,1,0:T(8,128)(2,1)S(1)}, u32[]{:S(2)}, u32[]{:S(2)}) collective-permute-start(bf16[1,4,64,256]{3,2,1,0:T(8,128)(2,1)} %get-tuple-element.12), channel_id=1, source_target_pairs={{0,2},{2,0},{1,3},{3,1},{4,6},{6,4},{5,7},{7,5},{8,10},{10,8},{9,1... | collective-permute-start | bytes 393224 | tf_op jit(solution)/shard_map/ppermute | solution.py:531

commit v6 on v5

--- a/solution.py
+++ b/solution.py
@@ -292,25 +292,20 @@
     copies = Copies(sems)
     even = gx_is_odd() == 1
     start = copies.start(start_hbm, start_ref)
-    loads = []
-    for tile in range(rows):
-        up, down = west_ref.at[0, tile % half, 0], east_ref.at[0, half + tile % half, 0]
-        if tile < half:
-            loads.append(copies.start_either(even, down, up, raw_ref.at[tile]))
-        else:
-            loads.append(copies.start_either(even, up, down, raw_ref.at[tile]))
-    loads.append(copies.start(south_ref.at[0, rows - 1, 0], raw_ref.at[rows]))
+    up, down = west_ref.at[0, 0:half, 0], east_ref.at[0, half:rows, 0]
+    loads = [
+        copies.start_either(even, down, up, raw_ref.at[0:half]),
+        copies.start_either(even, up, down, raw_ref.at[half:rows]),
+        copies.start(south_ref.at[0, rows - 1 : rows, 0], raw_ref.at[rows : rows + 1]),
+    ]
     stores = []
     start.wait()
     turns = turns_of(start_ref, sizes)
-    for tile in range(rows + 1):
-        loads[tile].wait()
-        cut_into(cut_ref.at[tile], raw_ref.at[tile], turns, sizes)
-        if tile < half:
-            target = first_out.at[tile]
-        else:
-            target = second_out.at[tile - half] if tile < rows else rim_out.at[0]
-        stores.append(copies.start(cut_ref.at[tile], target))
+    for load, block, target in zip(loads, (range(half), range(half, rows), range(rows, rows + 1)), (first_out, second_out, rim_out)):
+        load.wait()
+        for tile in block:
+            cut_into(cut_ref.at[tile], raw_ref.at[tile], turns, sizes)
+        stores.append(copies.start(cut_ref.at[block[0] : block[-1] + 1], target))
     for store in stores:
         store.wait()
 
@@ -321,16 +316,14 @@
     groups = rows * quads
     inner = groups - quads
     copies = Copies(sems)
+    half, inside = rows // 2, rows - 1
     batches = [[copies.start(start_hbm, start_ref)], [], []]
-    for tile in range(rows - 1):
-        batches[0].append(copies.start(south_ref.at[0, tile, 0], raw_ref.at[tile]))
-    for tile in range(rows - 1):
-        batches[1].append(copies.start(north_ref.at[0, tile + 1, 0], raw_ref.at[rows - 1 + tile]))
-    for tile in range(rows):
-        slot = 2 * rows - 2 + tile
-        source = east_ref if tile < rows // 2 else west_ref
-        batches[2].append(copies.start(source.at[0, tile, 0], raw_ref.at[slot]))
-    batches[2].append(copies.start(north_ref.at[0, 0, 0], raw_ref.at[3 * rows - 2]))
+    batches[0].append(copies.start(south_ref.at[0, 0:inside, 0], raw_ref.at[0:inside]))
+    batches[1].append(copies.start(north_ref.at[0, 1:rows, 0], raw_ref.at[inside : 2 * inside]))
+    base = 2 * inside
+    batches[2].append(copies.start(east_ref.at[0, 0:half, 0], raw_ref.at[base : base + half]))
+    batches[2].append(copies.start(west_ref.at[0, half:rows, 0], raw_ref.at[base + half : base + rows]))
+    batches[2].append(copies.start(north_ref.at[0, 0:1, 0], raw_ref.at[base + rows : base + rows + 1]))
     slots = [range(0, rows - 1), range(rows - 1, 2 * rows - 2), range(2 * rows - 2, 3 * rows - 1)]
 
     def arrive(batch):
@@ -557,7 +550,7 @@
             pltpu.SMEM((count,), jnp.int32),
             pltpu.VMEM((rows + 1, width, length), BF16),
             pltpu.VMEM((rows + 1, quads, width, span), BF16),
-            pltpu.SemaphoreType.DMA((2 * rows + 3,)),
+            pltpu.SemaphoreType.DMA((7,)),
         ],
         compiler_params=pltpu.CompilerParams(vmem_limit_bytes=CUT_VMEM),
         name="cut",
@@ -585,7 +578,7 @@
             pltpu.VMEM((3 * groups - quads, span // 2), F32),
             sums,
             pltpu.VMEM((8, 128), F32),
-            pltpu.SemaphoreType.DMA((3 * rows + 1,)),
+            pltpu.SemaphoreType.DMA((7,)),
         ],
         compiler_params=pltpu.CompilerParams(vmem_limit_bytes=SOUTH_VMEM),
         cost_estimate=pl.CostEstimate(flops=1_000, bytes_accessed=1_000, transcendentals=0),

time: 30.4 us -> 30.3 us (level)
  no operation moved by 1% of the time
where the time goes in v6:
time: 30.3 us; the launch traced here: 30.1 us
  Pallas kernels  11.6 us (38%)
  blocking collectives  10.5 us (35%)
  starting transfers between devices  6.58 us (22%)
  between operations  0.83 us (3%)
  waiting for transfers between devices  0.58 us (2%)
    all_to_all x1, blocking collectives, shards(): gathered = lax.all_to_all(packet, PART, 0, 0)  10.5 us
    ppermute x2, starting transfers between devices, exchange(): return lax.ppermute(block, 'gx', route)  6.57 us
    pallas_call x1, Pallas kernels, shards(): pl.pallas_call(functools.partial(south_kernel, sizes, rows), out_shape=[j...  5.54 us
    pallas_call x1, Pallas kernels, shards(): pl.pallas_call(functools.partial(east_kernel, sizes, rows), out_shape=jax...  2.77 us
    pallas_call x1, Pallas kernels, shards(): pl.pallas_call(functools.partial(cut_kernel, sizes, rows), out_shape=[jax...  2.43 us
    pallas_call x1, Pallas kernels, shards(): pl.pallas_call(functools.partial(relax_kernel, counts, rows, count), out_...  0.85 us
  transfers between devices with their start and end apart: 3, of which 1 were waited for; matrix products, arithmetic and copies ran while one was open for 0% of the time, Pallas kernels for 18%

profile of v6, /device:TPU:0, one launch (start us, length us, event | category | flops | bytes accessed | tf_op | source)
XLA Modules:
  0.0 30.1 jit_solution(4298879187133919392)
XLA Ops:
  0.6 0.0 copy-start.1
  0.6 0.0 copy-start.2
  0.7 0.0 copy-start.3
  0.7 0.0 copy-start.4
  0.7 0.0 copy-start.5
  0.7 0.0 copy-start.6
  0.7 0.0 copy-start
  0.7 0.0 copy-start.9
  0.7 0.0 copy-start.8
  0.7 0.0 copy-start.7
  0.7 2.4 %cut.1 = (bf16[2,4,64,256]{3,2,1,0:T(8,128)(2,1)}, bf16[2,4,64,256]{3,2,1,0:T(8,128)(2,1)}, bf16[1,4,64,256]{3,2,1,0:T(8,128)(2,1)}) custom-call(s32[16]{0:T(128)} %start_hbm.3, bf16[1,4,1,64,2048]{4,3,2,1,0:T(8,128)(2,1)} %west_ref.3, bf16[1,4,1,64,2048]{4,3,2,1,0:T(8,128)(2,1)} %east_ref.3, bf16[1,4,1,64,2048]{4,3,2,1,0:T(8,128)(2,1)} %south_ref.3), custom_call_target="tpu_custom_call" | custom-call | tf_op jit(solution)/shard_map/cut/pallas_call | solution.py:540
  3.2 0.7 %collective-permute-start = (bf16[2,4,64,256]{3,2,1,0:T(8,128)(2,1)}, bf16[2,4,64,256]{3,2,1,0:T(8,128)(2,1)S(1)}, u32[]{:S(2)}, u32[]{:S(2)}) collective-permute-start(bf16[2,4,64,256]{3,2,1,0:T(8,128)(2,1)} %get-tuple-element.10), channel_id=1, source_target_pairs={{4,8},{8,4},{5,9},{9,5},{6,10},{10,6},{7,11},{11,7},{20,24},{24,20... | collective-permute-start | bytes 786440 | tf_op jit(solution)/shard_map/ppermute | solution.py:518
  3.9 5.9 %collective-permute-start.1 = (bf16[2,4,64,256]{3,2,1,0:T(8,128)(2,1)}, bf16[2,4,64,256]{3,2,1,0:T(8,128)(2,1)S(1)}, u32[]{:S(2)}, u32[]{:S(2)}) collective-permute-start(bf16[2,4,64,256]{3,2,1,0:T(8,128)(2,1)} %get-tuple-element.11), channel_id=1, source_target_pairs={{0,4},{4,0},{8,12},{12,8},{1,5},{5,1},{9,13},{13,9},{2,6},{6,2},{1... | collective-permute-start | bytes 786440 | tf_op jit(solution)/shard_map/ppermute | solution.py:518
  9.8 0.0 collective-permute-start.2
  9.8 0.0 copy-done.1
  9.8 0.0 copy-done.2
  9.8 0.0 copy-done.3
  9.8 0.0 copy-done.4
  9.8 0.0 copy-done.5
  9.8 0.0 copy-done.6
  9.8 0.0 copy-done
  9.8 0.0 copy-done.9
  9.8 0.0 copy-done.8
  9.8 0.0 copy-done.7
  9.9 5.5 %south.1 = (f32[8,128]{1,0:T(8,128)S(1)}, f32[20,64,256]{2,1,0:T(8,128)}, f32[20,128]{1,0:T(8,128)S(1)}) custom-call(s32[16]{0:T(128)S(1)} %copy-done.6, bf16[1,4,1,64,2048]{4,3,2,1,0:T(8,128)(2,1)S(1)} %copy-done, bf16[1,4,1,64,2048]{4,3,2,1,0:T(8,128)(2,1)} %north_ref.1, bf16[1,4,1,64,2048]{4,3,2,1,0:T(8,128)(2,1)} %east_ref.3, ...), custom_call_target="tpu_custom_call" | custom-call | flops 1000 | bytes 1000 | tf_op jit(solution)/shard_map/south/pallas_call | solution.py:564
  15.4 0.0 collective-permute-done.2.rim_ref
  15.4 0.0 collective-permute-done.first_ref
  15.4 0.6 %collective-permute-done.1.second_ref = bf16[2,4,64,256]{3,2,1,0:T(8,128)(2,1)S(1)} collective-permute-done((bf16[2,4,64,256]{3,2,1,0:T(8,128)(2,1)}, bf16[2,4,64,256]{3,2,1,0:T(8,128)(2,1)S(1)}, u32[]{:S(2)}, u32[]{:S(2)}) %collective-permute-start.1) | collective-permute-done | bytes 262176 | tf_op jit(solution)/shard_map/ppermute | solution.py:518
  16.0 2.8 %east.1 = f32[16,4,128]{2,1,0:T(4,128)S(1)} custom-call(bf16[2,4,64,256]{3,2,1,0:T(8,128)(2,1)S(1)} %collective-permute-done.first_ref, bf16[2,4,64,256]{3,2,1,0:T(8,128)(2,1)S(1)} %collective-permute-done.1.second_ref, bf16[1,4,64,256]{3,2,1,0:T(8,128)(2,1)S(1)} %collective-permute-done.2.rim_ref, f32[20,64,256]{2,1,0:T(8,128)} %get-tuple-element.13.q_own, ...), custom_call_target="tpu_custom_call" | custom-call | flops 1000 | bytes 1000 | tf_op jit(solution)/shard_map/east/pallas_call | solution.py:597
  18.8 10.5 %all_to_all.5.all_ref = f32[16,4,128]{2,1,0:T(4,128)S(1)} all-to-all(f32[16,4,128]{2,1,0:T(4,128)S(1)} %east.1), channel_id=1, replica_groups=mesh['groups'=2,'gx'=4,'gy'=2,'gz'=2] {'gx','gz','gy'}, dimensions={0} | all-to-all | bytes 65536 | tf_op jit(solution)/shard_map/all_to_all | solution.py:616
  29.3 0.8 %relax.1 = (f32[1,4,1,2,2,16]{5,4,3,2,1,0:T(2,128)}, f32[1,1,2,4]{3,2,1,0:T(2,128)}) custom-call(f32[16,4,128]{2,1,0:T(4,128)S(1)} %all_to_all.5.all_ref), custom_call_target="tpu_custom_call" | custom-call | tf_op jit(solution)/shard_map/relax/pallas_call | solution.py:617
Async XLA Ops:
  0.6 9.1 %copy-start.1 = (bf16[512,256]{1,0:T(8,128)(2,1)S(1)}, bf16[512,256]{1,0:T(8,128)(2,1)}, u32[]{:S(2)}) copy-start(bf16[512,256]{1,0:T(8,128)(2,1)} %constant.11.clone.back_ref) | copy-start | bytes 786436
  0.6 9.1 %copy-start.2 = (bf16[512,256]{1,0:T(8,128)(2,1)S(1)}, bf16[512,256]{1,0:T(8,128)(2,1)}, u32[]{:S(2)}) copy-start(bf16[512,256]{1,0:T(8,128)(2,1)} %constant.10.clone.right_ref) | copy-start | bytes 786436
  0.7 9.1 %copy-start.3 = (bf16[256,256]{1,0:T(8,128)(2,1)S(1)}, bf16[256,256]{1,0:T(8,128)(2,1)}, u32[]{:S(2)}) copy-start(bf16[256,256]{1,0:T(8,128)(2,1)} %constant.13.clone.sums_ref) | copy-start | bytes 393220
  0.7 9.1 %copy-start.4 = (bf16[2,64,192]{2,1,0:T(8,128)(2,1)S(1)}, bf16[2,64,192]{2,1,0:T(8,128)(2,1)}, u32[]{:S(2)}) copy-start(bf16[2,64,192]{2,1,0:T(8,128)(2,1)} %constant.12.clone.left_ref) | copy-start | bytes 147460
  0.7 9.1 %copy-start.5 = (bf16[128,128]{1,0:T(8,128)(2,1)S(1)}, bf16[128,128]{1,0:T(8,128)(2,1)}, u32[]{:S(2)}) copy-start(bf16[128,128]{1,0:T(8,128)(2,1)} %constant.14.clone.ones_ref) | copy-start | bytes 98308
  0.7 9.1 %copy-start.6 = (s32[16]{0:T(128)S(1)}, s32[16]{0:T(128)}, u32[]{:S(2)}) copy-start(s32[16]{0:T(128)} %start_hbm.3) | copy-start | bytes 196
  0.7 9.1 %copy-start = (bf16[1,4,1,64,2048]{4,3,2,1,0:T(8,128)(2,1)S(1)}, bf16[1,4,1,64,2048]{4,3,2,1,0:T(8,128)(2,1)}, u32[]{:S(2)}) copy-start(bf16[1,4,1,64,2048]{4,3,2,1,0:T(8,128)(2,1)} %south_ref.3) | copy-start | bytes 3145732
  0.7 9.1 %copy-start.9 = (f32[1,4,1]{1,2,0:T(1,128)S(1)}, f32[1,4,1]{1,2,0:T(1,128)}, u32[]{:S(2)}) copy-start(f32[1,4,1]{1,2,0:T(1,128)} %param.20) | copy-start | bytes 52
  0.7 9.1 %copy-start.8 = (f32[1,4,1]{1,2,0:T(1,128)S(1)}, f32[1,4,1]{1,2,0:T(1,128)}, u32[]{:S(2)}) copy-start(f32[1,4,1]{1,2,0:T(1,128)} %param.19) | copy-start | bytes 52
  0.7 9.1 %copy-start.7 = (f32[1,4,1,2]{1,3,2,0:T(2,128)S(1)}, f32[1,4,1,2]{1,3,2,0:T(2,128)}, u32[]{:S(2)}) copy-start(f32[1,4,1,2]{1,3,2,0:T(2,128)} %param.18) | copy-start | bytes 100
  3.2 12.2 %collective-permute-start = (bf16[2,4,64,256]{3,2,1,0:T(8,128)(2,1)}, bf16[2,4,64,256]{3,2,1,0:T(8,128)(2,1)S(1)}, u32[]{:S(2)}, u32[]{:S(2)}) collective-permute-start(bf16[2,4,64,256]{3,2,1,0:T(8,128)(2,1)} %get-tuple-element.10), channel_id=1, source_target_pairs={{4,8},{8,4},{5,9},{9,5},{6,10},{10,6},{7,11},{11,7},{20,24},{24,20... | collective-permute-start | bytes 786440 | tf_op jit(solution)/shard_map/ppermute | solution.py:518
  3.9 12.1 %collective-permute-start.1 = (bf16[2,4,64,256]{3,2,1,0:T(8,128)(2,1)}, bf16[2,4,64,256]{3,2,1,0:T(8,128)(2,1)S(1)}, u32[]{:S(2)}, u32[]{:S(2)}) collective-permute-start(bf16[2,4,64,256]{3,2,1,0:T(8,128)(2,1)} %get-tuple-element.11), channel_id=1, source_target_pairs={{0,4},{4,0},{8,12},{12,8},{1,5},{5,1},{9,13},{13,9},{2,6},{6,2},{1... | collective-permute-start | bytes 786440 | tf_op jit(solution)/shard_map/ppermute | solution.py:518
  9.8 5.6 %collective-permute-start.2 = (bf16[1,4,64,256]{3,2,1,0:T(8,128)(2,1)}, bf16[1,4,64,256]{3,2,1,0:T(8,128)(2,1)S(1)}, u32[]{:S(2)}, u32[]{:S(2)}) collective-permute-start(bf16[1,4,64,256]{3,2,1,0:T(8,128)(2,1)} %get-tuple-element.12), channel_id=1, source_target_pairs={{0,2},{2,0},{1,3},{3,1},{4,6},{6,4},{5,7},{7,5},{8,10},{10,8},{9,1... | collective-permute-start | bytes 393224 | tf_op jit(solution)/shard_map/ppermute | solution.py:524
